TPU v7x, 256 devices: a whole 4x4x8 slice. The times are simulated.
256 devices in a mesh: pair: 128 (over y, z, x_hi, core), vir: 2 (over x_lo).
Axes of the slice: x: 4 (x_hi: 2, x_lo: 2; x = x_hi * 2 + x_lo), y: 4, z: 8, core: 2. Of those that a mesh axis runs over, the one named last changes fastest.
Arguments:
- amplitudes: bfloat16 [2, 768, 256, 256], P(None, 'pair', None, 'vir'), may hold values from -24 to 24
- integrals: bfloat16 [2, 4, 24, 256, 256], P(None, None, None, 'vir'), may hold values from -0.0546875 to 0.0546875
- pair_table: int32 [768], replicated, may hold values from 0 to 767, each once
- kramers: int32 [256], replicated, may hold values from 0 to 255, each once
Outputs:
- residual: bfloat16 [2, 4, 32, 256, 256], P(None, None, None, 'pair', 'vir')
Inputs may be any that keep to these rules, and one draw needn't show every extreme that they name: `pair_table`: a permutation: every occupied pair stands in exactly one slot. `kramers`: a permutation of the virtual spinors.
All inputs are finite; a program needn't handle non-finite values.
Results may differ from a plain program's by a relative error of at most 0.00105.
Values may be sent and summed in bfloat16 or wider, within the bound.
No kernel may reach another device: no remote copies, remote signals or barrier semaphores. Data moves between devices by JAX's collectives and lax.ppermute only.
A program may use at most 128 MiB of HBM per device.

v0:
```python
import jax
import jax.numpy as jnp
from jax import lax
from jax.sharding import PartitionSpec as P


def inverse_of(order):
    return jnp.zeros_like(order).at[order].set(jnp.arange(order.shape[0], dtype=jnp.int32))


def contract(moved, integrals, pair_order, back_order, occupied, summed_occ):
    rows_here = moved.shape[2]
    half_width = moved.shape[3]
    full_virtual = integrals.shape[4]
    ordered = jnp.take(moved, pair_order, axis=1)
    ordered = ordered.reshape(2, occupied, summed_occ, rows_here, half_width)
    matrices = jnp.transpose(ordered, (0, 1, 3, 2, 4)).reshape(
        2, occupied * rows_here, summed_occ * half_width
    )
    results = []
    for window in range(integrals.shape[1]):
        slab_matrix = integrals[:, window].reshape(2, summed_occ * half_width, full_virtual)
        real_part = jnp.dot(
            matrices[0], slab_matrix[0], preferred_element_type=jnp.float32
        ) - jnp.dot(matrices[1], slab_matrix[1], preferred_element_type=jnp.float32)
        imag_part = jnp.dot(
            matrices[0], slab_matrix[1], preferred_element_type=jnp.float32
        ) + jnp.dot(matrices[1], slab_matrix[0], preferred_element_type=jnp.float32)
        cycle = jnp.stack([real_part, imag_part]).reshape(2, occupied, rows_here, full_virtual)
        results.append(jnp.take(cycle, back_order, axis=3))
    return jnp.stack(results, axis=1)


def body(amplitudes, integrals, pair_table, kramers):
    summed_occ = integrals.shape[2]
    occupied = pair_table.shape[0] // summed_occ
    back_order = inverse_of(kramers)
    pair_order = inverse_of(pair_table)
    moved = lax.all_to_all(amplitudes, "pair", split_axis=2, concat_axis=1, tiled=True)
    cycle = contract(moved, integrals, pair_order, back_order, occupied, summed_occ)
    mirror = lax.all_to_all(cycle, "pair", split_axis=4, concat_axis=3, tiled=True)
    block = cycle - jnp.swapaxes(mirror, 3, 4)
    summed = lax.psum_scatter(block, "vir", scatter_dimension=4, tiled=True)
    return summed.astype(jnp.bfloat16)


def solution(mesh):
    placed = (P(None, "pair", None, "vir"), P(None, None, None, "vir", None), P(), P())
    return jax.shard_map(
        body,
        mesh=mesh,
        in_specs=placed,
        out_specs=P(None, None, None, "pair", "vir"),
        check_vma=False,
    )
```

profile of v0, /device:TPU:1, one launch (start us, length us, event | category | flops | bytes accessed | tf_op | source)
XLA Modules:
  0.0 175.4 jit_solution(11425294529882186683)
XLA Ops:
  0.0 2.7 %copy.62 = bf16[2,6,256,128]{3,1,0,2:T(8,128)(2,1)} copy(bf16[2,6,256,128]{3,2,1,0:T(8,128)(2,1)} %param.6) | data formatting | bytes 1572864 | tf_op args[0]
  2.7 16.4 %all-to-all-start = ((bf16[2,6,256,128]{3,1,0,2:T(8,128)(2,1)}), bf16[2,6,256,128]{3,1,0,2:T(8,128)(2,1)S(1)}, u32[]{:S(2)}, u32[]{:S(2)}) async-start(bf16[2,6,256,128]{3,1,0,2:T(8,128)(2,1)} %copy.62), calls=%async_computation | async-start | bytes 2097152 | tf_op jit(solution)/shard_map/all_to_all | solution.py:39
  19.1 3.4 %scatter_custom_fusion = s32[768]{0:T(1024)S(1)} fusion(s32[768]{0:T(1024)S(1)} %compare_select_fusion.1, s32[768]{0:T(1024)S(1)} %iota.6, s32[]{:T(128)} %constant.16.clone.1), kind=kCustom, calls=%fused_computation.74 | custom fusion | bytes 3076 | tf_op jit(solution)/shard_map/scatter | solution.py:8
  22.6 1.6 scatter_custom_fusion.1
  24.3 9.0 %fusion.45 = (bf16[1,1,24,128,256]{4,3,2,1,0:T(8,128)(2,1)}, bf16[1,1,24,128,256]{4,3,2,1,0:T(8,128)(2,1)}, bf16[1,1,24,128,256]{4,3,2,1,0:T(8,128)(2,1)}, bf16[...) fusion(bf16[2,4,24,128,256]{4,3,2,1,0:T(8,128)(2,1)} %param.7), kind=kLoop, calls=%fused_computation.80 | loop fusion | bytes 25165824 | tf_op jit(solution)/shard_map/slice | solution.py:24
  33.3 15.7 %all-to-all-done = bf16[2,6,256,128]{3,1,0,2:T(8,128)(2,1)S(1)} async-done(((bf16[2,6,256,128]{3,1,0,2:T(8,128)(2,1)}), bf16[2,6,256,128]{3,1,0,2:T(8,128)(2,1)S(1)}, u32[]{:S(2)}, u32[]{:S(2)}) %all-to-all-start) | async-done | bytes 786464 | tf_op jit(solution)/shard_map/all_to_all | solution.py:39
  49.0 0.8 copy.63
  49.8 3.1 %gather_fusion = bf16[768,2,2,128]{3,2,1,0:T(2,128)(2,1)S(1)} fusion(bf16[2,768,2,128]{3,2,1,0:T(2,128)(2,1)S(1)} %bitcast.135, s32[1024]{0:T(1024)S(1)} %pad_clamp_fusion.1), kind=kCustom, calls=%fused_computation.4 | custom fusion | bytes 1575936 | tf_op jit(solution)/shard_map/jit(_take)/gather | solution.py:15
  53.2 1.1 copy-done.5
  56.1 1.9 %fusion.23 = f32[64,256]{1,0:T(8,128)S(1)} fusion(bf16[3072,256]{1,0:T(8,128)(2,1)} %bitcast.123, bf16[8,8,24,128]{3,2,1,0:T(8,128)(2,1)S(1)} %bitcast.109), kind=kOutput, calls=%fused_computation.49 | convolution fusion | flops 100663296 | bytes 2031616 | tf_op jit(solution)/shard_map/dot_general | solution.py:23
  58.8 0.6 copy-done.3
  59.9 1.9 %fusion.17 = f32[64,256]{1,0:T(8,128)S(1)} fusion(bf16[3072,256]{1,0:T(8,128)(2,1)} %bitcast.119, bf16[8,8,24,128]{3,2,1,0:T(8,128)(2,1)S(1)} %bitcast.111), kind=kOutput, calls=%fused_computation.43 | convolution fusion | flops 100663296 | bytes 2031616 | tf_op jit(solution)/shard_map/dot_general | solution.py:26
  62.6 0.6 copy-done.1
  64.1 1.0 copy-done
  67.2 1.3 gather_fusion.4
  68.9 1.3 gather_fusion.2
  70.8 1.3 gather_fusion.1
  72.8 1.3 gather_fusion.3
  74.1 1.7 select_bitcast_fusion.3
  75.9 0.8 copy-done.7
  76.8 1.1 copy_bitcast_fusion
  77.9 2.8 %reshape.131 = f32[128,1,1024]{2,1,0:T(1,128)} reshape(f32[256,4,2,2,32]{4,3,2,1,0:T(2,128)S(1)} %copy_bitcast_fusion) | data formatting | bytes 1048576
  80.8 8.1 %all-to-all-start.1 = ((f32[128,1,1024]{2,1,0:T(1,128)}), f32[128,1,1024]{2,1,0:T(1,128)S(1)}, u32[]{:S(2)}, u32[]{:S(2)}) async-start(f32[128,1,1024]{2,1,0:T(1,128)} %reshape.131), calls=%async_computation.1 | async-start | bytes 1048576 | tf_op jit(solution)/shard_map/all_to_all | solution.py:41
  90.2 19.2 %all-to-all-done.1 = f32[128,1,1024]{2,1,0:T(1,128)S(1)} async-done(((f32[128,1,1024]{2,1,0:T(1,128)}), f32[128,1,1024]{2,1,0:T(1,128)S(1)}, u32[]{:S(2)}, u32[]{:S(2)}) %all-to-all-start.1) | async-done | bytes 524320 | tf_op jit(solution)/shard_map/all_to_all | solution.py:41
  109.9 2.8 %reduce = f32[128,1024]{1,0:T(8,128)} reduce(f32[128,1,1024]{2,1,0:T(1,128)S(1)} %all-to-all-done.1, f32[]{:T(128)} %broadcast.71), dimensions={1}, to_apply=%all_to_all.30.reduce_sub_computation | reduce | bytes 1048580 | tf_op jit(solution)/shard_map/all_to_all | solution.py:41
  112.7 3.0 %reshape.132 = f32[256,4,2,2,32]{4,3,2,1,0:T(2,128)S(1)} reshape(f32[128,1024]{1,0:T(8,128)} %reduce) | data formatting | bytes 1048576
  115.7 0.7 copy.74
  116.4 1.9 %copy.75 = f32[2,4,32,128,2,2]{2,4,3,5,1,0:T(2,128)S(1)} copy(f32[2,4,32,128,2,2]{2,5,3,4,1,0:T(2,128)S(1)} %bitcast.133) | data formatting | bytes 1048576 | tf_op jit(solution)/shard_map/all_to_all | solution.py:41
  118.3 2.5 %bitcast_subtract_fusion = f32[2,4,32,2,256]{2,3,0,4,1:T(2,128)S(1)} fusion(f32[2,4,32,256,2]{2,3,4,1,0:T(8,128)S(1)} %bitcast.131, f32[2,1,32,2,256]{2,3,0,4,1:T(2,128)S(1)} %copy-done.10, f32[2,1,32,2,256]{2,3,0,4,1:T(2,128)S(1)} %copy-done.8, f32[2,1,32,2,256]{2,3,0,4,1:T(2,128)S(1)} %get-tuple-element.17, f32[2,1,32,2,256]{2,3,0,4,1:T(2,128)S(1)} %get-tuple-element.16), kind=kLoop, calls=%fused_computation.8 | loop fusion | flops 524288 | bytes 1572864 | tf_op jit(solution)/shard_map/sub | solution.py:42
  120.8 1.4 copy.77
  122.2 51.8 %all-reduce.2 = bf16[2,4,32,2,256]{2,1,3,0,4:T(4,128)(2,1)S(1)} all-reduce(f32[2,4,32,2,256]{2,1,3,0,4:T(4,128)S(1)} %copy.77), channel_id=2, replica_groups=mesh['pair'=128,'vir'=2] {'vir'}, use_global_device_ids=true, to_apply=%region_2.0.clone | all-reduce | flops 131072 | bytes 786432
  174.7 0.8 copy.79
  (74 shorter events, 10.3 us)
Async XLA Ops:
  0.0 19.1 %copy-start.11 = (s32[768]{0:T(1024)S(1)}, s32[768]{0:T(1024)}, u32[]{:S(2)}) copy-start(s32[768]{0:T(1024)} %param.8) | copy-start | bytes 9220
  0.0 22.5 %copy-start.12 = (s32[256]{0:T(256)S(1)}, s32[256]{0:T(256)}, u32[]{:S(2)}) copy-start(s32[256]{0:T(256)} %param.9) | copy-start | bytes 3076
  2.7 46.3 %all-to-all-start = ((bf16[2,6,256,128]{3,1,0,2:T(8,128)(2,1)}), bf16[2,6,256,128]{3,1,0,2:T(8,128)(2,1)S(1)}, u32[]{:S(2)}, u32[]{:S(2)}) async-start(bf16[2,6,256,128]{3,1,0,2:T(8,128)(2,1)} %copy.62), calls=%async_computation | async-start | bytes 2097152 | tf_op jit(solution)/shard_map/all_to_all | solution.py:39
  53.0 1.4 copy-start.5
  53.1 1.7 copy-start.6
  56.1 1.9 %copy-start.4 = (bf16[1,1,24,128,256]{4,3,2,1,0:T(8,128)(2,1)S(1)}, bf16[1,1,24,128,256]{4,3,2,1,0:T(8,128)(2,1)}, u32[]{:S(2)}) copy-start(bf16[1,1,24,128,256]{4,3,2,1,0:T(8,128)(2,1)} %get-tuple-element.11) | copy-start | bytes 4718596
  58.0 1.4 copy-start.3
  59.9 1.9 %copy-start.2 = (bf16[1,1,24,128,256]{4,3,2,1,0:T(8,128)(2,1)S(1)}, bf16[1,1,24,128,256]{4,3,2,1,0:T(8,128)(2,1)}, u32[]{:S(2)}) copy-start(bf16[1,1,24,128,256]{4,3,2,1,0:T(8,128)(2,1)} %get-tuple-element.10) | copy-start | bytes 4718596
  61.8 1.4 copy-start.1
  63.7 1.4 copy-start
  75.8 0.8 copy-start.7
  75.8 1.0 copy-start.9
  77.9 11.0 %copy-start.13 = (u32[256]{0:T(256)S(1)}, u32[256]{0:T(256)}, u32[]{:S(2)}) copy-start(u32[256]{0:T(256)} %constant.34) | copy-start | bytes 3076
  80.8 28.6 %all-to-all-start.1 = ((f32[128,1,1024]{2,1,0:T(1,128)}), f32[128,1,1024]{2,1,0:T(1,128)S(1)}, u32[]{:S(2)}, u32[]{:S(2)}) async-start(f32[128,1,1024]{2,1,0:T(1,128)} %reshape.131), calls=%async_computation.1 | async-start | bytes 1048576 | tf_op jit(solution)/shard_map/all_to_all | solution.py:41
  116.4 1.9 %copy-start.8 = (f32[2,1,32,2,256]{2,3,0,4,1:T(2,128)S(1)}, f32[2,1,32,2,256]{2,3,0,4,1:T(2,128)}, u32[]{:S(2)}) copy-start(f32[2,1,32,2,256]{2,3,0,4,1:T(2,128)} %copy-done.7) | copy-start | bytes 393220
  116.4 1.9 %copy-start.10 = (f32[2,1,32,2,256]{2,3,0,4,1:T(2,128)S(1)}, f32[2,1,32,2,256]{2,3,0,4,1:T(2,128)}, u32[]{:S(2)}) copy-start(f32[2,1,32,2,256]{2,3,0,4,1:T(2,128)} %copy-done.9) | copy-start | bytes 393220
where the time goes:
time: 176 us; the launch traced here: 175 us
  blocking collectives  51.8 us (29%)
  local copies, waits for them, and re-layouts  44.5 us (25%)
  waiting for transfers between devices  34.8 us (20%)
  starting transfers between devices  24.5 us (14%)
  other arithmetic  9.5 us (5%)
  matrix products  8.94 us (5%)
    unnamed x1, blocking collectives  51.8 us
    all_to_all x1, waiting for transfers between devices, body(): lax.all_to_all(cycle, 'pair', split_axis=4, concat_axis=3, tiled=True)  19.2 us
    all_to_all x1, starting transfers between devices, body(): lax.all_to_all(amplitudes, 'pair', split_axis=2, concat_axis=1, tiled=True)  16.4 us
    all_to_all x1, waiting for transfers between devices, body(): lax.all_to_all(amplitudes, 'pair', split_axis=2, concat_axis=1, tiled=True)  15.7 us
    unnamed x33, local copies, waits for them, and re-layouts  13.9 us
    slice x1, local copies, waits for them, and re-layouts, contract(): slab_matrix[0]  9.05 us
    all_to_all x1, starting transfers between devices, body(): lax.all_to_all(cycle, 'pair', split_axis=4, concat_axis=3, tiled=True)  8.11 us
    gather x4, local copies, waits for them, and re-layouts, contract(): results.append(jnp.take(cycle, back_order, axis=3))  5.33 us
  transfers between devices with their start and end apart: 2, of which 2 were waited for; matrix products, arithmetic and copies ran while one was open for 8% of the time, Pallas kernels for 0%

commit v1 on v0

v1 whole, which is shorter than its diff:
```python
import functools

import jax
import jax.numpy as jnp
from jax import lax
from jax.experimental import pallas as pl
from jax.experimental.pallas import tpu as pltpu
from jax.sharding import Mesh
from jax.sharding import PartitionSpec as P

F32 = jnp.float32
BF16 = jnp.bfloat16
NT = (((1,), (1,)), ((), ()))
VMEM_LIMIT = 24 * 1024 * 1024
IN_VMEM = pl.BlockSpec(memory_space=pltpu.VMEM)
IN_HBM = pl.BlockSpec(memory_space=pl.ANY)
IN_SMEM = pl.BlockSpec(memory_space=pltpu.SMEM)
PARAMS = pltpu.CompilerParams(vmem_limit_bytes=VMEM_LIMIT)


def cost(flops, moved_bytes):
    return pl.CostEstimate(flops=int(flops), bytes_accessed=int(moved_bytes), transcendentals=0)


def regroup_kernel(src, dst, planes, sems):
    parts, slots = src.shape[:2]
    copies = [
        pltpu.make_async_copy(src.at[part, slot], planes.at[part, slot], sems.at[part, slot])
        for part in range(parts)
        for slot in range(slots)
    ]
    for copy in copies:
        copy.start()
    for part in range(parts):
        for slot in range(slots):
            copies[part * slots + slot].wait()
            dst[:, slot * parts + part] = planes[part, slot]


def regroup(amplitudes, chips):
    parts, slots, rows, width = amplitudes.shape
    here = rows // chips
    planes = amplitudes.reshape(parts, slots, chips, here, width)
    return pl.pallas_call(
        regroup_kernel,
        out_shape=jax.ShapeDtypeStruct((chips, parts * slots, here, width), amplitudes.dtype),
        in_specs=[IN_HBM],
        out_specs=IN_VMEM,
        scratch_shapes=[pltpu.VMEM(planes.shape, planes.dtype), pltpu.SemaphoreType.DMA((parts, slots))],
        compiler_params=PARAMS,
        name="regroup",
    )(pltpu.with_memory_space_constraint(planes, pltpu.HBM))


def slab_copies(place, turn, integrals, slabs, sems):
    vir, core = place[0] % 2, (place[0] // 2) % 2
    window = 2 * core + (1 - vir if turn == 0 else vir)
    return [pltpu.make_async_copy(integrals.at[part, window], slabs.at[part], sems.at[part]) for part in range(2)]


def spread_rows(moved, wide, slots_by):
    slots = slots_by.shape[0]
    width = moved.shape[1]
    rows = moved.shape[0] // slots
    pitch = slots + 1
    slots_a_step = 32

    def step(index, carry):
        at = index * slots_a_step
        values = moved[pl.ds(pl.multiple_of(at * rows, slots_a_step * rows), slots_a_step * rows), :].astype(F32)
        for slot in range(slots_a_step):
            wide[pl.ds(at + slot, rows, stride=pitch), :] = values[slot * rows : (slot + 1) * rows]
        return carry

    lax.fori_loop(0, slots // slots_a_step, step, 0)
    for row in range(rows):
        slots_by[:, row * width : (row + 1) * width] = wide[row * pitch : row * pitch + slots, :].astype(BF16)


def ordered_blocks(moved, chooser, wide, slots_by, occupied):
    spread_rows(moved, wide, slots_by)
    width = moved.shape[1]
    rows = slots_by.shape[1] // width
    ks_a_block = 8
    for start in range(0, chooser.shape[0] // occupied, ks_a_block):
        ordered = jnp.dot(
            chooser[start * occupied : (start + ks_a_block) * occupied, :], slots_by[...], preferred_element_type=F32
        ).astype(BF16)
        for k in range(ks_a_block):
            for row in range(rows):
                block = ordered[k * occupied : (k + 1) * occupied, row * width : (row + 1) * width]
                yield slice(row * occupied, (row + 1) * occupied), slice((start + k) * width, (start + k + 1) * width), block


def choose(chooser, table, occupied):
    pairs, slots = chooser.shape
    lanes = 128
    row = lax.broadcasted_iota(jnp.int32, (pairs, lanes), 0)
    wanted = row % occupied * (pairs // occupied) + row // occupied
    for start in range(0, slots, lanes):
        chooser[:, start : start + lanes] = (table[:, start : start + lanes] == wanted).astype(BF16)


def order_kernel(place, moved, tables, integrals, matrices, slabs, there, here, wide, slots_by, sems, *, occupied):
    copies = slab_copies(place, 0, integrals, slabs, sems)
    for copy in copies:
        copy.start()
    core = (place[0] // 2) % 2
    choose(here, tables[core], occupied)
    for at, lanes, block in ordered_blocks(moved, here, wide, slots_by, occupied):
        matrices[at, lanes] = block
    choose(there, tables[1 - core], occupied)
    for copy in copies:
        copy.wait()


def order(place, moved, tables, integrals, occupied):
    slots = tables.shape[2]
    pairs = 2 * slots
    width = moved.shape[1]
    rows = moved.shape[0] // slots
    return pl.pallas_call(
        functools.partial(order_kernel, occupied=occupied),
        out_shape=(
            pltpu.VMEM((rows * occupied, pairs // occupied * width), BF16),
            pltpu.VMEM((2,) + integrals.shape[2:], BF16),
            pltpu.VMEM((pairs, slots), BF16),
        ),
        in_specs=[IN_SMEM, IN_VMEM, IN_VMEM, IN_HBM],
        out_specs=(IN_VMEM,) * 3,
        scratch_shapes=[
            pltpu.VMEM((pairs, slots), BF16),
            pltpu.VMEM(((slots + 1) * rows, width), F32),
            pltpu.VMEM((slots, rows * width), BF16),
            pltpu.SemaphoreType.DMA((2,)),
        ],
        compiler_params=PARAMS,
        cost_estimate=cost(2 * pairs * slots * rows * width, integrals.size),
        name="order",
    )(place, moved, tables, integrals)


def product_into(out, matrices, slabs, copies=()):
    half = matrices.shape[0] // 2
    for copy in copies[:1]:
        copy.wait()
    by_real = jnp.dot(matrices[...], slabs[0], preferred_element_type=F32)
    for copy in copies[1:]:
        copy.wait()
    by_imag = jnp.dot(matrices[...], slabs[1], preferred_element_type=F32)
    out[:half] = by_real[:half] - by_imag[half:]
    out[half:] = by_real[half:] + by_imag[:half]


def first_kernel(mine, moved, chooser, slabs, matrices, out, wide, slots_by, *, occupied):
    for at, lanes, block in ordered_blocks(moved, chooser, wide, slots_by, occupied):
        matrices[at, lanes] = mine[at, lanes] + block
    product_into(out, matrices, slabs)


def first_window(mine, moved, chooser, slabs, occupied):
    width = moved.shape[1]
    slots = chooser.shape[1]
    rows = moved.shape[0] // slots
    full_virtual = slabs.shape[-1]
    return pl.pallas_call(
        functools.partial(first_kernel, occupied=occupied),
        out_shape=(
            jax.ShapeDtypeStruct(mine.shape, BF16),
            jax.ShapeDtypeStruct((mine.shape[0], full_virtual), F32),
        ),
        in_specs=[IN_VMEM] * 4,
        out_specs=(IN_VMEM,) * 2,
        scratch_shapes=[pltpu.VMEM(((slots + 1) * rows, width), F32), pltpu.VMEM((slots, rows * width), BF16)],
        compiler_params=PARAMS,
        cost_estimate=cost(4 * mine.size * full_virtual, 4 * mine.size),
        name="first_window",
    )(mine, moved, chooser, pltpu.with_memory_space_constraint(slabs, pltpu.VMEM))


def second_kernel(place, matrices, integrals, out, slabs, sems):
    vir, core = place[0] % 2, (place[0] // 2) % 2
    cuts = sems.shape[1]
    depth = slabs.shape[1] // cuts
    copies = [
        pltpu.make_async_copy(
            integrals.at[part, 2 * core + vir, pl.ds(cut * depth, depth)],
            slabs.at[part, pl.ds(cut * depth, depth)],
            sems.at[part, cut],
        )
        for part in range(2)
        for cut in range(cuts)
    ]
    copies[0].start()
    copies[1].start()
    for at, copy in enumerate(copies):
        copy.wait()
        if at + 2 < len(copies):
            copies[at + 2].start()
    product_into(out, matrices, slabs)


def second_window(place, matrices, integrals):
    depth, full_virtual = integrals.shape[2:]
    return pl.pallas_call(
        second_kernel,
        out_shape=jax.ShapeDtypeStruct((matrices.shape[0], full_virtual), F32),
        in_specs=[IN_SMEM, IN_VMEM, IN_HBM],
        out_specs=IN_VMEM,
        scratch_shapes=[pltpu.VMEM((2, depth, full_virtual), BF16), pltpu.SemaphoreType.DMA((2, 4))],
        compiler_params=PARAMS,
        cost_estimate=cost(4 * matrices.size * full_virtual, 4 * matrices.size),
        name="second_window",
    )(place, matrices, integrals)


def chosen(values, order_by):
    high = values.astype(BF16)
    rest = values - high.astype(F32)
    middle = rest.astype(BF16)
    low = (rest - middle.astype(F32)).astype(BF16)
    total = lax.dot_general(low, order_by, NT, preferred_element_type=F32)
    total += lax.dot_general(middle, order_by, NT, preferred_element_type=F32)
    return total + lax.dot_general(high, order_by, NT, preferred_element_type=F32)


def combine_kernel(kept, got, natural_order, chip_order, own, mirror):
    full_virtual = kept.shape[1]
    rows = kept.shape[0] // 2
    chips = mirror.shape[0] // 8
    here = full_virtual // chips
    occupied = rows // here
    lane = lax.broadcasted_iota(jnp.int32, (occupied, 2 * chips), 1)
    values = kept[...] + got[...]
    by_chip = chosen(values, chip_order[...])
    own[...] = chosen(values, natural_order[...])
    for part in range(2):
        for row in range(0, here, 2):
            at = part * rows + row * occupied
            blocks = []
            for other in range(0, here, 2):
                lanes = slice(other * chips, (other + 2) * chips)
                low = by_chip[at : at + occupied, lanes]
                high = by_chip[at + occupied : at + 2 * occupied, lanes]
                blocks.append(jnp.where(lane < chips, low, pltpu.roll(high, chips, 1)))
                blocks.append(jnp.where(lane < chips, pltpu.roll(low, chips, 1), high))
            turned = jnp.concatenate(blocks, axis=0).T
            mirror[pl.ds(2 * row + part, chips, stride=8), :] = turned[:chips]
            mirror[pl.ds(2 * (row + 1) + part, chips, stride=8), :] = turned[chips:]


def combine(kept, got, natural_order, chip_order, chips):
    return pl.pallas_call(
        combine_kernel,
        out_shape=(jax.ShapeDtypeStruct(kept.shape, F32), jax.ShapeDtypeStruct((chips * 8, kept.shape[0] // 2), F32)),
        compiler_params=PARAMS,
        name="combine",
    )(kept, got, natural_order, chip_order)


def subtract_kernel(place, own, mirror, keep, to_core, to_vir, to_both, block):
    vir, core = place[0] % 2, (place[0] // 2) % 2
    here = 2 * block.shape[1]
    rows, full_virtual = own.shape[0] // 2, own.shape[1]
    occupied = rows // here
    half = full_virtual // 2
    lanes = (slice(0, half), slice(half, full_virtual))
    for part in range(2):
        values = own[part * rows : (part + 1) * rows] - mirror[pl.ds(part, full_virtual, stride=2), :].T
        for row in range(here):
            for side in range(2):
                block[part, row // 2, side, pl.ds(row % 2, occupied, stride=2), :] = values[
                    row * occupied : (row + 1) * occupied, lanes[side]
                ]
    for target, to_side, to_half in (
        (keep, core, vir),
        (to_core, 1 - core, vir),
        (to_vir, core, 1 - vir),
        (to_both, 1 - core, 1 - vir),
    ):
        for part in range(2):
            target[part] = block[part, to_side, to_half].astype(BF16)


def subtract(place, own, mirror):
    rows, full_virtual = own.shape[0] // 2, own.shape[1]
    piece = jax.ShapeDtypeStruct((2, rows // 2, full_virtual // 2), BF16)
    return pl.pallas_call(
        subtract_kernel,
        out_shape=(piece,) * 4,
        in_specs=[IN_SMEM, IN_VMEM, IN_VMEM],
        out_specs=(IN_VMEM,) * 4,
        scratch_shapes=[pltpu.VMEM((2, 2, 2, rows // 2, full_virtual // 2), F32)],
        compiler_params=PARAMS,
        name="subtract",
    )(place, own, mirror)


def finish_kernel(place, keep, from_core, from_vir, from_both, out):
    vir, core = place[0] % 2, (place[0] // 2) % 2
    out[:, 2 * core + vir] = keep[...]
    out[:, 2 * (1 - core) + vir] = from_core[...]
    out[:, 2 * core + 1 - vir] = from_vir[...]
    out[:, 2 * (1 - core) + 1 - vir] = from_both[...]


def finish(place, pieces):
    _, rows, width = pieces[0].shape
    return pl.pallas_call(
        finish_kernel,
        out_shape=jax.ShapeDtypeStruct((2, 4, rows, width), BF16),
        in_specs=[IN_SMEM] + [IN_VMEM] * 4,
        out_specs=IN_VMEM,
        compiler_params=PARAMS,
        name="finish",
    )(place, *pieces)


SWAP = [(0, 1), (1, 0)]
SWAP_BOTH = [(0, 3), (1, 2), (2, 1), (3, 0)]


def body(amplitudes, integrals, pair_table, kramers):
    chips = lax.axis_size("chip")
    place = lax.axis_index(("chip", "core", "vir")).astype(jnp.int32).reshape(1)
    windows, summed_occ = integrals.shape[1:3]
    pairs = pair_table.shape[0]
    occupied = pairs // summed_occ
    slots, full_virtual, width = amplitudes.shape[1:]
    here = full_virtual // chips

    pieces = regroup(amplitudes, chips)
    moved = lax.all_to_all(pieces, "chip", split_axis=0, concat_axis=0, tiled=True)
    moved = moved.reshape(-1, width)
    flat = integrals.reshape(2, windows, summed_occ * integrals.shape[3], full_virtual)
    flat = pltpu.with_memory_space_constraint(flat, pltpu.HBM)
    across = lax.ppermute(moved, "core", SWAP)

    tables = pair_table.reshape(chips, 2, slots).transpose(1, 0, 2).reshape(2, 1, chips * slots)
    places = jnp.arange(full_virtual, dtype=jnp.int32)[:, None]
    natural_order = (kramers[None, :] == places).astype(BF16)
    chip_order = (kramers[None, :] == places % chips * here + places // chips).astype(BF16)

    mine, slabs, chooser = order(place, moved, tables, flat, occupied)
    matrices, to_send = first_window(mine, across, chooser, slabs, occupied)
    got = lax.ppermute(to_send, "vir", SWAP)
    kept = second_window(place, matrices, flat)
    own, mirror = combine(kept, got, natural_order, chip_order, chips)
    mirror = lax.all_to_all(mirror.reshape(chips, 8, -1), "chip", split_axis=0, concat_axis=0, tiled=True)
    keep, to_core, to_vir, to_both = subtract(place, own, mirror.reshape(chips * 8, -1))
    from_vir = lax.ppermute(to_vir, "vir", SWAP)
    from_both = lax.ppermute(to_both, ("core", "vir"), SWAP_BOTH)
    from_core = lax.ppermute(to_core, "core", SWAP)
    got_pieces = (keep, from_core, from_vir, from_both)
    out = finish(place, got_pieces)
    return out.reshape(2, windows, occupied, here // 2, width)


def solution(mesh):
    pair, vir = mesh.devices.shape
    split = Mesh(mesh.devices.reshape(pair // 2, 2, vir), ("chip", "core", "vir"))
    over_pair = ("chip", "core")
    placed = (P(None, over_pair, None, "vir"), P(None, None, None, "vir", None), P(), P())
    return jax.shard_map(
        body,
        mesh=split,
        in_specs=placed,
        out_specs=P(None, None, None, over_pair, "vir"),
        check_vma=False,
    )
```

time: 176 us -> 81.4 us (0.46)
  local copies, waits for them, and re-layouts: 44.5 us -> 0.31 us
  waiting for transfers between devices: 34.8 us -> 4.57 us
  starting transfers between devices: 24.5 us -> 8.17 us
  Pallas kernels: 0 us -> 13 us
  other arithmetic: 9.5 us -> 0.11 us
  matrix products: 8.94 us -> 0 us
  blocking collectives: 51.8 us -> 54.9 us
    all_to_all x0 -> x2, blocking collectives: none -> 54.9 us  [the longest x1 37.8 us: body(): lax.all_to_all(pieces, 'chip', split_axis=0, concat_axis=0, tiled=True)]
    unnamed x1 -> x0, blocking collectives: 51.8 us -> none
    all_to_all x2 -> x0, waiting for transfers between devices: 34.8 us -> none  [the longest x1 19.2 us: body(): lax.all_to_all(cycle, 'pair', split_axis=4, concat_axis=3, tiled=True)]
    all_to_all x2 -> x0, starting transfers between devices: 24.5 us -> none  [the longest x1 16.4 us: body(): lax.all_to_all(amplitudes, 'pair', split_axis=2, concat_axis=1, tiled=True)]
    unnamed x33 -> x4, local copies, waits for them, and re-layouts: 13.9 us -> 0.01 us
    pallas_call x0 -> x7, Pallas kernels: none -> 13 us  [the longest x1 5.24 us: second_window(): pl.pallas_call(second_kernel, out_shape=jax.ShapeDtypeStruct((matrices.sh...]
    slice x2 -> x0, local copies, waits for them, and re-layouts: 9.13 us -> none  [the longest x1 9.05 us: contract(): slab_matrix[0]]
    dot_general x16 -> x0, matrix products: 8.94 us -> none  [the longest x4 2.99 us: contract(): jnp.dot(matrices[0], slab_matrix[1], preferred_element_type=jnp.float32)]
  transfers between devices with their start and end apart: 2 -> 5, of which waited for: 2 -> 3; matrix products, arithmetic and copies ran while one was open for 8% -> 1% of each run, Pallas kernels for 0% -> 9%
where the time goes in v1:
time: 81.4 us; the launch traced here: 81.1 us
  blocking collectives  54.9 us (67%)
  Pallas kernels  13 us (16%)
  starting transfers between devices  8.17 us (10%)
  waiting for transfers between devices  4.57 us (6%)
    all_to_all x1, blocking collectives, body(): lax.all_to_all(pieces, 'chip', split_axis=0, concat_axis=0, tiled=True)  37.8 us
    all_to_all x1, blocking collectives, body(): lax.all_to_all(mirror.reshape(chips, 8, -1), 'chip', split_axis=0, concat...  17.1 us
    pallas_call x1, Pallas kernels, second_window(): pl.pallas_call(second_kernel, out_shape=jax.ShapeDtypeStruct((matrices.sh...  5.24 us
    pallas_call x1, Pallas kernels, first_window(): pl.pallas_call(functools.partial(first_kernel, occupied=occupied), out_sh...  3.13 us
    ppermute x1, starting transfers between devices, body(): across = lax.ppermute(moved, 'core', SWAP)  3.05 us
    ppermute x1, starting transfers between devices, body(): from_core = lax.ppermute(to_core, 'core', SWAP)  2.99 us
    ppermute x1, waiting for transfers between devices, body(): got = lax.ppermute(to_send, 'vir', SWAP)  2.27 us
    pallas_call x1, Pallas kernels, order(): pl.pallas_call(functools.partial(order_kernel, occupied=occupied), out_sh...  1.92 us
  transfers between devices with their start and end apart: 5, of which 3 were waited for; matrix products, arithmetic and copies ran while one was open for 1% of the time, Pallas kernels for 9%

profile of v1, /device:TPU:1, one launch (start us, length us, event | category | flops | bytes accessed | tf_op | source)
XLA Modules:
  0.0 81.1 jit_solution(5988618749569739426)
XLA Ops:
  0.0 0.0 copy-start
  0.0 1.3 %regroup.1 = bf16[64,12,4,128]{3,2,1,0:T(4,128)(2,1)S(1)} custom-call(bf16[2,6,64,4,128]{4,3,2,1,0:T(4,128)(2,1)} %bitcast.14), custom_call_target="tpu_custom_call" | custom-call | tf_op jit(solution)/shard_map/regroup/pallas_call | solution.py:44
  1.3 37.8 %all_to_all.10 = bf16[64,12,4,128]{3,2,1,0:T(4,128)(2,1)S(1)} all-to-all(bf16[64,12,4,128]{3,2,1,0:T(4,128)(2,1)S(1)} %regroup.1), channel_id=1, replica_groups=mesh['chip'=64,'core'=2,'vir'=2] {'chip'}, dimensions={0} | all-to-all | bytes 1572864 | tf_op jit(solution)/shard_map/all_to_all | solution.py:333
  39.1 3.0 %collective-permute-start = (bf16[3072,128]{1,0:T(8,128)(2,1)S(1)}, bf16[3072,128]{1,0:T(8,128)(2,1)S(1)}, u32[]{:S(2)}, u32[]{:S(2)}) collective-permute-start(bf16[3072,128]{1,0:T(8,128)(2,1)S(1)} %bitcast.8), channel_id=1, source_target_pairs={{0,2},{2,0},{1,3},{3,1},{4,6},{6,4},{5,7},{7,5},{8,10},{10,8},{9,1... | collective-permute-start | bytes 2359304 | tf_op jit(solution)/shard_map/ppermute | solution.py:337
  42.2 0.0 copy-done
  42.2 0.2 reshape.86
  42.3 0.1 reshape.92.tables
  42.5 1.9 %order.1 = (bf16[256,3072]{1,0:T(8,128)(2,1)S(1)}, bf16[2,3072,256]{2,1,0:T(8,128)(2,1)S(1)}, bf16[768,384]{1,0:T(8,128)(2,1)S(1)}) custom-call(s32[1]{0:T(128)} %bitcast.place, bf16[3072,128]{1,0:T(8,128)(2,1)S(1)} %bitcast.9, s32[2,1,384]{2,1,0:T(1,128)S(1)} %reshape.92.tables, bf16[2,4,3072,256]{3,2,1,0:T(8,128)(2,1)} %bitcast.12), custom_call_target="tpu_custom_call" | custom-call | flops 603979776 | bytes 6291456 | tf_op jit(solution)/shard_map/order/pallas_call | solution.py:122
  44.4 0.0 copy-start.1
  44.4 0.0 collective-permute-done.moved
  44.4 3.1 %first_window.1 = (bf16[256,3072]{1,0:T(8,128)(2,1)S(1)}, f32[256,256]{1,0:T(8,128)S(1)}) custom-call(bf16[256,3072]{1,0:T(8,128)(2,1)S(1)} %get-tuple-element.16.mine, bf16[3072,128]{1,0:T(8,128)(2,1)S(1)} %collective-permute-done.moved, bf16[768,384]{1,0:T(8,128)(2,1)S(1)} %get-tuple-element.17.chooser, bf16[2,3072,256]{2,1,0:T(8,128)(2,1)S(1)} %get-tuple-element.18.slabs), custom_call_target="tpu_custom_call" | custom-call | flops 805306368 | bytes 3145728 | tf_op jit(solution)/shard_map/first_window/pallas_call | solution.py:166
  47.6 0.4 collective-permute-start.1
  48.0 0.0 copy-done.1
  48.0 0.1 compare_convert_fusion
  48.1 5.2 %second_window.1.kept = f32[256,256]{1,0:T(8,128)S(1)} custom-call(s32[1]{0:T(128)} %bitcast.place, bf16[256,3072]{1,0:T(8,128)(2,1)S(1)} %get-tuple-element.19.matrices, bf16[2,4,3072,256]{3,2,1,0:T(8,128)(2,1)} %bitcast.13), custom_call_target="tpu_custom_call" | custom-call | flops 805306368 | bytes 3145728 | tf_op jit(solution)/shard_map/second_window/pallas_call | solution.py:205
  53.3 2.3 %collective-permute-done.1.got = f32[256,256]{1,0:T(8,128)S(1)} collective-permute-done((f32[256,256]{1,0:T(8,128)S(1)}, f32[256,256]{1,0:T(8,128)S(1)}, u32[]{:S(2)}, u32[]{:S(2)}) %collective-permute-start.1) | collective-permute-done | bytes 262176 | tf_op jit(solution)/shard_map/ppermute | solution.py:346
  55.6 0.6 combine.1
  56.2 17.1 %all_to_all.11 = f32[64,8,128]{2,1,0:T(8,128)S(1)} all-to-all(f32[64,8,128]{2,1,0:T(8,128)S(1)} %bitcast.11), channel_id=1, replica_groups=mesh['chip'=64,'core'=2,'vir'=2] {'chip'}, dimensions={0} | all-to-all | bytes 524288 | tf_op jit(solution)/shard_map/all_to_all | solution.py:349
  73.3 0.1 subtract.1
  73.5 3.0 %collective-permute-start.2 = (bf16[2,64,128]{2,1,0:T(8,128)(2,1)S(1)}, bf16[2,64,128]{2,1,0:T(8,128)(2,1)S(1)}, u32[]{:S(2)}, u32[]{:S(2)}) collective-permute-start(bf16[2,64,128]{2,1,0:T(8,128)(2,1)S(1)} %get-tuple-element.24), channel_id=1, source_target_pairs={{0,2},{2,0},{1,3},{3,1},{4,6},{6,4},{5,7},{7,5},{8,10},{10,8},{9,1... | collective-permute-start | bytes 98312 | tf_op jit(solution)/shard_map/ppermute | solution.py:353
  76.4 0.3 collective-permute-start.3
  76.8 1.4 %collective-permute-start.4 = (bf16[2,64,128]{2,1,0:T(8,128)(2,1)S(1)}, bf16[2,64,128]{2,1,0:T(8,128)(2,1)S(1)}, u32[]{:S(2)}, u32[]{:S(2)}) collective-permute-start(bf16[2,64,128]{2,1,0:T(8,128)(2,1)S(1)} %get-tuple-element.26), channel_id=1, source_target_pairs={{0,3},{1,2},{2,1},{3,0},{4,7},{5,6},{6,5},{7,4},{8,11},{9,10},{10,... | collective-permute-start | bytes 98312 | tf_op jit(solution)/shard_map/ppermute | solution.py:352
  78.2 0.0 collective-permute-done.2.from_core
  78.2 1.0 %collective-permute-done.3.from_vir = bf16[2,64,128]{2,1,0:T(8,128)(2,1)S(1)} collective-permute-done((bf16[2,64,128]{2,1,0:T(8,128)(2,1)S(1)}, bf16[2,64,128]{2,1,0:T(8,128)(2,1)S(1)}, u32[]{:S(2)}, u32[]{:S(2)}) %collective-permute-start.3) | collective-permute-done | bytes 32800 | tf_op jit(solution)/shard_map/ppermute | solution.py:351
  79.2 1.2 %collective-permute-done.4.from_both = bf16[2,64,128]{2,1,0:T(8,128)(2,1)S(1)} collective-permute-done((bf16[2,64,128]{2,1,0:T(8,128)(2,1)S(1)}, bf16[2,64,128]{2,1,0:T(8,128)(2,1)S(1)}, u32[]{:S(2)}, u32[]{:S(2)}) %collective-permute-start.4) | collective-permute-done | bytes 32800 | tf_op jit(solution)/shard_map/ppermute | solution.py:352
  80.5 0.7 finish.1
  (2 shorter events, 0.0 us)
Async XLA Ops:
  0.0 42.2 %copy-start = (s32[768]{0:T(1024)S(1)}, s32[768]{0:T(1024)}, u32[]{:S(2)}) copy-start(s32[768]{0:T(1024)} %param.6) | copy-start | bytes 9220
  39.1 5.3 %collective-permute-start = (bf16[3072,128]{1,0:T(8,128)(2,1)S(1)}, bf16[3072,128]{1,0:T(8,128)(2,1)S(1)}, u32[]{:S(2)}, u32[]{:S(2)}) collective-permute-start(bf16[3072,128]{1,0:T(8,128)(2,1)S(1)} %bitcast.8), channel_id=1, source_target_pairs={{0,2},{2,0},{1,3},{3,1},{4,6},{6,4},{5,7},{7,5},{8,10},{10,8},{9,1... | collective-permute-start | bytes 2359304 | tf_op jit(solution)/shard_map/ppermute | solution.py:337
  44.4 3.6 %copy-start.1 = (s32[256]{0:T(256)S(1)}, s32[256]{0:T(256)}, u32[]{:S(2)}) copy-start(s32[256]{0:T(256)} %param.7) | copy-start | bytes 3076
  47.6 8.0 %collective-permute-start.1 = (f32[256,256]{1,0:T(8,128)S(1)}, f32[256,256]{1,0:T(8,128)S(1)}, u32[]{:S(2)}, u32[]{:S(2)}) collective-permute-start(f32[256,256]{1,0:T(8,128)S(1)} %get-tuple-element.20), channel_id=1, source_target_pairs={{0,1},{1,0},{2,3},{3,2},{4,5},{5,4},{6,7},{7,6},{8,9},{9,8},{10,11... | collective-permute-start | bytes 786440 | tf_op jit(solution)/shard_map/ppermute | solution.py:346
  73.5 4.7 %collective-permute-start.2 = (bf16[2,64,128]{2,1,0:T(8,128)(2,1)S(1)}, bf16[2,64,128]{2,1,0:T(8,128)(2,1)S(1)}, u32[]{:S(2)}, u32[]{:S(2)}) collective-permute-start(bf16[2,64,128]{2,1,0:T(8,128)(2,1)S(1)} %get-tuple-element.24), channel_id=1, source_target_pairs={{0,2},{2,0},{1,3},{3,1},{4,6},{6,4},{5,7},{7,5},{8,10},{10,8},{9,1... | collective-permute-start | bytes 98312 | tf_op jit(solution)/shard_map/ppermute | solution.py:353
  76.4 2.8 %collective-permute-start.3 = (bf16[2,64,128]{2,1,0:T(8,128)(2,1)S(1)}, bf16[2,64,128]{2,1,0:T(8,128)(2,1)S(1)}, u32[]{:S(2)}, u32[]{:S(2)}) collective-permute-start(bf16[2,64,128]{2,1,0:T(8,128)(2,1)S(1)} %get-tuple-element.25), channel_id=1, source_target_pairs={{0,1},{1,0},{2,3},{3,2},{4,5},{5,4},{6,7},{7,6},{8,9},{9,8},{10,11... | collective-permute-start | bytes 98312 | tf_op jit(solution)/shard_map/ppermute | solution.py:351
  76.8 3.7 %collective-permute-start.4 = (bf16[2,64,128]{2,1,0:T(8,128)(2,1)S(1)}, bf16[2,64,128]{2,1,0:T(8,128)(2,1)S(1)}, u32[]{:S(2)}, u32[]{:S(2)}) collective-permute-start(bf16[2,64,128]{2,1,0:T(8,128)(2,1)S(1)} %get-tuple-element.26), channel_id=1, source_target_pairs={{0,3},{1,2},{2,1},{3,0},{4,7},{5,6},{6,5},{7,4},{8,11},{9,10},{10,... | collective-permute-start | bytes 98312 | tf_op jit(solution)/shard_map/ppermute | solution.py:352

commit v2 on v1

--- a/solution.py
+++ b/solution.py
@@ -13,6 +13,7 @@
 NT = (((1,), (1,)), ((), ()))
 VMEM_LIMIT = 24 * 1024 * 1024
 IN_VMEM = pl.BlockSpec(memory_space=pltpu.VMEM)
+KS_A_BLOCK = 8
 IN_HBM = pl.BlockSpec(memory_space=pl.ANY)
 IN_SMEM = pl.BlockSpec(memory_space=pltpu.SMEM)
 PARAMS = pltpu.CompilerParams(vmem_limit_bytes=VMEM_LIMIT)
@@ -77,19 +78,16 @@
         slots_by[:, row * width : (row + 1) * width] = wide[row * pitch : row * pitch + slots, :].astype(BF16)
 
 
-def ordered_blocks(moved, chooser, wide, slots_by, occupied):
-    spread_rows(moved, wide, slots_by)
-    width = moved.shape[1]
-    rows = slots_by.shape[1] // width
-    ks_a_block = 8
-    for start in range(0, chooser.shape[0] // occupied, ks_a_block):
-        ordered = jnp.dot(
-            chooser[start * occupied : (start + ks_a_block) * occupied, :], slots_by[...], preferred_element_type=F32
-        ).astype(BF16)
-        for k in range(ks_a_block):
-            for row in range(rows):
-                block = ordered[k * occupied : (k + 1) * occupied, row * width : (row + 1) * width]
-                yield slice(row * occupied, (row + 1) * occupied), slice((start + k) * width, (start + k + 1) * width), block
+def order_block(start, chooser, slots_by, matrices, mine, width, occupied):
+    ordered = jnp.dot(
+        chooser[start * occupied : (start + KS_A_BLOCK) * occupied, :], slots_by[...], preferred_element_type=F32
+    ).astype(BF16)
+    for k in range(KS_A_BLOCK):
+        for row in range(slots_by.shape[1] // width):
+            at = slice(row * occupied, (row + 1) * occupied)
+            lanes = slice((start + k) * width, (start + k + 1) * width)
+            block = ordered[k * occupied : (k + 1) * occupied, row * width : (row + 1) * width]
+            matrices[at, lanes] = block if mine is None else mine[at, lanes] + block
 
 
 def choose(chooser, table, occupied):
@@ -107,8 +105,9 @@
         copy.start()
     core = (place[0] // 2) % 2
     choose(here, tables[core], occupied)
-    for at, lanes, block in ordered_blocks(moved, here, wide, slots_by, occupied):
-        matrices[at, lanes] = block
+    spread_rows(moved, wide, slots_by)
+    for start in range(0, here.shape[0] // occupied, KS_A_BLOCK):
+        order_block(start, here, slots_by, matrices, None, moved.shape[1], occupied)
     choose(there, tables[1 - core], occupied)
     for copy in copies:
         copy.wait()
@@ -152,10 +151,18 @@
     out[half:] = by_real[half:] + by_imag[:half]
 
 
-def first_kernel(mine, moved, chooser, slabs, matrices, out, wide, slots_by, *, occupied):
-    for at, lanes, block in ordered_blocks(moved, chooser, wide, slots_by, occupied):
-        matrices[at, lanes] = mine[at, lanes] + block
-    product_into(out, matrices, slabs)
+def first_kernel(mine, moved, chooser, slabs, matrices, out, wide, slots_by, by_real, by_imag, *, occupied):
+    half = matrices.shape[0] // 2
+    width = moved.shape[1]
+    spread_rows(moved, wide, slots_by)
+    for start in range(0, chooser.shape[0] // occupied, KS_A_BLOCK):
+        order_block(start, chooser, slots_by, matrices, mine, width, occupied)
+        lanes = slice(start * width, (start + KS_A_BLOCK) * width)
+        for part, total in enumerate((by_real, by_imag)):
+            product = jnp.dot(matrices[:, lanes], slabs[part, lanes], preferred_element_type=F32)
+            total[...] = product if start == 0 else total[...] + product
+    out[:half] = by_real[:half] - by_imag[half:]
+    out[half:] = by_real[half:] + by_imag[:half]
 
 
 def first_window(mine, moved, chooser, slabs, occupied):
@@ -171,7 +178,12 @@
         ),
         in_specs=[IN_VMEM] * 4,
         out_specs=(IN_VMEM,) * 2,
-        scratch_shapes=[pltpu.VMEM(((slots + 1) * rows, width), F32), pltpu.VMEM((slots, rows * width), BF16)],
+        scratch_shapes=[
+            pltpu.VMEM(((slots + 1) * rows, width), F32),
+            pltpu.VMEM((slots, rows * width), BF16),
+            pltpu.VMEM((mine.shape[0], full_virtual), F32),
+            pltpu.VMEM((mine.shape[0], full_virtual), F32),
+        ],
         compiler_params=PARAMS,
         cost_estimate=cost(4 * mine.size * full_virtual, 4 * mine.size),
         name="first_window",
@@ -179,25 +191,10 @@
 
 
 def second_kernel(place, matrices, integrals, out, slabs, sems):
-    vir, core = place[0] % 2, (place[0] // 2) % 2
-    cuts = sems.shape[1]
-    depth = slabs.shape[1] // cuts
-    copies = [
-        pltpu.make_async_copy(
-            integrals.at[part, 2 * core + vir, pl.ds(cut * depth, depth)],
-            slabs.at[part, pl.ds(cut * depth, depth)],
-            sems.at[part, cut],
-        )
-        for part in range(2)
-        for cut in range(cuts)
-    ]
-    copies[0].start()
-    copies[1].start()
-    for at, copy in enumerate(copies):
-        copy.wait()
-        if at + 2 < len(copies):
-            copies[at + 2].start()
-    product_into(out, matrices, slabs)
+    copies = slab_copies(place, 1, integrals, slabs, sems)
+    for copy in copies:
+        copy.start()
+    product_into(out, matrices, slabs, copies)
 
 
 def second_window(place, matrices, integrals):
@@ -207,7 +204,7 @@
         out_shape=jax.ShapeDtypeStruct((matrices.shape[0], full_virtual), F32),
         in_specs=[IN_SMEM, IN_VMEM, IN_HBM],
         out_specs=IN_VMEM,
-        scratch_shapes=[pltpu.VMEM((2, depth, full_virtual), BF16), pltpu.SemaphoreType.DMA((2, 4))],
+        scratch_shapes=[pltpu.VMEM((2, depth, full_virtual), BF16), pltpu.SemaphoreType.DMA((2,))],
         compiler_params=PARAMS,
         cost_estimate=cost(4 * matrices.size * full_virtual, 4 * matrices.size),
         name="second_window",

time: 81.4 us -> 80.8 us (level)
  Pallas kernels: 13 us -> 10.6 us
  waiting for transfers between devices: 4.57 us -> 6.44 us
    pallas_call x1, Pallas kernels: 5.24 us -> 3.36 us  [second_window(): pl.pallas_call(second_kernel, out_shape=jax.ShapeDtypeStruct((matrices.sh...]
    ppermute x1, waiting for transfers between devices: 2.27 us -> 4.15 us  [body(): got = lax.ppermute(to_send, 'vir', SWAP)]
  transfers between devices with their start and end apart: 5 -> 5, of which waited for: 3 -> 3; matrix products, arithmetic and copies ran while one was open for 1% -> 1% of each run, Pallas kernels for 9% -> 7%
where the time goes in v2:
time: 80.8 us; the launch traced here: 80.6 us
  blocking collectives  54.9 us (68%)
  Pallas kernels  10.6 us (13%)
  starting transfers between devices  8.17 us (10%)
  waiting for transfers between devices  6.44 us (8%)
    all_to_all x1, blocking collectives, body(): lax.all_to_all(pieces, 'chip', split_axis=0, concat_axis=0, tiled=True)  37.8 us
    all_to_all x1, blocking collectives, body(): lax.all_to_all(mirror.reshape(chips, 8, -1), 'chip', split_axis=0, concat...  17.1 us
    ppermute x1, waiting for transfers between devices, body(): got = lax.ppermute(to_send, 'vir', SWAP)  4.15 us
    pallas_call x1, Pallas kernels, second_window(): pl.pallas_call(second_kernel, out_shape=jax.ShapeDtypeStruct((matrices.sh...  3.36 us
    ppermute x1, starting transfers between devices, body(): across = lax.ppermute(moved, 'core', SWAP)  3.05 us
    ppermute x1, starting transfers between devices, body(): from_core = lax.ppermute(to_core, 'core', SWAP)  2.99 us
    pallas_call x1, Pallas kernels, first_window(): pl.pallas_call(functools.partial(first_kernel, occupied=occupied), out_sh...  2.6 us
    pallas_call x1, Pallas kernels, order(): pl.pallas_call(functools.partial(order_kernel, occupied=occupied), out_sh...  1.92 us
  transfers between devices with their start and end apart: 5, of which 3 were waited for; matrix products, arithmetic and copies ran while one was open for 1% of the time, Pallas kernels for 7%

profile of v2, /device:TPU:1, one launch (start us, length us, event | category | flops | bytes accessed | tf_op | source)
XLA Modules:
  0.0 80.6 jit_solution(8089091318740049155)
XLA Ops:
  0.0 0.0 copy-start
  0.0 1.3 %regroup.1 = bf16[64,12,4,128]{3,2,1,0:T(4,128)(2,1)S(1)} custom-call(bf16[2,6,64,4,128]{4,3,2,1,0:T(4,128)(2,1)} %bitcast.14), custom_call_target="tpu_custom_call" | custom-call | tf_op jit(solution)/shard_map/regroup/pallas_call | solution.py:45
  1.3 37.8 %all_to_all.10 = bf16[64,12,4,128]{3,2,1,0:T(4,128)(2,1)S(1)} all-to-all(bf16[64,12,4,128]{3,2,1,0:T(4,128)(2,1)S(1)} %regroup.1), channel_id=1, replica_groups=mesh['chip'=64,'core'=2,'vir'=2] {'chip'}, dimensions={0} | all-to-all | bytes 1572864 | tf_op jit(solution)/shard_map/all_to_all | solution.py:330
  39.1 3.0 %collective-permute-start = (bf16[3072,128]{1,0:T(8,128)(2,1)S(1)}, bf16[3072,128]{1,0:T(8,128)(2,1)S(1)}, u32[]{:S(2)}, u32[]{:S(2)}) collective-permute-start(bf16[3072,128]{1,0:T(8,128)(2,1)S(1)} %bitcast.8), channel_id=1, source_target_pairs={{0,2},{2,0},{1,3},{3,1},{4,6},{6,4},{5,7},{7,5},{8,10},{10,8},{9,1... | collective-permute-start | bytes 2359304 | tf_op jit(solution)/shard_map/ppermute | solution.py:334
  42.2 0.0 copy-done
  42.2 0.2 reshape.86
  42.3 0.1 reshape.92.tables
  42.5 1.9 %order.1 = (bf16[256,3072]{1,0:T(8,128)(2,1)S(1)}, bf16[2,3072,256]{2,1,0:T(8,128)(2,1)S(1)}, bf16[768,384]{1,0:T(8,128)(2,1)S(1)}) custom-call(s32[1]{0:T(128)} %bitcast.place, bf16[3072,128]{1,0:T(8,128)(2,1)S(1)} %bitcast.9, s32[2,1,384]{2,1,0:T(1,128)S(1)} %reshape.92.tables, bf16[2,4,3072,256]{3,2,1,0:T(8,128)(2,1)} %bitcast.12), custom_call_target="tpu_custom_call" | custom-call | flops 603979776 | bytes 6291456 | tf_op jit(solution)/shard_map/order/pallas_call | solution.py:121
  44.4 0.0 copy-start.1
  44.4 0.0 collective-permute-done.moved
  44.4 2.6 %first_window.1 = (bf16[256,3072]{1,0:T(8,128)(2,1)S(1)}, f32[256,256]{1,0:T(8,128)S(1)}) custom-call(bf16[256,3072]{1,0:T(8,128)(2,1)S(1)} %get-tuple-element.16.mine, bf16[3072,128]{1,0:T(8,128)(2,1)S(1)} %collective-permute-done.moved, bf16[768,384]{1,0:T(8,128)(2,1)S(1)} %get-tuple-element.17.chooser, bf16[2,3072,256]{2,1,0:T(8,128)(2,1)S(1)} %get-tuple-element.18.slabs), custom_call_target="tpu_custom_call" | custom-call | flops 805306368 | bytes 3145728 | tf_op jit(solution)/shard_map/first_window/pallas_call | solution.py:173
  47.1 0.4 collective-permute-start.1
  47.5 0.0 copy-done.1
  47.5 0.1 compare_convert_fusion
  47.6 3.4 %second_window.1.kept = f32[256,256]{1,0:T(8,128)S(1)} custom-call(s32[1]{0:T(128)} %bitcast.place, bf16[256,3072]{1,0:T(8,128)(2,1)S(1)} %get-tuple-element.19.matrices, bf16[2,4,3072,256]{3,2,1,0:T(8,128)(2,1)} %bitcast.13), custom_call_target="tpu_custom_call" | custom-call | flops 805306368 | bytes 3145728 | tf_op jit(solution)/shard_map/second_window/pallas_call | solution.py:202
  50.9 4.1 %collective-permute-done.1.got = f32[256,256]{1,0:T(8,128)S(1)} collective-permute-done((f32[256,256]{1,0:T(8,128)S(1)}, f32[256,256]{1,0:T(8,128)S(1)}, u32[]{:S(2)}, u32[]{:S(2)}) %collective-permute-start.1) | collective-permute-done | bytes 262176 | tf_op jit(solution)/shard_map/ppermute | solution.py:343
  55.1 0.6 combine.1
  55.7 17.1 %all_to_all.11 = f32[64,8,128]{2,1,0:T(8,128)S(1)} all-to-all(f32[64,8,128]{2,1,0:T(8,128)S(1)} %bitcast.11), channel_id=1, replica_groups=mesh['chip'=64,'core'=2,'vir'=2] {'chip'}, dimensions={0} | all-to-all | bytes 524288 | tf_op jit(solution)/shard_map/all_to_all | solution.py:346
  72.8 0.1 subtract.1
  72.9 3.0 %collective-permute-start.2 = (bf16[2,64,128]{2,1,0:T(8,128)(2,1)S(1)}, bf16[2,64,128]{2,1,0:T(8,128)(2,1)S(1)}, u32[]{:S(2)}, u32[]{:S(2)}) collective-permute-start(bf16[2,64,128]{2,1,0:T(8,128)(2,1)S(1)} %get-tuple-element.24), channel_id=1, source_target_pairs={{0,2},{2,0},{1,3},{3,1},{4,6},{6,4},{5,7},{7,5},{8,10},{10,8},{9,1... | collective-permute-start | bytes 98312 | tf_op jit(solution)/shard_map/ppermute | solution.py:350
  75.9 0.3 collective-permute-start.3
  76.2 1.4 %collective-permute-start.4 = (bf16[2,64,128]{2,1,0:T(8,128)(2,1)S(1)}, bf16[2,64,128]{2,1,0:T(8,128)(2,1)S(1)}, u32[]{:S(2)}, u32[]{:S(2)}) collective-permute-start(bf16[2,64,128]{2,1,0:T(8,128)(2,1)S(1)} %get-tuple-element.26), channel_id=1, source_target_pairs={{0,3},{1,2},{2,1},{3,0},{4,7},{5,6},{6,5},{7,4},{8,11},{9,10},{10,... | collective-permute-start | bytes 98312 | tf_op jit(solution)/shard_map/ppermute | solution.py:349
  77.7 0.0 collective-permute-done.2.from_core
  77.7 1.0 %collective-permute-done.3.from_vir = bf16[2,64,128]{2,1,0:T(8,128)(2,1)S(1)} collective-permute-done((bf16[2,64,128]{2,1,0:T(8,128)(2,1)S(1)}, bf16[2,64,128]{2,1,0:T(8,128)(2,1)S(1)}, u32[]{:S(2)}, u32[]{:S(2)}) %collective-permute-start.3) | collective-permute-done | bytes 32800 | tf_op jit(solution)/shard_map/ppermute | solution.py:348
  78.7 1.2 %collective-permute-done.4.from_both = bf16[2,64,128]{2,1,0:T(8,128)(2,1)S(1)} collective-permute-done((bf16[2,64,128]{2,1,0:T(8,128)(2,1)S(1)}, bf16[2,64,128]{2,1,0:T(8,128)(2,1)S(1)}, u32[]{:S(2)}, u32[]{:S(2)}) %collective-permute-start.4) | collective-permute-done | bytes 32800 | tf_op jit(solution)/shard_map/ppermute | solution.py:349
  80.0 0.7 finish.1
  (2 shorter events, 0.0 us)
Async XLA Ops:
  0.0 42.2 %copy-start = (s32[768]{0:T(1024)S(1)}, s32[768]{0:T(1024)}, u32[]{:S(2)}) copy-start(s32[768]{0:T(1024)} %param.6) | copy-start | bytes 9220
  39.1 5.3 %collective-permute-start = (bf16[3072,128]{1,0:T(8,128)(2,1)S(1)}, bf16[3072,128]{1,0:T(8,128)(2,1)S(1)}, u32[]{:S(2)}, u32[]{:S(2)}) collective-permute-start(bf16[3072,128]{1,0:T(8,128)(2,1)S(1)} %bitcast.8), channel_id=1, source_target_pairs={{0,2},{2,0},{1,3},{3,1},{4,6},{6,4},{5,7},{7,5},{8,10},{10,8},{9,1... | collective-permute-start | bytes 2359304 | tf_op jit(solution)/shard_map/ppermute | solution.py:334
  44.4 3.0 %copy-start.1 = (s32[256]{0:T(256)S(1)}, s32[256]{0:T(256)}, u32[]{:S(2)}) copy-start(s32[256]{0:T(256)} %param.7) | copy-start | bytes 3076
  47.1 8.0 %collective-permute-start.1 = (f32[256,256]{1,0:T(8,128)S(1)}, f32[256,256]{1,0:T(8,128)S(1)}, u32[]{:S(2)}, u32[]{:S(2)}) collective-permute-start(f32[256,256]{1,0:T(8,128)S(1)} %get-tuple-element.20), channel_id=1, source_target_pairs={{0,1},{1,0},{2,3},{3,2},{4,5},{5,4},{6,7},{7,6},{8,9},{9,8},{10,11... | collective-permute-start | bytes 786440 | tf_op jit(solution)/shard_map/ppermute | solution.py:343
  72.9 4.7 %collective-permute-start.2 = (bf16[2,64,128]{2,1,0:T(8,128)(2,1)S(1)}, bf16[2,64,128]{2,1,0:T(8,128)(2,1)S(1)}, u32[]{:S(2)}, u32[]{:S(2)}) collective-permute-start(bf16[2,64,128]{2,1,0:T(8,128)(2,1)S(1)} %get-tuple-element.24), channel_id=1, source_target_pairs={{0,2},{2,0},{1,3},{3,1},{4,6},{6,4},{5,7},{7,5},{8,10},{10,8},{9,1... | collective-permute-start | bytes 98312 | tf_op jit(solution)/shard_map/ppermute | solution.py:350
  75.9 2.8 %collective-permute-start.3 = (bf16[2,64,128]{2,1,0:T(8,128)(2,1)S(1)}, bf16[2,64,128]{2,1,0:T(8,128)(2,1)S(1)}, u32[]{:S(2)}, u32[]{:S(2)}) collective-permute-start(bf16[2,64,128]{2,1,0:T(8,128)(2,1)S(1)} %get-tuple-element.25), channel_id=1, source_target_pairs={{0,1},{1,0},{2,3},{3,2},{4,5},{5,4},{6,7},{7,6},{8,9},{9,8},{10,11... | collective-permute-start | bytes 98312 | tf_op jit(solution)/shard_map/ppermute | solution.py:348
  76.2 3.7 %collective-permute-start.4 = (bf16[2,64,128]{2,1,0:T(8,128)(2,1)S(1)}, bf16[2,64,128]{2,1,0:T(8,128)(2,1)S(1)}, u32[]{:S(2)}, u32[]{:S(2)}) collective-permute-start(bf16[2,64,128]{2,1,0:T(8,128)(2,1)S(1)} %get-tuple-element.26), channel_id=1, source_target_pairs={{0,3},{1,2},{2,1},{3,0},{4,7},{5,6},{6,5},{7,4},{8,11},{9,10},{10,... | collective-permute-start | bytes 98312 | tf_op jit(solution)/shard_map/ppermute | solution.py:349

commit v3 on v2

--- a/solution.py
+++ b/solution.py
@@ -155,8 +155,11 @@
     half = matrices.shape[0] // 2
     width = moved.shape[1]
     spread_rows(moved, wide, slots_by)
-    for start in range(0, chooser.shape[0] // occupied, KS_A_BLOCK):
-        order_block(start, chooser, slots_by, matrices, mine, width, occupied)
+    summed_occ = chooser.shape[0] // occupied
+    order_block(0, chooser, slots_by, matrices, mine, width, occupied)
+    for start in range(0, summed_occ, KS_A_BLOCK):
+        if start + KS_A_BLOCK < summed_occ:
+            order_block(start + KS_A_BLOCK, chooser, slots_by, matrices, mine, width, occupied)
         lanes = slice(start * width, (start + KS_A_BLOCK) * width)
         for part, total in enumerate((by_real, by_imag)):
             product = jnp.dot(matrices[:, lanes], slabs[part, lanes], preferred_element_type=F32)

time: 80.8 us -> 80.9 us (level)
  no operation moved by 1% of the time
where the time goes in v3:
time: 80.9 us; the launch traced here: 80.7 us
  blocking collectives  54.9 us (68%)
  Pallas kernels  10.6 us (13%)
  starting transfers between devices  8.14 us (10%)
  waiting for transfers between devices  6.44 us (8%)
    all_to_all x1, blocking collectives, body(): lax.all_to_all(pieces, 'chip', split_axis=0, concat_axis=0, tiled=True)  37.8 us
    all_to_all x1, blocking collectives, body(): lax.all_to_all(mirror.reshape(chips, 8, -1), 'chip', split_axis=0, concat...  17.1 us
    ppermute x1, waiting for transfers between devices, body(): got = lax.ppermute(to_send, 'vir', SWAP)  4.15 us
    pallas_call x1, Pallas kernels, second_window(): pl.pallas_call(second_kernel, out_shape=jax.ShapeDtypeStruct((matrices.sh...  3.36 us
    ppermute x1, starting transfers between devices, body(): across = lax.ppermute(moved, 'core', SWAP)  3.05 us
    ppermute x1, starting transfers between devices, body(): from_core = lax.ppermute(to_core, 'core', SWAP)  2.96 us
    pallas_call x1, Pallas kernels, first_window(): pl.pallas_call(functools.partial(first_kernel, occupied=occupied), out_sh...  2.66 us
    pallas_call x1, Pallas kernels, order(): pl.pallas_call(functools.partial(order_kernel, occupied=occupied), out_sh...  1.92 us
  transfers between devices with their start and end apart: 5, of which 3 were waited for; matrix products, arithmetic and copies ran while one was open for 1% of the time, Pallas kernels for 7%

profile of v3, /device:TPU:1, one launch (start us, length us, event | category | flops | bytes accessed | tf_op | source)
XLA Modules:
  0.0 80.7 jit_solution(7578386010368624795)
XLA Ops:
  0.0 0.0 copy-start
  0.0 1.3 %regroup.1 = bf16[64,12,4,128]{3,2,1,0:T(4,128)(2,1)S(1)} custom-call(bf16[2,6,64,4,128]{4,3,2,1,0:T(4,128)(2,1)} %bitcast.14), custom_call_target="tpu_custom_call" | custom-call | tf_op jit(solution)/shard_map/regroup/pallas_call | solution.py:45
  1.3 37.8 %all_to_all.10 = bf16[64,12,4,128]{3,2,1,0:T(4,128)(2,1)S(1)} all-to-all(bf16[64,12,4,128]{3,2,1,0:T(4,128)(2,1)S(1)} %regroup.1), channel_id=1, replica_groups=mesh['chip'=64,'core'=2,'vir'=2] {'chip'}, dimensions={0} | all-to-all | bytes 1572864 | tf_op jit(solution)/shard_map/all_to_all | solution.py:333
  39.1 3.0 %collective-permute-start = (bf16[3072,128]{1,0:T(8,128)(2,1)S(1)}, bf16[3072,128]{1,0:T(8,128)(2,1)S(1)}, u32[]{:S(2)}, u32[]{:S(2)}) collective-permute-start(bf16[3072,128]{1,0:T(8,128)(2,1)S(1)} %bitcast.8), channel_id=1, source_target_pairs={{0,2},{2,0},{1,3},{3,1},{4,6},{6,4},{5,7},{7,5},{8,10},{10,8},{9,1... | collective-permute-start | bytes 2359304 | tf_op jit(solution)/shard_map/ppermute | solution.py:337
  42.2 0.0 copy-done
  42.2 0.2 reshape.86
  42.3 0.1 reshape.92.tables
  42.5 1.9 %order.1 = (bf16[256,3072]{1,0:T(8,128)(2,1)S(1)}, bf16[2,3072,256]{2,1,0:T(8,128)(2,1)S(1)}, bf16[768,384]{1,0:T(8,128)(2,1)S(1)}) custom-call(s32[1]{0:T(128)} %bitcast.place, bf16[3072,128]{1,0:T(8,128)(2,1)S(1)} %bitcast.9, s32[2,1,384]{2,1,0:T(1,128)S(1)} %reshape.92.tables, bf16[2,4,3072,256]{3,2,1,0:T(8,128)(2,1)} %bitcast.12), custom_call_target="tpu_custom_call" | custom-call | flops 603979776 | bytes 6291456 | tf_op jit(solution)/shard_map/order/pallas_call | solution.py:121
  44.4 0.0 copy-start.1
  44.4 0.0 collective-permute-done.moved
  44.4 2.7 %first_window.1 = (bf16[256,3072]{1,0:T(8,128)(2,1)S(1)}, f32[256,256]{1,0:T(8,128)S(1)}) custom-call(bf16[256,3072]{1,0:T(8,128)(2,1)S(1)} %get-tuple-element.16.mine, bf16[3072,128]{1,0:T(8,128)(2,1)S(1)} %collective-permute-done.moved, bf16[768,384]{1,0:T(8,128)(2,1)S(1)} %get-tuple-element.17.chooser, bf16[2,3072,256]{2,1,0:T(8,128)(2,1)S(1)} %get-tuple-element.18.slabs), custom_call_target="tpu_custom_call" | custom-call | flops 805306368 | bytes 3145728 | tf_op jit(solution)/shard_map/first_window/pallas_call | solution.py:176
  47.1 0.4 collective-permute-start.1
  47.5 0.0 copy-done.1
  47.5 0.1 compare_convert_fusion
  47.6 3.4 %second_window.1.kept = f32[256,256]{1,0:T(8,128)S(1)} custom-call(s32[1]{0:T(128)} %bitcast.place, bf16[256,3072]{1,0:T(8,128)(2,1)S(1)} %get-tuple-element.19.matrices, bf16[2,4,3072,256]{3,2,1,0:T(8,128)(2,1)} %bitcast.13), custom_call_target="tpu_custom_call" | custom-call | flops 805306368 | bytes 3145728 | tf_op jit(solution)/shard_map/second_window/pallas_call | solution.py:205
  51.0 4.1 %collective-permute-done.1.got = f32[256,256]{1,0:T(8,128)S(1)} collective-permute-done((f32[256,256]{1,0:T(8,128)S(1)}, f32[256,256]{1,0:T(8,128)S(1)}, u32[]{:S(2)}, u32[]{:S(2)}) %collective-permute-start.1) | collective-permute-done | bytes 262176 | tf_op jit(solution)/shard_map/ppermute | solution.py:346
  55.1 0.6 combine.1
  55.7 17.1 %all_to_all.11 = f32[64,8,128]{2,1,0:T(8,128)S(1)} all-to-all(f32[64,8,128]{2,1,0:T(8,128)S(1)} %bitcast.11), channel_id=1, replica_groups=mesh['chip'=64,'core'=2,'vir'=2] {'chip'}, dimensions={0} | all-to-all | bytes 524288 | tf_op jit(solution)/shard_map/all_to_all | solution.py:349
  72.8 0.1 subtract.1
  73.0 3.0 %collective-permute-start.2 = (bf16[2,64,128]{2,1,0:T(8,128)(2,1)S(1)}, bf16[2,64,128]{2,1,0:T(8,128)(2,1)S(1)}, u32[]{:S(2)}, u32[]{:S(2)}) collective-permute-start(bf16[2,64,128]{2,1,0:T(8,128)(2,1)S(1)} %get-tuple-element.24), channel_id=1, source_target_pairs={{0,2},{2,0},{1,3},{3,1},{4,6},{6,4},{5,7},{7,5},{8,10},{10,8},{9,1... | collective-permute-start | bytes 98312 | tf_op jit(solution)/shard_map/ppermute | solution.py:353
  76.0 0.3 collective-permute-start.3
  76.3 1.4 %collective-permute-start.4 = (bf16[2,64,128]{2,1,0:T(8,128)(2,1)S(1)}, bf16[2,64,128]{2,1,0:T(8,128)(2,1)S(1)}, u32[]{:S(2)}, u32[]{:S(2)}) collective-permute-start(bf16[2,64,128]{2,1,0:T(8,128)(2,1)S(1)} %get-tuple-element.26), channel_id=1, source_target_pairs={{0,3},{1,2},{2,1},{3,0},{4,7},{5,6},{6,5},{7,4},{8,11},{9,10},{10,... | collective-permute-start | bytes 98312 | tf_op jit(solution)/shard_map/ppermute | solution.py:352
  77.7 0.0 collective-permute-done.2.from_core
  77.7 1.0 %collective-permute-done.3.from_vir = bf16[2,64,128]{2,1,0:T(8,128)(2,1)S(1)} collective-permute-done((bf16[2,64,128]{2,1,0:T(8,128)(2,1)S(1)}, bf16[2,64,128]{2,1,0:T(8,128)(2,1)S(1)}, u32[]{:S(2)}, u32[]{:S(2)}) %collective-permute-start.3) | collective-permute-done | bytes 32800 | tf_op jit(solution)/shard_map/ppermute | solution.py:351
  78.7 1.2 %collective-permute-done.4.from_both = bf16[2,64,128]{2,1,0:T(8,128)(2,1)S(1)} collective-permute-done((bf16[2,64,128]{2,1,0:T(8,128)(2,1)S(1)}, bf16[2,64,128]{2,1,0:T(8,128)(2,1)S(1)}, u32[]{:S(2)}, u32[]{:S(2)}) %collective-permute-start.4) | collective-permute-done | bytes 32800 | tf_op jit(solution)/shard_map/ppermute | solution.py:352
  80.0 0.7 finish.1
  (2 shorter events, 0.0 us)
Async XLA Ops:
  0.0 42.2 %copy-start = (s32[768]{0:T(1024)S(1)}, s32[768]{0:T(1024)}, u32[]{:S(2)}) copy-start(s32[768]{0:T(1024)} %param.6) | copy-start | bytes 9220
  39.1 5.3 %collective-permute-start = (bf16[3072,128]{1,0:T(8,128)(2,1)S(1)}, bf16[3072,128]{1,0:T(8,128)(2,1)S(1)}, u32[]{:S(2)}, u32[]{:S(2)}) collective-permute-start(bf16[3072,128]{1,0:T(8,128)(2,1)S(1)} %bitcast.8), channel_id=1, source_target_pairs={{0,2},{2,0},{1,3},{3,1},{4,6},{6,4},{5,7},{7,5},{8,10},{10,8},{9,1... | collective-permute-start | bytes 2359304 | tf_op jit(solution)/shard_map/ppermute | solution.py:337
  44.4 3.1 %copy-start.1 = (s32[256]{0:T(256)S(1)}, s32[256]{0:T(256)}, u32[]{:S(2)}) copy-start(s32[256]{0:T(256)} %param.7) | copy-start | bytes 3076
  47.1 8.0 %collective-permute-start.1 = (f32[256,256]{1,0:T(8,128)S(1)}, f32[256,256]{1,0:T(8,128)S(1)}, u32[]{:S(2)}, u32[]{:S(2)}) collective-permute-start(f32[256,256]{1,0:T(8,128)S(1)} %get-tuple-element.20), channel_id=1, source_target_pairs={{0,1},{1,0},{2,3},{3,2},{4,5},{5,4},{6,7},{7,6},{8,9},{9,8},{10,11... | collective-permute-start | bytes 786440 | tf_op jit(solution)/shard_map/ppermute | solution.py:346
  73.0 4.7 %collective-permute-start.2 = (bf16[2,64,128]{2,1,0:T(8,128)(2,1)S(1)}, bf16[2,64,128]{2,1,0:T(8,128)(2,1)S(1)}, u32[]{:S(2)}, u32[]{:S(2)}) collective-permute-start(bf16[2,64,128]{2,1,0:T(8,128)(2,1)S(1)} %get-tuple-element.24), channel_id=1, source_target_pairs={{0,2},{2,0},{1,3},{3,1},{4,6},{6,4},{5,7},{7,5},{8,10},{10,8},{9,1... | collective-permute-start | bytes 98312 | tf_op jit(solution)/shard_map/ppermute | solution.py:353
  76.0 2.8 %collective-permute-start.3 = (bf16[2,64,128]{2,1,0:T(8,128)(2,1)S(1)}, bf16[2,64,128]{2,1,0:T(8,128)(2,1)S(1)}, u32[]{:S(2)}, u32[]{:S(2)}) collective-permute-start(bf16[2,64,128]{2,1,0:T(8,128)(2,1)S(1)} %get-tuple-element.25), channel_id=1, source_target_pairs={{0,1},{1,0},{2,3},{3,2},{4,5},{5,4},{6,7},{7,6},{8,9},{9,8},{10,11... | collective-permute-start | bytes 98312 | tf_op jit(solution)/shard_map/ppermute | solution.py:351
  76.3 3.7 %collective-permute-start.4 = (bf16[2,64,128]{2,1,0:T(8,128)(2,1)S(1)}, bf16[2,64,128]{2,1,0:T(8,128)(2,1)S(1)}, u32[]{:S(2)}, u32[]{:S(2)}) collective-permute-start(bf16[2,64,128]{2,1,0:T(8,128)(2,1)S(1)} %get-tuple-element.26), channel_id=1, source_target_pairs={{0,3},{1,2},{2,1},{3,0},{4,7},{5,6},{6,5},{7,4},{8,11},{9,10},{10,... | collective-permute-start | bytes 98312 | tf_op jit(solution)/shard_map/ppermute | solution.py:352

commit v4 on v3

--- a/solution.py
+++ b/solution.py
@@ -151,7 +151,17 @@
     out[half:] = by_real[half:] + by_imag[:half]
 
 
-def first_kernel(mine, moved, chooser, slabs, matrices, out, wide, slots_by, by_real, by_imag, *, occupied):
+def first_kernel(
+    place, mine, moved, chooser, slabs, integrals, matrices, out, early, wide, slots_by, by_real, by_imag, own_slabs, sems, *, occupied
+):
+    copies = slab_copies(place, 1, integrals, own_slabs, sems)
+    core = (place[0] // 2) % 2
+
+    @pl.when(core == 1)
+    def _():
+        for copy in copies:
+            copy.start()
+
     half = matrices.shape[0] // 2
     width = moved.shape[1]
     spread_rows(moved, wide, slots_by)
@@ -167,8 +177,12 @@
     out[:half] = by_real[:half] - by_imag[half:]
     out[half:] = by_real[half:] + by_imag[:half]
 
-
-def first_window(mine, moved, chooser, slabs, occupied):
+    @pl.when(core == 1)
+    def _():
+        product_into(early, matrices, own_slabs, copies)
+
+
+def first_window(place, mine, moved, chooser, slabs, integrals, occupied):
     width = moved.shape[1]
     slots = chooser.shape[1]
     rows = moved.shape[0] // slots
@@ -178,40 +192,51 @@
         out_shape=(
             jax.ShapeDtypeStruct(mine.shape, BF16),
             jax.ShapeDtypeStruct((mine.shape[0], full_virtual), F32),
+            jax.ShapeDtypeStruct((mine.shape[0], full_virtual), F32),
         ),
-        in_specs=[IN_VMEM] * 4,
-        out_specs=(IN_VMEM,) * 2,
+        in_specs=[IN_SMEM] + [IN_VMEM] * 4 + [IN_HBM],
+        out_specs=(IN_VMEM,) * 3,
         scratch_shapes=[
             pltpu.VMEM(((slots + 1) * rows, width), F32),
             pltpu.VMEM((slots, rows * width), BF16),
             pltpu.VMEM((mine.shape[0], full_virtual), F32),
             pltpu.VMEM((mine.shape[0], full_virtual), F32),
+            pltpu.VMEM(slabs.shape, BF16),
+            pltpu.SemaphoreType.DMA((2,)),
         ],
         compiler_params=PARAMS,
         cost_estimate=cost(4 * mine.size * full_virtual, 4 * mine.size),
         name="first_window",
-    )(mine, moved, chooser, pltpu.with_memory_space_constraint(slabs, pltpu.VMEM))
-
-
-def second_kernel(place, matrices, integrals, out, slabs, sems):
+    )(place, mine, moved, chooser, pltpu.with_memory_space_constraint(slabs, pltpu.VMEM), integrals)
+
+
+def second_kernel(place, matrices, early, integrals, out, slabs, sems):
     copies = slab_copies(place, 1, integrals, slabs, sems)
-    for copy in copies:
-        copy.start()
-    product_into(out, matrices, slabs, copies)
-
-
-def second_window(place, matrices, integrals):
+    core = (place[0] // 2) % 2
+
+    @pl.when(core == 0)
+    def _():
+        for copy in copies:
+            copy.start()
+        product_into(out, matrices, slabs, copies)
+
+    @pl.when(core == 1)
+    def _():
+        out[...] = early[...]
+
+
+def second_window(place, matrices, early, integrals):
     depth, full_virtual = integrals.shape[2:]
     return pl.pallas_call(
         second_kernel,
         out_shape=jax.ShapeDtypeStruct((matrices.shape[0], full_virtual), F32),
-        in_specs=[IN_SMEM, IN_VMEM, IN_HBM],
+        in_specs=[IN_SMEM, IN_VMEM, IN_VMEM, IN_HBM],
         out_specs=IN_VMEM,
         scratch_shapes=[pltpu.VMEM((2, depth, full_virtual), BF16), pltpu.SemaphoreType.DMA((2,))],
         compiler_params=PARAMS,
         cost_estimate=cost(4 * matrices.size * full_virtual, 4 * matrices.size),
         name="second_window",
-    )(place, matrices, integrals)
+    )(place, matrices, early, integrals)
 
 
 def chosen(values, order_by):
@@ -342,9 +367,9 @@
     chip_order = (kramers[None, :] == places % chips * here + places // chips).astype(BF16)
 
     mine, slabs, chooser = order(place, moved, tables, flat, occupied)
-    matrices, to_send = first_window(mine, across, chooser, slabs, occupied)
+    matrices, to_send, early = first_window(place, mine, across, chooser, slabs, flat, occupied)
     got = lax.ppermute(to_send, "vir", SWAP)
-    kept = second_window(place, matrices, flat)
+    kept = second_window(place, matrices, early, flat)
     own, mirror = combine(kept, got, natural_order, chip_order, chips)
     mirror = lax.all_to_all(mirror.reshape(chips, 8, -1), "chip", split_axis=0, concat_axis=0, tiled=True)
     keep, to_core, to_vir, to_both = subtract(place, own, mirror.reshape(chips * 8, -1))

time: 80.9 us -> 81.2 us (level)
  starting transfers between devices: 8.14 us -> 5.71 us
  blocking collectives: 54.9 us -> 57.1 us
  waiting for transfers between devices: 6.44 us -> 8.38 us
  Pallas kernels: 10.6 us -> 9.3 us
    pallas_call x1, Pallas kernels: 3.36 us -> 0.06 us  [second_window(): pl.pallas_call(second_kernel, out_shape=jax.ShapeDtypeStruct((matrices.sh...]
    ppermute x1, starting transfers between devices: 2.96 us -> 0.48 us  [body(): from_core = lax.ppermute(to_core, 'core', SWAP)]
    all_to_all x1, blocking collectives: 17.1 us -> 19.3 us  [body(): lax.all_to_all(mirror.reshape(chips, 8, -1), 'chip', split_axis=0, concat...]
    pallas_call x1, Pallas kernels: 2.66 us -> 4.63 us  [first_window(): pl.pallas_call(functools.partial(first_kernel, occupied=occupied), out_sh...]
    ppermute x1, waiting for transfers between devices: 4.15 us -> 6.08 us  [body(): got = lax.ppermute(to_send, 'vir', SWAP)]
  transfers between devices with their start and end apart: 5 -> 5, of which waited for: 3 -> 3; matrix products, arithmetic and copies ran while one was open for 1% -> 1% of each run, Pallas kernels for 7% -> 2%
where the time goes in v4:
time: 81.2 us; the launch traced here: 81 us
  blocking collectives  57.1 us (70%)
  Pallas kernels  9.3 us (11%)
  waiting for transfers between devices  8.38 us (10%)
  starting transfers between devices  5.71 us (7%)
    all_to_all x1, blocking collectives, body(): lax.all_to_all(pieces, 'chip', split_axis=0, concat_axis=0, tiled=True)  37.8 us
    all_to_all x1, blocking collectives, body(): lax.all_to_all(mirror.reshape(chips, 8, -1), 'chip', split_axis=0, concat...  19.3 us
    ppermute x1, waiting for transfers between devices, body(): got = lax.ppermute(to_send, 'vir', SWAP)  6.08 us
    pallas_call x1, Pallas kernels, first_window(): pl.pallas_call(functools.partial(first_kernel, occupied=occupied), out_sh...  4.63 us
    ppermute x1, starting transfers between devices, body(): across = lax.ppermute(moved, 'core', SWAP)  3.05 us
    pallas_call x1, Pallas kernels, order(): pl.pallas_call(functools.partial(order_kernel, occupied=occupied), out_sh...  1.92 us
  transfers between devices with their start and end apart: 5, of which 3 were waited for; matrix products, arithmetic and copies ran while one was open for 1% of the time, Pallas kernels for 2%

profile of v4, /device:TPU:1, one launch (start us, length us, event | category | flops | bytes accessed | tf_op | source)
XLA Modules:
  0.0 81.0 jit_solution(13984094205284418576)
XLA Ops:
  0.0 0.0 copy-start
  0.0 1.3 %regroup.1 = bf16[64,12,4,128]{3,2,1,0:T(4,128)(2,1)S(1)} custom-call(bf16[2,6,64,4,128]{4,3,2,1,0:T(4,128)(2,1)} %bitcast.15), custom_call_target="tpu_custom_call" | custom-call | tf_op jit(solution)/shard_map/regroup/pallas_call | solution.py:45
  1.3 37.8 %all_to_all.10 = bf16[64,12,4,128]{3,2,1,0:T(4,128)(2,1)S(1)} all-to-all(bf16[64,12,4,128]{3,2,1,0:T(4,128)(2,1)S(1)} %regroup.1), channel_id=1, replica_groups=mesh['chip'=64,'core'=2,'vir'=2] {'chip'}, dimensions={0} | all-to-all | bytes 1572864 | tf_op jit(solution)/shard_map/all_to_all | solution.py:358
  39.1 3.0 %collective-permute-start = (bf16[3072,128]{1,0:T(8,128)(2,1)S(1)}, bf16[3072,128]{1,0:T(8,128)(2,1)S(1)}, u32[]{:S(2)}, u32[]{:S(2)}) collective-permute-start(bf16[3072,128]{1,0:T(8,128)(2,1)S(1)} %bitcast.8), channel_id=1, source_target_pairs={{0,2},{2,0},{1,3},{3,1},{4,6},{6,4},{5,7},{7,5},{8,10},{10,8},{9,1... | collective-permute-start | bytes 2359304 | tf_op jit(solution)/shard_map/ppermute | solution.py:362
  42.2 0.0 copy-done
  42.2 0.2 reshape.86
  42.3 0.1 reshape.92.tables
  42.5 1.9 %order.1 = (bf16[256,3072]{1,0:T(8,128)(2,1)S(1)}, bf16[2,3072,256]{2,1,0:T(8,128)(2,1)S(1)}, bf16[768,384]{1,0:T(8,128)(2,1)S(1)}) custom-call(s32[1]{0:T(128)} %bitcast.place, bf16[3072,128]{1,0:T(8,128)(2,1)S(1)} %bitcast.9, s32[2,1,384]{2,1,0:T(1,128)S(1)} %reshape.92.tables, bf16[2,4,3072,256]{3,2,1,0:T(8,128)(2,1)} %bitcast.12), custom_call_target="tpu_custom_call" | custom-call | flops 603979776 | bytes 6291456 | tf_op jit(solution)/shard_map/order/pallas_call | solution.py:121
  44.4 0.0 collective-permute-done.moved
  44.4 0.0 copy-start.1
  44.4 4.6 %first_window.1 = (bf16[256,3072]{1,0:T(8,128)(2,1)S(1)}, f32[256,256]{1,0:T(8,128)S(1)}, f32[256,256]{1,0:T(8,128)S(1)}) custom-call(s32[1]{0:T(128)} %bitcast.place, bf16[256,3072]{1,0:T(8,128)(2,1)S(1)} %get-tuple-element.17.mine, bf16[3072,128]{1,0:T(8,128)(2,1)S(1)} %collective-permute-done.moved, bf16[768,384]{1,0:T(8,128)(2,1)S(1)} %get-tuple-element.18.chooser, ...), custom_call_target="tpu_custom_call" | custom-call | flops 805306368 | bytes 3145728 | tf_op jit(solution)/shard_map/first_window/pallas_call | solution.py:190
  49.1 0.4 collective-permute-start.1
  49.5 0.0 copy-done.1
  49.5 0.1 compare_convert_fusion
  49.6 0.1 second_window.1.kept
  49.7 6.1 %collective-permute-done.1.got = f32[256,256]{1,0:T(8,128)S(1)} collective-permute-done((f32[256,256]{1,0:T(8,128)S(1)}, f32[256,256]{1,0:T(8,128)S(1)}, u32[]{:S(2)}, u32[]{:S(2)}) %collective-permute-start.1) | collective-permute-done | bytes 262176 | tf_op jit(solution)/shard_map/ppermute | solution.py:371
  55.7 0.6 combine.1
  56.3 19.3 %all_to_all.11 = f32[64,8,128]{2,1,0:T(8,128)S(1)} all-to-all(f32[64,8,128]{2,1,0:T(8,128)S(1)} %bitcast.11), channel_id=1, replica_groups=mesh['chip'=64,'core'=2,'vir'=2] {'chip'}, dimensions={0} | all-to-all | bytes 524288 | tf_op jit(solution)/shard_map/all_to_all | solution.py:374
  75.6 0.1 subtract.1
  75.8 0.5 collective-permute-start.2
  76.3 0.3 collective-permute-start.3
  76.6 1.5 %collective-permute-start.4 = (bf16[2,64,128]{2,1,0:T(8,128)(2,1)S(1)}, bf16[2,64,128]{2,1,0:T(8,128)(2,1)S(1)}, u32[]{:S(2)}, u32[]{:S(2)}) collective-permute-start(bf16[2,64,128]{2,1,0:T(8,128)(2,1)S(1)} %get-tuple-element.28), channel_id=1, source_target_pairs={{0,3},{1,2},{2,1},{3,0},{4,7},{5,6},{6,5},{7,4},{8,11},{9,10},{10,... | collective-permute-start | bytes 98312 | tf_op jit(solution)/shard_map/ppermute | solution.py:377
  78.1 0.0 collective-permute-done.2.from_core
  78.1 1.0 %collective-permute-done.3.from_vir = bf16[2,64,128]{2,1,0:T(8,128)(2,1)S(1)} collective-permute-done((bf16[2,64,128]{2,1,0:T(8,128)(2,1)S(1)}, bf16[2,64,128]{2,1,0:T(8,128)(2,1)S(1)}, u32[]{:S(2)}, u32[]{:S(2)}) %collective-permute-start.3) | collective-permute-done | bytes 32800 | tf_op jit(solution)/shard_map/ppermute | solution.py:376
  79.0 1.3 %collective-permute-done.4.from_both = bf16[2,64,128]{2,1,0:T(8,128)(2,1)S(1)} collective-permute-done((bf16[2,64,128]{2,1,0:T(8,128)(2,1)S(1)}, bf16[2,64,128]{2,1,0:T(8,128)(2,1)S(1)}, u32[]{:S(2)}, u32[]{:S(2)}) %collective-permute-start.4) | collective-permute-done | bytes 32800 | tf_op jit(solution)/shard_map/ppermute | solution.py:377
  80.3 0.7 finish.1
  (2 shorter events, 0.0 us)
Async XLA Ops:
  0.0 42.2 %copy-start = (s32[768]{0:T(1024)S(1)}, s32[768]{0:T(1024)}, u32[]{:S(2)}) copy-start(s32[768]{0:T(1024)} %param.6) | copy-start | bytes 9220
  39.1 5.3 %collective-permute-start = (bf16[3072,128]{1,0:T(8,128)(2,1)S(1)}, bf16[3072,128]{1,0:T(8,128)(2,1)S(1)}, u32[]{:S(2)}, u32[]{:S(2)}) collective-permute-start(bf16[3072,128]{1,0:T(8,128)(2,1)S(1)} %bitcast.8), channel_id=1, source_target_pairs={{0,2},{2,0},{1,3},{3,1},{4,6},{6,4},{5,7},{7,5},{8,10},{10,8},{9,1... | collective-permute-start | bytes 2359304 | tf_op jit(solution)/shard_map/ppermute | solution.py:362
  44.4 5.0 %copy-start.1 = (s32[256]{0:T(256)S(1)}, s32[256]{0:T(256)}, u32[]{:S(2)}) copy-start(s32[256]{0:T(256)} %param.7) | copy-start | bytes 3076
  49.1 6.7 %collective-permute-start.1 = (f32[256,256]{1,0:T(8,128)S(1)}, f32[256,256]{1,0:T(8,128)S(1)}, u32[]{:S(2)}, u32[]{:S(2)}) collective-permute-start(f32[256,256]{1,0:T(8,128)S(1)} %get-tuple-element.22), channel_id=1, source_target_pairs={{0,1},{1,0},{2,3},{3,2},{4,5},{5,4},{6,7},{7,6},{8,9},{9,8},{10,11... | collective-permute-start | bytes 786440 | tf_op jit(solution)/shard_map/ppermute | solution.py:371
  75.8 2.3 %collective-permute-start.2 = (bf16[2,64,128]{2,1,0:T(8,128)(2,1)S(1)}, bf16[2,64,128]{2,1,0:T(8,128)(2,1)S(1)}, u32[]{:S(2)}, u32[]{:S(2)}) collective-permute-start(bf16[2,64,128]{2,1,0:T(8,128)(2,1)S(1)} %get-tuple-element.26), channel_id=1, source_target_pairs={{0,2},{2,0},{1,3},{3,1},{4,6},{6,4},{5,7},{7,5},{8,10},{10,8},{9,1... | collective-permute-start | bytes 98312 | tf_op jit(solution)/shard_map/ppermute | solution.py:378
  76.3 2.8 %collective-permute-start.3 = (bf16[2,64,128]{2,1,0:T(8,128)(2,1)S(1)}, bf16[2,64,128]{2,1,0:T(8,128)(2,1)S(1)}, u32[]{:S(2)}, u32[]{:S(2)}) collective-permute-start(bf16[2,64,128]{2,1,0:T(8,128)(2,1)S(1)} %get-tuple-element.27), channel_id=1, source_target_pairs={{0,1},{1,0},{2,3},{3,2},{4,5},{5,4},{6,7},{7,6},{8,9},{9,8},{10,11... | collective-permute-start | bytes 98312 | tf_op jit(solution)/shard_map/ppermute | solution.py:376
  76.6 3.8 %collective-permute-start.4 = (bf16[2,64,128]{2,1,0:T(8,128)(2,1)S(1)}, bf16[2,64,128]{2,1,0:T(8,128)(2,1)S(1)}, u32[]{:S(2)}, u32[]{:S(2)}) collective-permute-start(bf16[2,64,128]{2,1,0:T(8,128)(2,1)S(1)} %get-tuple-element.28), channel_id=1, source_target_pairs={{0,3},{1,2},{2,1},{3,0},{4,7},{5,6},{6,5},{7,4},{8,11},{9,10},{10,... | collective-permute-start | bytes 98312 | tf_op jit(solution)/shard_map/ppermute | solution.py:377

commit v5 on v3

--- a/solution.py
+++ b/solution.py
@@ -13,7 +13,7 @@
 NT = (((1,), (1,)), ((), ()))
 VMEM_LIMIT = 24 * 1024 * 1024
 IN_VMEM = pl.BlockSpec(memory_space=pltpu.VMEM)
-KS_A_BLOCK = 8
+KS_A_BLOCK = 6
 IN_HBM = pl.BlockSpec(memory_space=pl.ANY)
 IN_SMEM = pl.BlockSpec(memory_space=pltpu.SMEM)
 PARAMS = pltpu.CompilerParams(vmem_limit_bytes=VMEM_LIMIT)

time: 80.9 us -> 80.8 us (level)
  no operation moved by 1% of the time
where the time goes in v5:
time: 80.8 us; the launch traced here: 80.6 us
  blocking collectives  54.9 us (68%)
  Pallas kernels  10.6 us (13%)
  starting transfers between devices  8.17 us (10%)
  waiting for transfers between devices  6.45 us (8%)
    all_to_all x1, blocking collectives, body(): lax.all_to_all(pieces, 'chip', split_axis=0, concat_axis=0, tiled=True)  37.8 us
    all_to_all x1, blocking collectives, body(): lax.all_to_all(mirror.reshape(chips, 8, -1), 'chip', split_axis=0, concat...  17.1 us
    ppermute x1, waiting for transfers between devices, body(): got = lax.ppermute(to_send, 'vir', SWAP)  4.15 us
    pallas_call x1, Pallas kernels, second_window(): pl.pallas_call(second_kernel, out_shape=jax.ShapeDtypeStruct((matrices.sh...  3.36 us
    ppermute x1, starting transfers between devices, body(): across = lax.ppermute(moved, 'core', SWAP)  3.05 us
    ppermute x1, starting transfers between devices, body(): from_core = lax.ppermute(to_core, 'core', SWAP)  2.99 us
    pallas_call x1, Pallas kernels, first_window(): pl.pallas_call(functools.partial(first_kernel, occupied=occupied), out_sh...  2.6 us
    pallas_call x1, Pallas kernels, order(): pl.pallas_call(functools.partial(order_kernel, occupied=occupied), out_sh...  1.92 us
  transfers between devices with their start and end apart: 5, of which 3 were waited for; matrix products, arithmetic and copies ran while one was open for 1% of the time, Pallas kernels for 7%

profile of v5, /device:TPU:1, one launch (start us, length us, event | category | flops | bytes accessed | tf_op | source)
XLA Modules:
  0.0 80.6 jit_solution(14252766656035246361)
XLA Ops:
  0.0 0.0 copy-start
  0.0 1.3 %regroup.1 = bf16[64,12,4,128]{3,2,1,0:T(4,128)(2,1)S(1)} custom-call(bf16[2,6,64,4,128]{4,3,2,1,0:T(4,128)(2,1)} %bitcast.14), custom_call_target="tpu_custom_call" | custom-call | tf_op jit(solution)/shard_map/regroup/pallas_call | solution.py:45
  1.3 37.8 %all_to_all.10 = bf16[64,12,4,128]{3,2,1,0:T(4,128)(2,1)S(1)} all-to-all(bf16[64,12,4,128]{3,2,1,0:T(4,128)(2,1)S(1)} %regroup.1), channel_id=1, replica_groups=mesh['chip'=64,'core'=2,'vir'=2] {'chip'}, dimensions={0} | all-to-all | bytes 1572864 | tf_op jit(solution)/shard_map/all_to_all | solution.py:333
  39.1 3.0 %collective-permute-start = (bf16[3072,128]{1,0:T(8,128)(2,1)S(1)}, bf16[3072,128]{1,0:T(8,128)(2,1)S(1)}, u32[]{:S(2)}, u32[]{:S(2)}) collective-permute-start(bf16[3072,128]{1,0:T(8,128)(2,1)S(1)} %bitcast.8), channel_id=1, source_target_pairs={{0,2},{2,0},{1,3},{3,1},{4,6},{6,4},{5,7},{7,5},{8,10},{10,8},{9,1... | collective-permute-start | bytes 2359304 | tf_op jit(solution)/shard_map/ppermute | solution.py:337
  42.2 0.0 copy-done
  42.2 0.2 reshape.86
  42.3 0.1 reshape.92.tables
  42.5 1.9 %order.1 = (bf16[256,3072]{1,0:T(8,128)(2,1)S(1)}, bf16[2,3072,256]{2,1,0:T(8,128)(2,1)S(1)}, bf16[768,384]{1,0:T(8,128)(2,1)S(1)}) custom-call(s32[1]{0:T(128)} %bitcast.place, bf16[3072,128]{1,0:T(8,128)(2,1)S(1)} %bitcast.9, s32[2,1,384]{2,1,0:T(1,128)S(1)} %reshape.92.tables, bf16[2,4,3072,256]{3,2,1,0:T(8,128)(2,1)} %bitcast.12), custom_call_target="tpu_custom_call" | custom-call | flops 603979776 | bytes 6291456 | tf_op jit(solution)/shard_map/order/pallas_call | solution.py:121
  44.4 0.0 copy-start.1
  44.4 0.0 collective-permute-done.moved
  44.4 2.6 %first_window.1 = (bf16[256,3072]{1,0:T(8,128)(2,1)S(1)}, f32[256,256]{1,0:T(8,128)S(1)}) custom-call(bf16[256,3072]{1,0:T(8,128)(2,1)S(1)} %get-tuple-element.16.mine, bf16[3072,128]{1,0:T(8,128)(2,1)S(1)} %collective-permute-done.moved, bf16[768,384]{1,0:T(8,128)(2,1)S(1)} %get-tuple-element.17.chooser, bf16[2,3072,256]{2,1,0:T(8,128)(2,1)S(1)} %get-tuple-element.18.slabs), custom_call_target="tpu_custom_call" | custom-call | flops 805306368 | bytes 3145728 | tf_op jit(solution)/shard_map/first_window/pallas_call | solution.py:176
  47.1 0.4 collective-permute-start.1
  47.5 0.0 copy-done.1
  47.5 0.1 compare_convert_fusion
  47.6 3.4 %second_window.1.kept = f32[256,256]{1,0:T(8,128)S(1)} custom-call(s32[1]{0:T(128)} %bitcast.place, bf16[256,3072]{1,0:T(8,128)(2,1)S(1)} %get-tuple-element.19.matrices, bf16[2,4,3072,256]{3,2,1,0:T(8,128)(2,1)} %bitcast.13), custom_call_target="tpu_custom_call" | custom-call | flops 805306368 | bytes 3145728 | tf_op jit(solution)/shard_map/second_window/pallas_call | solution.py:205
  50.9 4.1 %collective-permute-done.1.got = f32[256,256]{1,0:T(8,128)S(1)} collective-permute-done((f32[256,256]{1,0:T(8,128)S(1)}, f32[256,256]{1,0:T(8,128)S(1)}, u32[]{:S(2)}, u32[]{:S(2)}) %collective-permute-start.1) | collective-permute-done | bytes 262176 | tf_op jit(solution)/shard_map/ppermute | solution.py:346
  55.1 0.6 combine.1
  55.7 17.1 %all_to_all.11 = f32[64,8,128]{2,1,0:T(8,128)S(1)} all-to-all(f32[64,8,128]{2,1,0:T(8,128)S(1)} %bitcast.11), channel_id=1, replica_groups=mesh['chip'=64,'core'=2,'vir'=2] {'chip'}, dimensions={0} | all-to-all | bytes 524288 | tf_op jit(solution)/shard_map/all_to_all | solution.py:349
  72.8 0.1 subtract.1
  72.9 3.0 %collective-permute-start.2 = (bf16[2,64,128]{2,1,0:T(8,128)(2,1)S(1)}, bf16[2,64,128]{2,1,0:T(8,128)(2,1)S(1)}, u32[]{:S(2)}, u32[]{:S(2)}) collective-permute-start(bf16[2,64,128]{2,1,0:T(8,128)(2,1)S(1)} %get-tuple-element.24), channel_id=1, source_target_pairs={{0,2},{2,0},{1,3},{3,1},{4,6},{6,4},{5,7},{7,5},{8,10},{10,8},{9,1... | collective-permute-start | bytes 98312 | tf_op jit(solution)/shard_map/ppermute | solution.py:353
  75.9 0.3 collective-permute-start.3
  76.2 1.4 %collective-permute-start.4 = (bf16[2,64,128]{2,1,0:T(8,128)(2,1)S(1)}, bf16[2,64,128]{2,1,0:T(8,128)(2,1)S(1)}, u32[]{:S(2)}, u32[]{:S(2)}) collective-permute-start(bf16[2,64,128]{2,1,0:T(8,128)(2,1)S(1)} %get-tuple-element.26), channel_id=1, source_target_pairs={{0,3},{1,2},{2,1},{3,0},{4,7},{5,6},{6,5},{7,4},{8,11},{9,10},{10,... | collective-permute-start | bytes 98312 | tf_op jit(solution)/shard_map/ppermute | solution.py:352
  77.6 0.0 collective-permute-done.2.from_core
  77.6 1.0 %collective-permute-done.3.from_vir = bf16[2,64,128]{2,1,0:T(8,128)(2,1)S(1)} collective-permute-done((bf16[2,64,128]{2,1,0:T(8,128)(2,1)S(1)}, bf16[2,64,128]{2,1,0:T(8,128)(2,1)S(1)}, u32[]{:S(2)}, u32[]{:S(2)}) %collective-permute-start.3) | collective-permute-done | bytes 32800 | tf_op jit(solution)/shard_map/ppermute | solution.py:351
  78.7 1.2 %collective-permute-done.4.from_both = bf16[2,64,128]{2,1,0:T(8,128)(2,1)S(1)} collective-permute-done((bf16[2,64,128]{2,1,0:T(8,128)(2,1)S(1)}, bf16[2,64,128]{2,1,0:T(8,128)(2,1)S(1)}, u32[]{:S(2)}, u32[]{:S(2)}) %collective-permute-start.4) | collective-permute-done | bytes 32800 | tf_op jit(solution)/shard_map/ppermute | solution.py:352
  79.9 0.7 finish.1
  (2 shorter events, 0.0 us)
Async XLA Ops:
  0.0 42.2 %copy-start = (s32[768]{0:T(1024)S(1)}, s32[768]{0:T(1024)}, u32[]{:S(2)}) copy-start(s32[768]{0:T(1024)} %param.6) | copy-start | bytes 9220
  39.1 5.3 %collective-permute-start = (bf16[3072,128]{1,0:T(8,128)(2,1)S(1)}, bf16[3072,128]{1,0:T(8,128)(2,1)S(1)}, u32[]{:S(2)}, u32[]{:S(2)}) collective-permute-start(bf16[3072,128]{1,0:T(8,128)(2,1)S(1)} %bitcast.8), channel_id=1, source_target_pairs={{0,2},{2,0},{1,3},{3,1},{4,6},{6,4},{5,7},{7,5},{8,10},{10,8},{9,1... | collective-permute-start | bytes 2359304 | tf_op jit(solution)/shard_map/ppermute | solution.py:337
  44.4 3.0 %copy-start.1 = (s32[256]{0:T(256)S(1)}, s32[256]{0:T(256)}, u32[]{:S(2)}) copy-start(s32[256]{0:T(256)} %param.7) | copy-start | bytes 3076
  47.1 8.0 %collective-permute-start.1 = (f32[256,256]{1,0:T(8,128)S(1)}, f32[256,256]{1,0:T(8,128)S(1)}, u32[]{:S(2)}, u32[]{:S(2)}) collective-permute-start(f32[256,256]{1,0:T(8,128)S(1)} %get-tuple-element.20), channel_id=1, source_target_pairs={{0,1},{1,0},{2,3},{3,2},{4,5},{5,4},{6,7},{7,6},{8,9},{9,8},{10,11... | collective-permute-start | bytes 786440 | tf_op jit(solution)/shard_map/ppermute | solution.py:346
  72.9 4.7 %collective-permute-start.2 = (bf16[2,64,128]{2,1,0:T(8,128)(2,1)S(1)}, bf16[2,64,128]{2,1,0:T(8,128)(2,1)S(1)}, u32[]{:S(2)}, u32[]{:S(2)}) collective-permute-start(bf16[2,64,128]{2,1,0:T(8,128)(2,1)S(1)} %get-tuple-element.24), channel_id=1, source_target_pairs={{0,2},{2,0},{1,3},{3,1},{4,6},{6,4},{5,7},{7,5},{8,10},{10,8},{9,1... | collective-permute-start | bytes 98312 | tf_op jit(solution)/shard_map/ppermute | solution.py:353
  75.9 2.8 %collective-permute-start.3 = (bf16[2,64,128]{2,1,0:T(8,128)(2,1)S(1)}, bf16[2,64,128]{2,1,0:T(8,128)(2,1)S(1)}, u32[]{:S(2)}, u32[]{:S(2)}) collective-permute-start(bf16[2,64,128]{2,1,0:T(8,128)(2,1)S(1)} %get-tuple-element.25), channel_id=1, source_target_pairs={{0,1},{1,0},{2,3},{3,2},{4,5},{5,4},{6,7},{7,6},{8,9},{9,8},{10,11... | collective-permute-start | bytes 98312 | tf_op jit(solution)/shard_map/ppermute | solution.py:351
  76.2 3.7 %collective-permute-start.4 = (bf16[2,64,128]{2,1,0:T(8,128)(2,1)S(1)}, bf16[2,64,128]{2,1,0:T(8,128)(2,1)S(1)}, u32[]{:S(2)}, u32[]{:S(2)}) collective-permute-start(bf16[2,64,128]{2,1,0:T(8,128)(2,1)S(1)} %get-tuple-element.26), channel_id=1, source_target_pairs={{0,3},{1,2},{2,1},{3,0},{4,7},{5,6},{6,5},{7,4},{8,11},{9,10},{10,... | collective-permute-start | bytes 98312 | tf_op jit(solution)/shard_map/ppermute | solution.py:352

commit v6 on v5

--- a/solution.py
+++ b/solution.py
@@ -99,11 +99,35 @@
         chooser[:, start : start + lanes] = (table[:, start : start + lanes] == wanted).astype(BF16)
 
 
-def order_kernel(place, moved, tables, integrals, matrices, slabs, there, here, wide, slots_by, sems, *, occupied):
+def sort_table(table, tables, select, slots_a_chip):
+    pairs = table.shape[1]
+    slots = pairs // 2
+    lanes = 128
+    column = lax.broadcasted_iota(jnp.int32, (1, pairs), 1)
+    core = (column >= slots).astype(jnp.int32)
+    within = column - core * slots
+    chip = within // slots_a_chip
+    stored = within + (chip + core) * slots_a_chip
+    row = lax.broadcasted_iota(jnp.int32, (pairs, lanes), 0)
+    for start in range(0, pairs, lanes):
+        select[:, start : start + lanes] = (row == stored[:, start : start + lanes]).astype(BF16)
+    values = jnp.broadcast_to(table[...], (16, pairs))
+    digit = lax.broadcasted_iota(jnp.int32, (16, pairs), 0)
+    digits = jnp.where(digit == 0, values // 32, values % 32).astype(F32).astype(BF16)
+    moved = jnp.dot(digits, select[...], preferred_element_type=F32)
+    sorted_table = (moved[0:1] * 32 + moved[1:2]).astype(jnp.int32)
+    tables[0] = sorted_table[:, :slots]
+    tables[1] = sorted_table[:, slots:]
+
+
+def order_kernel(
+    place, moved, table, integrals, matrices, slabs, there, here, wide, slots_by, tables, select, sems, *, occupied, chips
+):
     copies = slab_copies(place, 0, integrals, slabs, sems)
     for copy in copies:
         copy.start()
     core = (place[0] // 2) % 2
+    sort_table(table, tables, select, here.shape[1] // chips)
     choose(here, tables[core], occupied)
     spread_rows(moved, wide, slots_by)
     for start in range(0, here.shape[0] // occupied, KS_A_BLOCK):
@@ -113,13 +137,13 @@
         copy.wait()
 
 
-def order(place, moved, tables, integrals, occupied):
-    slots = tables.shape[2]
-    pairs = 2 * slots
+def order(place, moved, table, integrals, occupied, chips):
+    pairs = table.shape[1]
+    slots = pairs // 2
     width = moved.shape[1]
     rows = moved.shape[0] // slots
     return pl.pallas_call(
-        functools.partial(order_kernel, occupied=occupied),
+        functools.partial(order_kernel, occupied=occupied, chips=chips),
         out_shape=(
             pltpu.VMEM((rows * occupied, pairs // occupied * width), BF16),
             pltpu.VMEM((2,) + integrals.shape[2:], BF16),
@@ -131,12 +155,14 @@
             pltpu.VMEM((pairs, slots), BF16),
             pltpu.VMEM(((slots + 1) * rows, width), F32),
             pltpu.VMEM((slots, rows * width), BF16),
+            pltpu.VMEM((2, 1, slots), jnp.int32),
+            pltpu.VMEM((pairs, pairs), BF16),
             pltpu.SemaphoreType.DMA((2,)),
         ],
         compiler_params=PARAMS,
         cost_estimate=cost(2 * pairs * slots * rows * width, integrals.size),
         name="order",
-    )(place, moved, tables, integrals)
+    )(place, moved, table, integrals)
 
 
 def product_into(out, matrices, slabs, copies=()):
@@ -154,7 +180,11 @@
 def first_kernel(mine, moved, chooser, slabs, matrices, out, wide, slots_by, by_real, by_imag, *, occupied):
     half = matrices.shape[0] // 2
     width = moved.shape[1]
-    spread_rows(moved, wide, slots_by)
+    slots = slots_by.shape[0]
+    rows = moved.shape[0] // slots
+    wide[...] = moved[...].astype(F32)
+    for row in range(rows):
+        slots_by[:, row * width : (row + 1) * width] = wide[pl.ds(row, slots, stride=rows), :].astype(BF16)
     summed_occ = chooser.shape[0] // occupied
     order_block(0, chooser, slots_by, matrices, mine, width, occupied)
     for start in range(0, summed_occ, KS_A_BLOCK):
@@ -182,7 +212,7 @@
         in_specs=[IN_VMEM] * 4,
         out_specs=(IN_VMEM,) * 2,
         scratch_shapes=[
-            pltpu.VMEM(((slots + 1) * rows, width), F32),
+            pltpu.VMEM(moved.shape, F32),
             pltpu.VMEM((slots, rows * width), BF16),
             pltpu.VMEM((mine.shape[0], full_virtual), F32),
             pltpu.VMEM((mine.shape[0], full_virtual), F32),
@@ -336,12 +366,11 @@
     flat = pltpu.with_memory_space_constraint(flat, pltpu.HBM)
     across = lax.ppermute(moved, "core", SWAP)
 
-    tables = pair_table.reshape(chips, 2, slots).transpose(1, 0, 2).reshape(2, 1, chips * slots)
     places = jnp.arange(full_virtual, dtype=jnp.int32)[:, None]
     natural_order = (kramers[None, :] == places).astype(BF16)
     chip_order = (kramers[None, :] == places % chips * here + places // chips).astype(BF16)
 
-    mine, slabs, chooser = order(place, moved, tables, flat, occupied)
+    mine, slabs, chooser = order(place, moved, pair_table.reshape(1, pairs), flat, occupied, chips)
     matrices, to_send = first_window(mine, across, chooser, slabs, occupied)
     got = lax.ppermute(to_send, "vir", SWAP)
     kept = second_window(place, matrices, flat)

time: 80.8 us -> 80.8 us (level)
  transfers between devices with their start and end apart: 5 -> 5, of which waited for: 3 -> 3; matrix products, arithmetic and copies ran while one was open for 1% -> 0% of each run, Pallas kernels for 7% -> 7%
where the time goes in v6:
time: 80.8 us; the launch traced here: 80.6 us
  blocking collectives  54.9 us (68%)
  Pallas kernels  10.9 us (13%)
  starting transfers between devices  8.25 us (10%)
  waiting for transfers between devices  6.4 us (8%)
    all_to_all x1, blocking collectives, body(): lax.all_to_all(pieces, 'chip', split_axis=0, concat_axis=0, tiled=True)  37.8 us
    all_to_all x1, blocking collectives, body(): lax.all_to_all(mirror.reshape(chips, 8, -1), 'chip', split_axis=0, concat...  17.1 us
    ppermute x1, waiting for transfers between devices, body(): got = lax.ppermute(to_send, 'vir', SWAP)  4.1 us
    pallas_call x1, Pallas kernels, second_window(): pl.pallas_call(second_kernel, out_shape=jax.ShapeDtypeStruct((matrices.sh...  3.36 us
    ppermute x1, starting transfers between devices, body(): from_core = lax.ppermute(to_core, 'core', SWAP)  3.07 us
    ppermute x1, starting transfers between devices, body(): across = lax.ppermute(moved, 'core', SWAP)  3.05 us
    pallas_call x1, Pallas kernels, first_window(): pl.pallas_call(functools.partial(first_kernel, occupied=occupied), out_sh...  2.64 us
    pallas_call x1, Pallas kernels, order(): pl.pallas_call(functools.partial(order_kernel, occupied=occupied, chips=c...  2.19 us
  transfers between devices with their start and end apart: 5, of which 3 were waited for; matrix products, arithmetic and copies ran while one was open for 0% of the time, Pallas kernels for 7%

profile of v6, /device:TPU:1, one launch (start us, length us, event | category | flops | bytes accessed | tf_op | source)
XLA Modules:
  0.0 80.6 jit_solution(8375861292017081774)
XLA Ops:
  0.0 0.0 copy-start
  0.0 1.3 %regroup.1 = bf16[64,12,4,128]{3,2,1,0:T(4,128)(2,1)S(1)} custom-call(bf16[2,6,64,4,128]{4,3,2,1,0:T(4,128)(2,1)} %bitcast.13), custom_call_target="tpu_custom_call" | custom-call | tf_op jit(solution)/shard_map/regroup/pallas_call | solution.py:45
  1.3 37.8 %all_to_all.10 = bf16[64,12,4,128]{3,2,1,0:T(4,128)(2,1)S(1)} all-to-all(bf16[64,12,4,128]{3,2,1,0:T(4,128)(2,1)S(1)} %regroup.1), channel_id=1, replica_groups=mesh['chip'=64,'core'=2,'vir'=2] {'chip'}, dimensions={0} | all-to-all | bytes 1572864 | tf_op jit(solution)/shard_map/all_to_all | solution.py:363
  39.1 3.0 %collective-permute-start = (bf16[3072,128]{1,0:T(8,128)(2,1)S(1)}, bf16[3072,128]{1,0:T(8,128)(2,1)S(1)}, u32[]{:S(2)}, u32[]{:S(2)}) collective-permute-start(bf16[3072,128]{1,0:T(8,128)(2,1)S(1)} %bitcast.7), channel_id=1, source_target_pairs={{0,2},{2,0},{1,3},{3,1},{4,6},{6,4},{5,7},{7,5},{8,10},{10,8},{9,1... | collective-permute-start | bytes 2359304 | tf_op jit(solution)/shard_map/ppermute | solution.py:367
  42.2 0.0 copy-done
  42.2 2.2 %order.1 = (bf16[256,3072]{1,0:T(8,128)(2,1)S(1)}, bf16[2,3072,256]{2,1,0:T(8,128)(2,1)S(1)}, bf16[768,384]{1,0:T(8,128)(2,1)S(1)}) custom-call(s32[1]{0:T(128)} %bitcast.place, bf16[3072,128]{1,0:T(8,128)(2,1)S(1)} %bitcast.8, s32[1,768]{1,0:T(1,128)S(1)} %reshape.83.table, bf16[2,4,3072,256]{3,2,1,0:T(8,128)(2,1)} %bitcast.11), custom_call_target="tpu_custom_call" | custom-call | flops 603979776 | bytes 6291456 | tf_op jit(solution)/shard_map/order/pallas_call | solution.py:145
  44.4 0.0 copy-start.1
  44.4 0.0 collective-permute-done.moved
  44.4 2.6 %first_window.1 = (bf16[256,3072]{1,0:T(8,128)(2,1)S(1)}, f32[256,256]{1,0:T(8,128)S(1)}) custom-call(bf16[256,3072]{1,0:T(8,128)(2,1)S(1)} %get-tuple-element.16.mine, bf16[3072,128]{1,0:T(8,128)(2,1)S(1)} %collective-permute-done.moved, bf16[768,384]{1,0:T(8,128)(2,1)S(1)} %get-tuple-element.17.chooser, bf16[2,3072,256]{2,1,0:T(8,128)(2,1)S(1)} %get-tuple-element.18.slabs), custom_call_target="tpu_custom_call" | custom-call | flops 805306368 | bytes 3145728 | tf_op jit(solution)/shard_map/first_window/pallas_call | solution.py:206
  47.0 0.4 collective-permute-start.1
  47.4 0.0 copy-done.1
  47.4 0.1 compare_convert_fusion
  47.5 3.4 %second_window.1.kept = f32[256,256]{1,0:T(8,128)S(1)} custom-call(s32[1]{0:T(128)} %bitcast.place, bf16[256,3072]{1,0:T(8,128)(2,1)S(1)} %get-tuple-element.19.matrices, bf16[2,4,3072,256]{3,2,1,0:T(8,128)(2,1)} %bitcast.12), custom_call_target="tpu_custom_call" | custom-call | flops 805306368 | bytes 3145728 | tf_op jit(solution)/shard_map/second_window/pallas_call | solution.py:235
  50.9 4.1 %collective-permute-done.1.got = f32[256,256]{1,0:T(8,128)S(1)} collective-permute-done((f32[256,256]{1,0:T(8,128)S(1)}, f32[256,256]{1,0:T(8,128)S(1)}, u32[]{:S(2)}, u32[]{:S(2)}) %collective-permute-start.1) | collective-permute-done | bytes 262176 | tf_op jit(solution)/shard_map/ppermute | solution.py:375
  55.0 0.6 combine.1
  55.6 17.1 %all_to_all.11 = f32[64,8,128]{2,1,0:T(8,128)S(1)} all-to-all(f32[64,8,128]{2,1,0:T(8,128)S(1)} %bitcast.10), channel_id=1, replica_groups=mesh['chip'=64,'core'=2,'vir'=2] {'chip'}, dimensions={0} | all-to-all | bytes 524288 | tf_op jit(solution)/shard_map/all_to_all | solution.py:378
  72.7 0.1 subtract.1
  72.8 3.1 %collective-permute-start.2 = (bf16[2,64,128]{2,1,0:T(8,128)(2,1)S(1)}, bf16[2,64,128]{2,1,0:T(8,128)(2,1)S(1)}, u32[]{:S(2)}, u32[]{:S(2)}) collective-permute-start(bf16[2,64,128]{2,1,0:T(8,128)(2,1)S(1)} %get-tuple-element.24), channel_id=1, source_target_pairs={{0,2},{2,0},{1,3},{3,1},{4,6},{6,4},{5,7},{7,5},{8,10},{10,8},{9,1... | collective-permute-start | bytes 98312 | tf_op jit(solution)/shard_map/ppermute | solution.py:382
  75.9 0.3 collective-permute-start.3
  76.2 1.4 %collective-permute-start.4 = (bf16[2,64,128]{2,1,0:T(8,128)(2,1)S(1)}, bf16[2,64,128]{2,1,0:T(8,128)(2,1)S(1)}, u32[]{:S(2)}, u32[]{:S(2)}) collective-permute-start(bf16[2,64,128]{2,1,0:T(8,128)(2,1)S(1)} %get-tuple-element.26), channel_id=1, source_target_pairs={{0,3},{1,2},{2,1},{3,0},{4,7},{5,6},{6,5},{7,4},{8,11},{9,10},{10,... | collective-permute-start | bytes 98312 | tf_op jit(solution)/shard_map/ppermute | solution.py:381
  77.6 0.0 collective-permute-done.2.from_core
  77.7 1.0 %collective-permute-done.3.from_vir = bf16[2,64,128]{2,1,0:T(8,128)(2,1)S(1)} collective-permute-done((bf16[2,64,128]{2,1,0:T(8,128)(2,1)S(1)}, bf16[2,64,128]{2,1,0:T(8,128)(2,1)S(1)}, u32[]{:S(2)}, u32[]{:S(2)}) %collective-permute-start.3) | collective-permute-done | bytes 32800 | tf_op jit(solution)/shard_map/ppermute | solution.py:380
  78.7 1.2 %collective-permute-done.4.from_both = bf16[2,64,128]{2,1,0:T(8,128)(2,1)S(1)} collective-permute-done((bf16[2,64,128]{2,1,0:T(8,128)(2,1)S(1)}, bf16[2,64,128]{2,1,0:T(8,128)(2,1)S(1)}, u32[]{:S(2)}, u32[]{:S(2)}) %collective-permute-start.4) | collective-permute-done | bytes 32800 | tf_op jit(solution)/shard_map/ppermute | solution.py:381
  79.9 0.7 finish.1
  (2 shorter events, 0.0 us)
Async XLA Ops:
  0.0 42.2 %copy-start = (s32[768]{0:T(1024)S(1)}, s32[768]{0:T(1024)}, u32[]{:S(2)}) copy-start(s32[768]{0:T(1024)} %param.6) | copy-start | bytes 9220
  39.1 5.3 %collective-permute-start = (bf16[3072,128]{1,0:T(8,128)(2,1)S(1)}, bf16[3072,128]{1,0:T(8,128)(2,1)S(1)}, u32[]{:S(2)}, u32[]{:S(2)}) collective-permute-start(bf16[3072,128]{1,0:T(8,128)(2,1)S(1)} %bitcast.7), channel_id=1, source_target_pairs={{0,2},{2,0},{1,3},{3,1},{4,6},{6,4},{5,7},{7,5},{8,10},{10,8},{9,1... | collective-permute-start | bytes 2359304 | tf_op jit(solution)/shard_map/ppermute | solution.py:367
  44.4 3.1 %copy-start.1 = (s32[256]{0:T(256)S(1)}, s32[256]{0:T(256)}, u32[]{:S(2)}) copy-start(s32[256]{0:T(256)} %param.7) | copy-start | bytes 3076
  47.0 8.0 %collective-permute-start.1 = (f32[256,256]{1,0:T(8,128)S(1)}, f32[256,256]{1,0:T(8,128)S(1)}, u32[]{:S(2)}, u32[]{:S(2)}) collective-permute-start(f32[256,256]{1,0:T(8,128)S(1)} %get-tuple-element.20), channel_id=1, source_target_pairs={{0,1},{1,0},{2,3},{3,2},{4,5},{5,4},{6,7},{7,6},{8,9},{9,8},{10,11... | collective-permute-start | bytes 786440 | tf_op jit(solution)/shard_map/ppermute | solution.py:375
  72.8 4.8 %collective-permute-start.2 = (bf16[2,64,128]{2,1,0:T(8,128)(2,1)S(1)}, bf16[2,64,128]{2,1,0:T(8,128)(2,1)S(1)}, u32[]{:S(2)}, u32[]{:S(2)}) collective-permute-start(bf16[2,64,128]{2,1,0:T(8,128)(2,1)S(1)} %get-tuple-element.24), channel_id=1, source_target_pairs={{0,2},{2,0},{1,3},{3,1},{4,6},{6,4},{5,7},{7,5},{8,10},{10,8},{9,1... | collective-permute-start | bytes 98312 | tf_op jit(solution)/shard_map/ppermute | solution.py:382
  75.9 2.8 %collective-permute-start.3 = (bf16[2,64,128]{2,1,0:T(8,128)(2,1)S(1)}, bf16[2,64,128]{2,1,0:T(8,128)(2,1)S(1)}, u32[]{:S(2)}, u32[]{:S(2)}) collective-permute-start(bf16[2,64,128]{2,1,0:T(8,128)(2,1)S(1)} %get-tuple-element.25), channel_id=1, source_target_pairs={{0,1},{1,0},{2,3},{3,2},{4,5},{5,4},{6,7},{7,6},{8,9},{9,8},{10,11... | collective-permute-start | bytes 98312 | tf_op jit(solution)/shard_map/ppermute | solution.py:380
  76.2 3.7 %collective-permute-start.4 = (bf16[2,64,128]{2,1,0:T(8,128)(2,1)S(1)}, bf16[2,64,128]{2,1,0:T(8,128)(2,1)S(1)}, u32[]{:S(2)}, u32[]{:S(2)}) collective-permute-start(bf16[2,64,128]{2,1,0:T(8,128)(2,1)S(1)} %get-tuple-element.26), channel_id=1, source_target_pairs={{0,3},{1,2},{2,1},{3,0},{4,7},{5,6},{6,5},{7,4},{8,11},{9,10},{10,... | collective-permute-start | bytes 98312 | tf_op jit(solution)/shard_map/ppermute | solution.py:381

commit v7 on v3

--- a/solution.py
+++ b/solution.py
@@ -224,7 +224,7 @@
     return total + lax.dot_general(high, order_by, NT, preferred_element_type=F32)
 
 
-def combine_kernel(kept, got, natural_order, chip_order, own, mirror):
+def combine_kernel(kept, got, chip_order, own, mirror):
     full_virtual = kept.shape[1]
     rows = kept.shape[0] // 2
     chips = mirror.shape[0] // 8
@@ -233,7 +233,7 @@
     lane = lax.broadcasted_iota(jnp.int32, (occupied, 2 * chips), 1)
     values = kept[...] + got[...]
     by_chip = chosen(values, chip_order[...])
-    own[...] = chosen(values, natural_order[...])
+    own[...] = by_chip
     for part in range(2):
         for row in range(0, here, 2):
             at = part * rows + row * occupied
@@ -249,24 +249,27 @@
             mirror[pl.ds(2 * (row + 1) + part, chips, stride=8), :] = turned[chips:]
 
 
-def combine(kept, got, natural_order, chip_order, chips):
+def combine(kept, got, chip_order, chips):
     return pl.pallas_call(
         combine_kernel,
         out_shape=(jax.ShapeDtypeStruct(kept.shape, F32), jax.ShapeDtypeStruct((chips * 8, kept.shape[0] // 2), F32)),
         compiler_params=PARAMS,
         name="combine",
-    )(kept, got, natural_order, chip_order)
-
-
-def subtract_kernel(place, own, mirror, keep, to_core, to_vir, to_both, block):
+    )(kept, got, chip_order)
+
+
+def subtract_kernel(place, own, mirror, to_natural, keep, to_core, to_vir, to_both, block):
     vir, core = place[0] % 2, (place[0] // 2) % 2
     here = 2 * block.shape[1]
     rows, full_virtual = own.shape[0] // 2, own.shape[1]
     occupied = rows // here
     half = full_virtual // 2
     lanes = (slice(0, half), slice(half, full_virtual))
+    chips = mirror.shape[0] // 8
     for part in range(2):
-        values = own[part * rows : (part + 1) * rows] - mirror[pl.ds(part, full_virtual, stride=2), :].T
+        turned = jnp.concatenate([mirror[pl.ds(2 * row + part, chips, stride=8), :] for row in range(here)], axis=0).T
+        values = (own[part * rows : (part + 1) * rows] - turned).astype(BF16)
+        values = jnp.dot(values, to_natural[...], preferred_element_type=F32)
         for row in range(here):
             for side in range(2):
                 block[part, row // 2, side, pl.ds(row % 2, occupied, stride=2), :] = values[
@@ -282,18 +285,18 @@
             target[part] = block[part, to_side, to_half].astype(BF16)
 
 
-def subtract(place, own, mirror):
+def subtract(place, own, mirror, to_natural):
     rows, full_virtual = own.shape[0] // 2, own.shape[1]
     piece = jax.ShapeDtypeStruct((2, rows // 2, full_virtual // 2), BF16)
     return pl.pallas_call(
         subtract_kernel,
         out_shape=(piece,) * 4,
-        in_specs=[IN_SMEM, IN_VMEM, IN_VMEM],
+        in_specs=[IN_SMEM] + [IN_VMEM] * 3,
         out_specs=(IN_VMEM,) * 4,
         scratch_shapes=[pltpu.VMEM((2, 2, 2, rows // 2, full_virtual // 2), F32)],
         compiler_params=PARAMS,
         name="subtract",
-    )(place, own, mirror)
+    )(place, own, mirror, to_natural)
 
 
 def finish_kernel(place, keep, from_core, from_vir, from_both, out):
@@ -338,16 +341,16 @@
 
     tables = pair_table.reshape(chips, 2, slots).transpose(1, 0, 2).reshape(2, 1, chips * slots)
     places = jnp.arange(full_virtual, dtype=jnp.int32)[:, None]
-    natural_order = (kramers[None, :] == places).astype(BF16)
+    to_natural = (places % chips * here + places // chips == places.T).astype(BF16)
     chip_order = (kramers[None, :] == places % chips * here + places // chips).astype(BF16)
 
     mine, slabs, chooser = order(place, moved, tables, flat, occupied)
     matrices, to_send = first_window(mine, across, chooser, slabs, occupied)
     got = lax.ppermute(to_send, "vir", SWAP)
     kept = second_window(place, matrices, flat)
-    own, mirror = combine(kept, got, natural_order, chip_order, chips)
+    own, mirror = combine(kept, got, chip_order, chips)
     mirror = lax.all_to_all(mirror.reshape(chips, 8, -1), "chip", split_axis=0, concat_axis=0, tiled=True)
-    keep, to_core, to_vir, to_both = subtract(place, own, mirror.reshape(chips * 8, -1))
+    keep, to_core, to_vir, to_both = subtract(place, own, mirror.reshape(chips * 8, -1), to_natural)
     from_vir = lax.ppermute(to_vir, "vir", SWAP)
     from_both = lax.ppermute(to_both, ("core", "vir"), SWAP_BOTH)
     from_core = lax.ppermute(to_core, "core", SWAP)

time: 80.9 us -> 81 us (level)
  no operation moved by 1% of the time
where the time goes in v7:
time: 81 us; the launch traced here: 80.7 us
  blocking collectives  54.9 us (68%)
  Pallas kernels  10.7 us (13%)
  starting transfers between devices  8.17 us (10%)
  waiting for transfers between devices  6.44 us (8%)
    all_to_all x1, blocking collectives, body(): lax.all_to_all(pieces, 'chip', split_axis=0, concat_axis=0, tiled=True)  37.8 us
    all_to_all x1, blocking collectives, body(): lax.all_to_all(mirror.reshape(chips, 8, -1), 'chip', split_axis=0, concat...  17.1 us
    ppermute x1, waiting for transfers between devices, body(): got = lax.ppermute(to_send, 'vir', SWAP)  4.14 us
    pallas_call x1, Pallas kernels, second_window(): pl.pallas_call(second_kernel, out_shape=jax.ShapeDtypeStruct((matrices.sh...  3.36 us
    ppermute x1, starting transfers between devices, body(): across = lax.ppermute(moved, 'core', SWAP)  3.05 us
    ppermute x1, starting transfers between devices, body(): from_core = lax.ppermute(to_core, 'core', SWAP)  2.99 us
    pallas_call x1, Pallas kernels, first_window(): pl.pallas_call(functools.partial(first_kernel, occupied=occupied), out_sh...  2.66 us
    pallas_call x1, Pallas kernels, order(): pl.pallas_call(functools.partial(order_kernel, occupied=occupied), out_sh...  1.92 us
  transfers between devices with their start and end apart: 5, of which 3 were waited for; matrix products, arithmetic and copies ran while one was open for 1% of the time, Pallas kernels for 7%

profile of v7, /device:TPU:1, one launch (start us, length us, event | category | flops | bytes accessed | tf_op | source)
XLA Modules:
  0.0 80.7 jit_solution(11474462443950385628)
XLA Ops:
  0.0 0.0 copy-start
  0.0 1.3 %regroup.1 = bf16[64,12,4,128]{3,2,1,0:T(4,128)(2,1)S(1)} custom-call(bf16[2,6,64,4,128]{4,3,2,1,0:T(4,128)(2,1)} %bitcast.14), custom_call_target="tpu_custom_call" | custom-call | tf_op jit(solution)/shard_map/regroup/pallas_call | solution.py:45
  1.3 37.8 %all_to_all.10 = bf16[64,12,4,128]{3,2,1,0:T(4,128)(2,1)S(1)} all-to-all(bf16[64,12,4,128]{3,2,1,0:T(4,128)(2,1)S(1)} %regroup.1), channel_id=1, replica_groups=mesh['chip'=64,'core'=2,'vir'=2] {'chip'}, dimensions={0} | all-to-all | bytes 1572864 | tf_op jit(solution)/shard_map/all_to_all | solution.py:336
  39.1 3.0 %collective-permute-start = (bf16[3072,128]{1,0:T(8,128)(2,1)S(1)}, bf16[3072,128]{1,0:T(8,128)(2,1)S(1)}, u32[]{:S(2)}, u32[]{:S(2)}) collective-permute-start(bf16[3072,128]{1,0:T(8,128)(2,1)S(1)} %bitcast.8), channel_id=1, source_target_pairs={{0,2},{2,0},{1,3},{3,1},{4,6},{6,4},{5,7},{7,5},{8,10},{10,8},{9,1... | collective-permute-start | bytes 2359304 | tf_op jit(solution)/shard_map/ppermute | solution.py:340
  42.2 0.0 copy-done
  42.2 0.2 reshape.86
  42.3 0.1 reshape.92.tables
  42.5 1.9 %order.1 = (bf16[256,3072]{1,0:T(8,128)(2,1)S(1)}, bf16[2,3072,256]{2,1,0:T(8,128)(2,1)S(1)}, bf16[768,384]{1,0:T(8,128)(2,1)S(1)}) custom-call(s32[1]{0:T(128)} %bitcast.place, bf16[3072,128]{1,0:T(8,128)(2,1)S(1)} %bitcast.9, s32[2,1,384]{2,1,0:T(1,128)S(1)} %reshape.92.tables, bf16[2,4,3072,256]{3,2,1,0:T(8,128)(2,1)} %bitcast.12), custom_call_target="tpu_custom_call" | custom-call | flops 603979776 | bytes 6291456 | tf_op jit(solution)/shard_map/order/pallas_call | solution.py:121
  44.4 0.0 copy-start.1
  44.4 0.0 collective-permute-done.moved
  44.4 2.7 %first_window.1 = (bf16[256,3072]{1,0:T(8,128)(2,1)S(1)}, f32[256,256]{1,0:T(8,128)S(1)}) custom-call(bf16[256,3072]{1,0:T(8,128)(2,1)S(1)} %get-tuple-element.16.mine, bf16[3072,128]{1,0:T(8,128)(2,1)S(1)} %collective-permute-done.moved, bf16[768,384]{1,0:T(8,128)(2,1)S(1)} %get-tuple-element.17.chooser, bf16[2,3072,256]{2,1,0:T(8,128)(2,1)S(1)} %get-tuple-element.18.slabs), custom_call_target="tpu_custom_call" | custom-call | flops 805306368 | bytes 3145728 | tf_op jit(solution)/shard_map/first_window/pallas_call | solution.py:176
  47.1 0.4 collective-permute-start.1
  47.5 0.0 copy-done.1
  47.5 0.1 fusion
  47.6 3.4 %second_window.1.kept = f32[256,256]{1,0:T(8,128)S(1)} custom-call(s32[1]{0:T(128)} %bitcast.place, bf16[256,3072]{1,0:T(8,128)(2,1)S(1)} %get-tuple-element.19.matrices, bf16[2,4,3072,256]{3,2,1,0:T(8,128)(2,1)} %bitcast.13), custom_call_target="tpu_custom_call" | custom-call | flops 805306368 | bytes 3145728 | tf_op jit(solution)/shard_map/second_window/pallas_call | solution.py:205
  51.0 4.1 %collective-permute-done.1.got = f32[256,256]{1,0:T(8,128)S(1)} collective-permute-done((f32[256,256]{1,0:T(8,128)S(1)}, f32[256,256]{1,0:T(8,128)S(1)}, u32[]{:S(2)}, u32[]{:S(2)}) %collective-permute-start.1) | collective-permute-done | bytes 262176 | tf_op jit(solution)/shard_map/ppermute | solution.py:349
  55.1 0.5 combine.1
  55.7 17.1 %all_to_all.11 = f32[64,8,128]{2,1,0:T(8,128)S(1)} all-to-all(f32[64,8,128]{2,1,0:T(8,128)S(1)} %bitcast.11), channel_id=1, replica_groups=mesh['chip'=64,'core'=2,'vir'=2] {'chip'}, dimensions={0} | all-to-all | bytes 524288 | tf_op jit(solution)/shard_map/all_to_all | solution.py:352
  72.8 0.3 subtract.1
  73.1 3.0 %collective-permute-start.2 = (bf16[2,64,128]{2,1,0:T(8,128)(2,1)S(1)}, bf16[2,64,128]{2,1,0:T(8,128)(2,1)S(1)}, u32[]{:S(2)}, u32[]{:S(2)}) collective-permute-start(bf16[2,64,128]{2,1,0:T(8,128)(2,1)S(1)} %get-tuple-element.24), channel_id=1, source_target_pairs={{0,2},{2,0},{1,3},{3,1},{4,6},{6,4},{5,7},{7,5},{8,10},{10,8},{9,1... | collective-permute-start | bytes 98312 | tf_op jit(solution)/shard_map/ppermute | solution.py:356
  76.1 0.3 collective-permute-start.3
  76.4 1.4 %collective-permute-start.4 = (bf16[2,64,128]{2,1,0:T(8,128)(2,1)S(1)}, bf16[2,64,128]{2,1,0:T(8,128)(2,1)S(1)}, u32[]{:S(2)}, u32[]{:S(2)}) collective-permute-start(bf16[2,64,128]{2,1,0:T(8,128)(2,1)S(1)} %get-tuple-element.26), channel_id=1, source_target_pairs={{0,3},{1,2},{2,1},{3,0},{4,7},{5,6},{6,5},{7,4},{8,11},{9,10},{10,... | collective-permute-start | bytes 98312 | tf_op jit(solution)/shard_map/ppermute | solution.py:355
  77.8 0.0 collective-permute-done.2.from_core
  77.8 1.0 %collective-permute-done.3.from_vir = bf16[2,64,128]{2,1,0:T(8,128)(2,1)S(1)} collective-permute-done((bf16[2,64,128]{2,1,0:T(8,128)(2,1)S(1)}, bf16[2,64,128]{2,1,0:T(8,128)(2,1)S(1)}, u32[]{:S(2)}, u32[]{:S(2)}) %collective-permute-start.3) | collective-permute-done | bytes 32800 | tf_op jit(solution)/shard_map/ppermute | solution.py:354
  78.8 1.2 %collective-permute-done.4.from_both = bf16[2,64,128]{2,1,0:T(8,128)(2,1)S(1)} collective-permute-done((bf16[2,64,128]{2,1,0:T(8,128)(2,1)S(1)}, bf16[2,64,128]{2,1,0:T(8,128)(2,1)S(1)}, u32[]{:S(2)}, u32[]{:S(2)}) %collective-permute-start.4) | collective-permute-done | bytes 32800 | tf_op jit(solution)/shard_map/ppermute | solution.py:355
  80.1 0.7 finish.1
  (2 shorter events, 0.0 us)
Async XLA Ops:
  0.0 42.2 %copy-start = (s32[768]{0:T(1024)S(1)}, s32[768]{0:T(1024)}, u32[]{:S(2)}) copy-start(s32[768]{0:T(1024)} %param.6) | copy-start | bytes 9220
  39.1 5.3 %collective-permute-start = (bf16[3072,128]{1,0:T(8,128)(2,1)S(1)}, bf16[3072,128]{1,0:T(8,128)(2,1)S(1)}, u32[]{:S(2)}, u32[]{:S(2)}) collective-permute-start(bf16[3072,128]{1,0:T(8,128)(2,1)S(1)} %bitcast.8), channel_id=1, source_target_pairs={{0,2},{2,0},{1,3},{3,1},{4,6},{6,4},{5,7},{7,5},{8,10},{10,8},{9,1... | collective-permute-start | bytes 2359304 | tf_op jit(solution)/shard_map/ppermute | solution.py:340
  44.4 3.1 %copy-start.1 = (s32[256]{0:T(256)S(1)}, s32[256]{0:T(256)}, u32[]{:S(2)}) copy-start(s32[256]{0:T(256)} %param.7) | copy-start | bytes 3076
  47.1 8.0 %collective-permute-start.1 = (f32[256,256]{1,0:T(8,128)S(1)}, f32[256,256]{1,0:T(8,128)S(1)}, u32[]{:S(2)}, u32[]{:S(2)}) collective-permute-start(f32[256,256]{1,0:T(8,128)S(1)} %get-tuple-element.20), channel_id=1, source_target_pairs={{0,1},{1,0},{2,3},{3,2},{4,5},{5,4},{6,7},{7,6},{8,9},{9,8},{10,11... | collective-permute-start | bytes 786440 | tf_op jit(solution)/shard_map/ppermute | solution.py:349
  73.1 4.7 %collective-permute-start.2 = (bf16[2,64,128]{2,1,0:T(8,128)(2,1)S(1)}, bf16[2,64,128]{2,1,0:T(8,128)(2,1)S(1)}, u32[]{:S(2)}, u32[]{:S(2)}) collective-permute-start(bf16[2,64,128]{2,1,0:T(8,128)(2,1)S(1)} %get-tuple-element.24), channel_id=1, source_target_pairs={{0,2},{2,0},{1,3},{3,1},{4,6},{6,4},{5,7},{7,5},{8,10},{10,8},{9,1... | collective-permute-start | bytes 98312 | tf_op jit(solution)/shard_map/ppermute | solution.py:356
  76.1 2.8 %collective-permute-start.3 = (bf16[2,64,128]{2,1,0:T(8,128)(2,1)S(1)}, bf16[2,64,128]{2,1,0:T(8,128)(2,1)S(1)}, u32[]{:S(2)}, u32[]{:S(2)}) collective-permute-start(bf16[2,64,128]{2,1,0:T(8,128)(2,1)S(1)} %get-tuple-element.25), channel_id=1, source_target_pairs={{0,1},{1,0},{2,3},{3,2},{4,5},{5,4},{6,7},{7,6},{8,9},{9,8},{10,11... | collective-permute-start | bytes 98312 | tf_op jit(solution)/shard_map/ppermute | solution.py:354
  76.4 3.7 %collective-permute-start.4 = (bf16[2,64,128]{2,1,0:T(8,128)(2,1)S(1)}, bf16[2,64,128]{2,1,0:T(8,128)(2,1)S(1)}, u32[]{:S(2)}, u32[]{:S(2)}) collective-permute-start(bf16[2,64,128]{2,1,0:T(8,128)(2,1)S(1)} %get-tuple-element.26), channel_id=1, source_target_pairs={{0,3},{1,2},{2,1},{3,0},{4,7},{5,6},{6,5},{7,4},{8,11},{9,10},{10,... | collective-permute-start | bytes 98312 | tf_op jit(solution)/shard_map/ppermute | solution.py:355

commit v8 on v3

--- a/solution.py
+++ b/solution.py
@@ -151,7 +151,7 @@
     out[half:] = by_real[half:] + by_imag[:half]
 
 
-def first_kernel(mine, moved, chooser, slabs, matrices, out, wide, slots_by, by_real, by_imag, *, occupied):
+def first_kernel(mine, moved, chooser, slabs, matrices, real, imag, wide, slots_by, by_real, by_imag, *, occupied):
     half = matrices.shape[0] // 2
     width = moved.shape[1]
     spread_rows(moved, wide, slots_by)
@@ -164,8 +164,8 @@
         for part, total in enumerate((by_real, by_imag)):
             product = jnp.dot(matrices[:, lanes], slabs[part, lanes], preferred_element_type=F32)
             total[...] = product if start == 0 else total[...] + product
-    out[:half] = by_real[:half] - by_imag[half:]
-    out[half:] = by_real[half:] + by_imag[:half]
+    real[...] = by_real[:half] - by_imag[half:]
+    imag[...] = by_real[half:] + by_imag[:half]
 
 
 def first_window(mine, moved, chooser, slabs, occupied):
@@ -177,10 +177,11 @@
         functools.partial(first_kernel, occupied=occupied),
         out_shape=(
             jax.ShapeDtypeStruct(mine.shape, BF16),
-            jax.ShapeDtypeStruct((mine.shape[0], full_virtual), F32),
+            jax.ShapeDtypeStruct((mine.shape[0] // 2, full_virtual), F32),
+            jax.ShapeDtypeStruct((mine.shape[0] // 2, full_virtual), F32),
         ),
         in_specs=[IN_VMEM] * 4,
-        out_specs=(IN_VMEM,) * 2,
+        out_specs=(IN_VMEM,) * 3,
         scratch_shapes=[
             pltpu.VMEM(((slots + 1) * rows, width), F32),
             pltpu.VMEM((slots, rows * width), BF16),
@@ -224,49 +225,61 @@
     return total + lax.dot_general(high, order_by, NT, preferred_element_type=F32)
 
 
-def combine_kernel(kept, got, natural_order, chip_order, own, mirror):
+def combine_kernel(kept, got, natural_order, chip_order, *refs, part):
+    own, mirror = refs[-2:]
     full_virtual = kept.shape[1]
     rows = kept.shape[0] // 2
-    chips = mirror.shape[0] // 8
+    chips = full_virtual // 4
     here = full_virtual // chips
     occupied = rows // here
     lane = lax.broadcasted_iota(jnp.int32, (occupied, 2 * chips), 1)
-    values = kept[...] + got[...]
+    values = kept[part * rows : (part + 1) * rows] + got[...]
     by_chip = chosen(values, chip_order[...])
     own[...] = chosen(values, natural_order[...])
-    for part in range(2):
-        for row in range(0, here, 2):
-            at = part * rows + row * occupied
-            blocks = []
-            for other in range(0, here, 2):
-                lanes = slice(other * chips, (other + 2) * chips)
-                low = by_chip[at : at + occupied, lanes]
-                high = by_chip[at + occupied : at + 2 * occupied, lanes]
-                blocks.append(jnp.where(lane < chips, low, pltpu.roll(high, chips, 1)))
-                blocks.append(jnp.where(lane < chips, pltpu.roll(low, chips, 1), high))
-            turned = jnp.concatenate(blocks, axis=0).T
-            mirror[pl.ds(2 * row + part, chips, stride=8), :] = turned[:chips]
-            mirror[pl.ds(2 * (row + 1) + part, chips, stride=8), :] = turned[chips:]
-
-
-def combine(kept, got, natural_order, chip_order, chips):
-    return pl.pallas_call(
-        combine_kernel,
-        out_shape=(jax.ShapeDtypeStruct(kept.shape, F32), jax.ShapeDtypeStruct((chips * 8, kept.shape[0] // 2), F32)),
-        compiler_params=PARAMS,
+    if part == 1:
+        for row in range(here):
+            mirror[pl.ds(2 * row, chips, stride=8), :] = refs[0][pl.ds(row, chips, stride=4), :]
+    for row in range(0, here, 2):
+        at = row * occupied
+        blocks = []
+        for other in range(0, here, 2):
+            lanes = slice(other * chips, (other + 2) * chips)
+            low = by_chip[at : at + occupied, lanes]
+            high = by_chip[at + occupied : at + 2 * occupied, lanes]
+            blocks.append(jnp.where(lane < chips, low, pltpu.roll(high, chips, 1)))
+            blocks.append(jnp.where(lane < chips, pltpu.roll(low, chips, 1), high))
+        turned = jnp.concatenate(blocks, axis=0).T
+        for side in range(2):
+            half = turned[side * chips : (side + 1) * chips]
+            if part == 0:
+                mirror[pl.ds(row + side, chips, stride=4), :] = half
+            else:
+                mirror[pl.ds(2 * (row + side) + 1, chips, stride=8), :] = half
+
+
+def combine(part, kept, got, natural_order, chip_order, chips, *before):
+    rows, full_virtual = got.shape
+    return pl.pallas_call(
+        functools.partial(combine_kernel, part=part),
+        out_shape=(
+            jax.ShapeDtypeStruct((rows, full_virtual), F32),
+            jax.ShapeDtypeStruct((chips * (4 + 4 * part), rows), F32),
+        ),
+        compiler_params=PARAMS,
+        cost_estimate=cost(12 * rows * full_virtual * full_virtual, 16 * rows * full_virtual),
         name="combine",
-    )(kept, got, natural_order, chip_order)
-
-
-def subtract_kernel(place, own, mirror, keep, to_core, to_vir, to_both, block):
+    )(kept, got, natural_order, chip_order, *before)
+
+
+def subtract_kernel(place, real, imag, mirror, keep, to_core, to_vir, to_both, block):
     vir, core = place[0] % 2, (place[0] // 2) % 2
     here = 2 * block.shape[1]
-    rows, full_virtual = own.shape[0] // 2, own.shape[1]
+    rows, full_virtual = real.shape
     occupied = rows // here
     half = full_virtual // 2
     lanes = (slice(0, half), slice(half, full_virtual))
     for part in range(2):
-        values = own[part * rows : (part + 1) * rows] - mirror[pl.ds(part, full_virtual, stride=2), :].T
+        values = (real, imag)[part][...] - mirror[pl.ds(part, full_virtual, stride=2), :].T
         for row in range(here):
             for side in range(2):
                 block[part, row // 2, side, pl.ds(row % 2, occupied, stride=2), :] = values[
@@ -282,18 +295,18 @@
             target[part] = block[part, to_side, to_half].astype(BF16)
 
 
-def subtract(place, own, mirror):
-    rows, full_virtual = own.shape[0] // 2, own.shape[1]
+def subtract(place, real, imag, mirror):
+    rows, full_virtual = real.shape
     piece = jax.ShapeDtypeStruct((2, rows // 2, full_virtual // 2), BF16)
     return pl.pallas_call(
         subtract_kernel,
         out_shape=(piece,) * 4,
-        in_specs=[IN_SMEM, IN_VMEM, IN_VMEM],
+        in_specs=[IN_SMEM] + [IN_VMEM] * 3,
         out_specs=(IN_VMEM,) * 4,
         scratch_shapes=[pltpu.VMEM((2, 2, 2, rows // 2, full_virtual // 2), F32)],
         compiler_params=PARAMS,
         name="subtract",
-    )(place, own, mirror)
+    )(place, real, imag, mirror)
 
 
 def finish_kernel(place, keep, from_core, from_vir, from_both, out):
@@ -342,12 +355,14 @@
     chip_order = (kramers[None, :] == places % chips * here + places // chips).astype(BF16)
 
     mine, slabs, chooser = order(place, moved, tables, flat, occupied)
-    matrices, to_send = first_window(mine, across, chooser, slabs, occupied)
-    got = lax.ppermute(to_send, "vir", SWAP)
+    matrices, real, imag = first_window(mine, across, chooser, slabs, occupied)
+    got_real = lax.ppermute(real, "vir", SWAP)
+    got_imag = lax.ppermute(imag, "vir", SWAP)
     kept = second_window(place, matrices, flat)
-    own, mirror = combine(kept, got, natural_order, chip_order, chips)
+    real, before = combine(0, kept, got_real, natural_order, chip_order, chips)
+    imag, mirror = combine(1, kept, got_imag, natural_order, chip_order, chips, before)
     mirror = lax.all_to_all(mirror.reshape(chips, 8, -1), "chip", split_axis=0, concat_axis=0, tiled=True)
-    keep, to_core, to_vir, to_both = subtract(place, own, mirror.reshape(chips * 8, -1))
+    keep, to_core, to_vir, to_both = subtract(place, real, imag, mirror.reshape(chips * 8, -1))
     from_vir = lax.ppermute(to_vir, "vir", SWAP)
     from_both = lax.ppermute(to_both, ("core", "vir"), SWAP_BOTH)
     from_core = lax.ppermute(to_core, "core", SWAP)

time: 80.9 us -> 80.9 us (level)
  waiting for transfers between devices: 6.44 us -> 4.73 us
  starting transfers between devices: 8.14 us -> 9.32 us
    ppermute x1 -> x2, waiting for transfers between devices: 4.15 us -> 2.43 us  [the longest x1 2.25 us: body(): got_imag = lax.ppermute(imag, 'vir', SWAP)]
    ppermute x1 -> x2, starting transfers between devices: 0.4 us -> 1.55 us  [the longest x1 1.15 us: body(): got_imag = lax.ppermute(imag, 'vir', SWAP)]
  transfers between devices with their start and end apart: 5 -> 6, of which waited for: 3 -> 4; matrix products, arithmetic and copies ran while one was open for 1% -> 1% of each run, Pallas kernels for 7% -> 7%
where the time goes in v8:
time: 80.9 us; the launch traced here: 80.7 us
  blocking collectives  54.9 us (68%)
  Pallas kernels  11.2 us (14%)
  starting transfers between devices  9.32 us (12%)
  waiting for transfers between devices  4.73 us (6%)
    all_to_all x1, blocking collectives, body(): lax.all_to_all(pieces, 'chip', split_axis=0, concat_axis=0, tiled=True)  37.8 us
    all_to_all x1, blocking collectives, body(): lax.all_to_all(mirror.reshape(chips, 8, -1), 'chip', split_axis=0, concat...  17.1 us
    pallas_call x1, Pallas kernels, second_window(): pl.pallas_call(second_kernel, out_shape=jax.ShapeDtypeStruct((matrices.sh...  3.36 us
    ppermute x1, starting transfers between devices, body(): across = lax.ppermute(moved, 'core', SWAP)  3.05 us
    ppermute x1, starting transfers between devices, body(): from_core = lax.ppermute(to_core, 'core', SWAP)  2.99 us
    pallas_call x1, Pallas kernels, first_window(): pl.pallas_call(functools.partial(first_kernel, occupied=occupied), out_sh...  2.66 us
    ppermute x1, waiting for transfers between devices, body(): got_imag = lax.ppermute(imag, 'vir', SWAP)  2.25 us
    pallas_call x1, Pallas kernels, order(): pl.pallas_call(functools.partial(order_kernel, occupied=occupied), out_sh...  1.92 us
  transfers between devices with their start and end apart: 6, of which 4 were waited for; matrix products, arithmetic and copies ran while one was open for 1% of the time, Pallas kernels for 7%

profile of v8, /device:TPU:1, one launch (start us, length us, event | category | flops | bytes accessed | tf_op | source)
XLA Modules:
  0.0 80.7 jit_solution(13872788412036352465)
XLA Ops:
  0.0 0.0 copy-start
  0.0 1.3 %regroup.1 = bf16[64,12,4,128]{3,2,1,0:T(4,128)(2,1)S(1)} custom-call(bf16[2,6,64,4,128]{4,3,2,1,0:T(4,128)(2,1)} %bitcast.14), custom_call_target="tpu_custom_call" | custom-call | tf_op jit(solution)/shard_map/regroup/pallas_call | solution.py:45
  1.3 37.8 %all_to_all.10 = bf16[64,12,4,128]{3,2,1,0:T(4,128)(2,1)S(1)} all-to-all(bf16[64,12,4,128]{3,2,1,0:T(4,128)(2,1)S(1)} %regroup.1), channel_id=1, replica_groups=mesh['chip'=64,'core'=2,'vir'=2] {'chip'}, dimensions={0} | all-to-all | bytes 1572864 | tf_op jit(solution)/shard_map/all_to_all | solution.py:346
  39.1 3.0 %collective-permute-start = (bf16[3072,128]{1,0:T(8,128)(2,1)S(1)}, bf16[3072,128]{1,0:T(8,128)(2,1)S(1)}, u32[]{:S(2)}, u32[]{:S(2)}) collective-permute-start(bf16[3072,128]{1,0:T(8,128)(2,1)S(1)} %bitcast.8), channel_id=1, source_target_pairs={{0,2},{2,0},{1,3},{3,1},{4,6},{6,4},{5,7},{7,5},{8,10},{10,8},{9,1... | collective-permute-start | bytes 2359304 | tf_op jit(solution)/shard_map/ppermute | solution.py:350
  42.2 0.0 copy-done
  42.2 0.2 reshape.86
  42.3 0.1 reshape.92.tables
  42.5 1.9 %order.1 = (bf16[256,3072]{1,0:T(8,128)(2,1)S(1)}, bf16[2,3072,256]{2,1,0:T(8,128)(2,1)S(1)}, bf16[768,384]{1,0:T(8,128)(2,1)S(1)}) custom-call(s32[1]{0:T(128)} %bitcast.place, bf16[3072,128]{1,0:T(8,128)(2,1)S(1)} %bitcast.9, s32[2,1,384]{2,1,0:T(1,128)S(1)} %reshape.92.tables, bf16[2,4,3072,256]{3,2,1,0:T(8,128)(2,1)} %bitcast.12), custom_call_target="tpu_custom_call" | custom-call | flops 603979776 | bytes 6291456 | tf_op jit(solution)/shard_map/order/pallas_call | solution.py:121
  44.4 0.0 copy-start.1
  44.4 0.0 collective-permute-done.moved
  44.4 2.7 %first_window.1 = (bf16[256,3072]{1,0:T(8,128)(2,1)S(1)}, f32[128,256]{1,0:T(8,128)S(1)}, f32[128,256]{1,0:T(8,128)S(1)}) custom-call(bf16[256,3072]{1,0:T(8,128)(2,1)S(1)} %get-tuple-element.19.mine, bf16[3072,128]{1,0:T(8,128)(2,1)S(1)} %collective-permute-done.moved, bf16[768,384]{1,0:T(8,128)(2,1)S(1)} %get-tuple-element.20.chooser, ...), custom_call_target="tpu_custom_call" | custom-call | flops 805306368 | bytes 3145728 | tf_op jit(solution)/shard_map/first_window/pallas_call | solution.py:176
  47.1 0.4 collective-permute-start.1
  47.5 1.2 %collective-permute-start.2 = (f32[128,256]{1,0:T(8,128)S(1)}, f32[128,256]{1,0:T(8,128)S(1)}, u32[]{:S(2)}, u32[]{:S(2)}) collective-permute-start(f32[128,256]{1,0:T(8,128)S(1)} %get-tuple-element.25), channel_id=1, source_target_pairs={{0,1},{1,0},{2,3},{3,2},{4,5},{5,4},{6,7},{7,6},{8,9},{9,8},{10,11... | collective-permute-start | bytes 393224 | tf_op jit(solution)/shard_map/ppermute | solution.py:360
  48.7 0.0 copy-done.1
  48.7 0.1 compare_convert_fusion
  48.8 3.4 %second_window.1.kept = f32[256,256]{1,0:T(8,128)S(1)} custom-call(s32[1]{0:T(128)} %bitcast.place, bf16[256,3072]{1,0:T(8,128)(2,1)S(1)} %get-tuple-element.22.matrices, bf16[2,4,3072,256]{3,2,1,0:T(8,128)(2,1)} %bitcast.13), custom_call_target="tpu_custom_call" | custom-call | flops 805306368 | bytes 3145728 | tf_op jit(solution)/shard_map/second_window/pallas_call | solution.py:206
  52.1 0.2 collective-permute-done.1.got
  52.3 0.6 combine.2
  52.9 2.2 %collective-permute-done.2.got = f32[128,256]{1,0:T(8,128)S(1)} collective-permute-done((f32[128,256]{1,0:T(8,128)S(1)}, f32[128,256]{1,0:T(8,128)S(1)}, u32[]{:S(2)}, u32[]{:S(2)}) %collective-permute-start.2) | collective-permute-done | bytes 131104 | tf_op jit(solution)/shard_map/ppermute | solution.py:360
  55.1 0.6 combine.3
  55.7 17.1 %all_to_all.11 = f32[64,8,128]{2,1,0:T(8,128)S(1)} all-to-all(f32[64,8,128]{2,1,0:T(8,128)S(1)} %bitcast.11), channel_id=1, replica_groups=mesh['chip'=64,'core'=2,'vir'=2] {'chip'}, dimensions={0} | all-to-all | bytes 524288 | tf_op jit(solution)/shard_map/all_to_all | solution.py:364
  72.8 0.1 subtract.1
  73.0 3.0 %collective-permute-start.3 = (bf16[2,64,128]{2,1,0:T(8,128)(2,1)S(1)}, bf16[2,64,128]{2,1,0:T(8,128)(2,1)S(1)}, u32[]{:S(2)}, u32[]{:S(2)}) collective-permute-start(bf16[2,64,128]{2,1,0:T(8,128)(2,1)S(1)} %get-tuple-element.30), channel_id=1, source_target_pairs={{0,2},{2,0},{1,3},{3,1},{4,6},{6,4},{5,7},{7,5},{8,10},{10,8},{9,1... | collective-permute-start | bytes 98312 | tf_op jit(solution)/shard_map/ppermute | solution.py:368
  76.0 0.3 collective-permute-start.4
  76.3 1.4 %collective-permute-start.5 = (bf16[2,64,128]{2,1,0:T(8,128)(2,1)S(1)}, bf16[2,64,128]{2,1,0:T(8,128)(2,1)S(1)}, u32[]{:S(2)}, u32[]{:S(2)}) collective-permute-start(bf16[2,64,128]{2,1,0:T(8,128)(2,1)S(1)} %get-tuple-element.32), channel_id=1, source_target_pairs={{0,3},{1,2},{2,1},{3,0},{4,7},{5,6},{6,5},{7,4},{8,11},{9,10},{10,... | collective-permute-start | bytes 98312 | tf_op jit(solution)/shard_map/ppermute | solution.py:367
  77.7 0.0 collective-permute-done.3.from_core
  77.7 1.0 %collective-permute-done.4.from_vir = bf16[2,64,128]{2,1,0:T(8,128)(2,1)S(1)} collective-permute-done((bf16[2,64,128]{2,1,0:T(8,128)(2,1)S(1)}, bf16[2,64,128]{2,1,0:T(8,128)(2,1)S(1)}, u32[]{:S(2)}, u32[]{:S(2)}) %collective-permute-start.4) | collective-permute-done | bytes 32800 | tf_op jit(solution)/shard_map/ppermute | solution.py:366
  78.7 1.2 %collective-permute-done.5.from_both = bf16[2,64,128]{2,1,0:T(8,128)(2,1)S(1)} collective-permute-done((bf16[2,64,128]{2,1,0:T(8,128)(2,1)S(1)}, bf16[2,64,128]{2,1,0:T(8,128)(2,1)S(1)}, u32[]{:S(2)}, u32[]{:S(2)}) %collective-permute-start.5) | collective-permute-done | bytes 32800 | tf_op jit(solution)/shard_map/ppermute | solution.py:367
  80.0 0.7 finish.1
  (2 shorter events, 0.0 us)
Async XLA Ops:
  0.0 42.2 %copy-start = (s32[768]{0:T(1024)S(1)}, s32[768]{0:T(1024)}, u32[]{:S(2)}) copy-start(s32[768]{0:T(1024)} %param.6) | copy-start | bytes 9220
  39.1 5.3 %collective-permute-start = (bf16[3072,128]{1,0:T(8,128)(2,1)S(1)}, bf16[3072,128]{1,0:T(8,128)(2,1)S(1)}, u32[]{:S(2)}, u32[]{:S(2)}) collective-permute-start(bf16[3072,128]{1,0:T(8,128)(2,1)S(1)} %bitcast.8), channel_id=1, source_target_pairs={{0,2},{2,0},{1,3},{3,1},{4,6},{6,4},{5,7},{7,5},{8,10},{10,8},{9,1... | collective-permute-start | bytes 2359304 | tf_op jit(solution)/shard_map/ppermute | solution.py:350
  44.4 4.2 %copy-start.1 = (s32[256]{0:T(256)S(1)}, s32[256]{0:T(256)}, u32[]{:S(2)}) copy-start(s32[256]{0:T(256)} %param.7) | copy-start | bytes 3076
  47.1 5.2 %collective-permute-start.1 = (f32[128,256]{1,0:T(8,128)S(1)}, f32[128,256]{1,0:T(8,128)S(1)}, u32[]{:S(2)}, u32[]{:S(2)}) collective-permute-start(f32[128,256]{1,0:T(8,128)S(1)} %get-tuple-element.23), channel_id=1, source_target_pairs={{0,1},{1,0},{2,3},{3,2},{4,5},{5,4},{6,7},{7,6},{8,9},{9,8},{10,11... | collective-permute-start | bytes 393224 | tf_op jit(solution)/shard_map/ppermute | solution.py:359
  47.5 7.6 %collective-permute-start.2 = (f32[128,256]{1,0:T(8,128)S(1)}, f32[128,256]{1,0:T(8,128)S(1)}, u32[]{:S(2)}, u32[]{:S(2)}) collective-permute-start(f32[128,256]{1,0:T(8,128)S(1)} %get-tuple-element.25), channel_id=1, source_target_pairs={{0,1},{1,0},{2,3},{3,2},{4,5},{5,4},{6,7},{7,6},{8,9},{9,8},{10,11... | collective-permute-start | bytes 393224 | tf_op jit(solution)/shard_map/ppermute | solution.py:360
  73.0 4.7 %collective-permute-start.3 = (bf16[2,64,128]{2,1,0:T(8,128)(2,1)S(1)}, bf16[2,64,128]{2,1,0:T(8,128)(2,1)S(1)}, u32[]{:S(2)}, u32[]{:S(2)}) collective-permute-start(bf16[2,64,128]{2,1,0:T(8,128)(2,1)S(1)} %get-tuple-element.30), channel_id=1, source_target_pairs={{0,2},{2,0},{1,3},{3,1},{4,6},{6,4},{5,7},{7,5},{8,10},{10,8},{9,1... | collective-permute-start | bytes 98312 | tf_op jit(solution)/shard_map/ppermute | solution.py:368
  76.0 2.8 %collective-permute-start.4 = (bf16[2,64,128]{2,1,0:T(8,128)(2,1)S(1)}, bf16[2,64,128]{2,1,0:T(8,128)(2,1)S(1)}, u32[]{:S(2)}, u32[]{:S(2)}) collective-permute-start(bf16[2,64,128]{2,1,0:T(8,128)(2,1)S(1)} %get-tuple-element.31), channel_id=1, source_target_pairs={{0,1},{1,0},{2,3},{3,2},{4,5},{5,4},{6,7},{7,6},{8,9},{9,8},{10,11... | collective-permute-start | bytes 98312 | tf_op jit(solution)/shard_map/ppermute | solution.py:366
  76.3 3.7 %collective-permute-start.5 = (bf16[2,64,128]{2,1,0:T(8,128)(2,1)S(1)}, bf16[2,64,128]{2,1,0:T(8,128)(2,1)S(1)}, u32[]{:S(2)}, u32[]{:S(2)}) collective-permute-start(bf16[2,64,128]{2,1,0:T(8,128)(2,1)S(1)} %get-tuple-element.32), channel_id=1, source_target_pairs={{0,3},{1,2},{2,1},{3,0},{4,7},{5,6},{6,5},{7,4},{8,11},{9,10},{10,... | collective-permute-start | bytes 98312 | tf_op jit(solution)/shard_map/ppermute | solution.py:367

commit v9 on v3

--- a/solution.py
+++ b/solution.py
@@ -214,17 +214,18 @@
     )(place, matrices, integrals)
 
 
-def chosen(values, order_by):
+def chosen(values, orders):
+    rows = values.shape[0]
     high = values.astype(BF16)
     rest = values - high.astype(F32)
     middle = rest.astype(BF16)
     low = (rest - middle.astype(F32)).astype(BF16)
-    total = lax.dot_general(low, order_by, NT, preferred_element_type=F32)
-    total += lax.dot_general(middle, order_by, NT, preferred_element_type=F32)
-    return total + lax.dot_general(high, order_by, NT, preferred_element_type=F32)
-
-
-def combine_kernel(kept, got, natural_order, chip_order, own, mirror):
+    parts = jnp.concatenate([low, middle, high], axis=0)
+    parts = lax.dot_general(parts, orders, NT, preferred_element_type=F32)
+    return parts[:rows] + parts[rows : 2 * rows] + parts[2 * rows :]
+
+
+def combine_kernel(kept, got, orders, own, mirror):
     full_virtual = kept.shape[1]
     rows = kept.shape[0] // 2
     chips = mirror.shape[0] // 8
@@ -232,8 +233,9 @@
     occupied = rows // here
     lane = lax.broadcasted_iota(jnp.int32, (occupied, 2 * chips), 1)
     values = kept[...] + got[...]
-    by_chip = chosen(values, chip_order[...])
-    own[...] = chosen(values, natural_order[...])
+    ordered = chosen(values, orders[...])
+    own[...] = ordered[:, :full_virtual]
+    by_chip = ordered[:, full_virtual:]
     for part in range(2):
         for row in range(0, here, 2):
             at = part * rows + row * occupied
@@ -249,13 +251,13 @@
             mirror[pl.ds(2 * (row + 1) + part, chips, stride=8), :] = turned[chips:]
 
 
-def combine(kept, got, natural_order, chip_order, chips):
+def combine(kept, got, orders, chips):
     return pl.pallas_call(
         combine_kernel,
         out_shape=(jax.ShapeDtypeStruct(kept.shape, F32), jax.ShapeDtypeStruct((chips * 8, kept.shape[0] // 2), F32)),
         compiler_params=PARAMS,
         name="combine",
-    )(kept, got, natural_order, chip_order)
+    )(kept, got, orders)
 
 
 def subtract_kernel(place, own, mirror, keep, to_core, to_vir, to_both, block):
@@ -337,15 +339,15 @@
     across = lax.ppermute(moved, "core", SWAP)
 
     tables = pair_table.reshape(chips, 2, slots).transpose(1, 0, 2).reshape(2, 1, chips * slots)
-    places = jnp.arange(full_virtual, dtype=jnp.int32)[:, None]
-    natural_order = (kramers[None, :] == places).astype(BF16)
-    chip_order = (kramers[None, :] == places % chips * here + places // chips).astype(BF16)
+    places = jnp.arange(full_virtual, dtype=jnp.int32)
+    places = jnp.concatenate([places, places % chips * here + places // chips])[:, None]
+    orders = (kramers[None, :] == places).astype(BF16)
 
     mine, slabs, chooser = order(place, moved, tables, flat, occupied)
     matrices, to_send = first_window(mine, across, chooser, slabs, occupied)
     got = lax.ppermute(to_send, "vir", SWAP)
     kept = second_window(place, matrices, flat)
-    own, mirror = combine(kept, got, natural_order, chip_order, chips)
+    own, mirror = combine(kept, got, orders, chips)
     mirror = lax.all_to_all(mirror.reshape(chips, 8, -1), "chip", split_axis=0, concat_axis=0, tiled=True)
     keep, to_core, to_vir, to_both = subtract(place, own, mirror.reshape(chips * 8, -1))
     from_vir = lax.ppermute(to_vir, "vir", SWAP)

time: 80.9 us -> 80.9 us (level)
  no operation moved by 1% of the time
where the time goes in v9:
time: 80.9 us; the launch traced here: 80.7 us
  blocking collectives  54.9 us (68%)
  Pallas kernels  10.6 us (13%)
  starting transfers between devices  8.19 us (10%)
  waiting for transfers between devices  6.41 us (8%)
    all_to_all x1, blocking collectives, body(): lax.all_to_all(pieces, 'chip', split_axis=0, concat_axis=0, tiled=True)  37.8 us
    all_to_all x1, blocking collectives, body(): lax.all_to_all(mirror.reshape(chips, 8, -1), 'chip', split_axis=0, concat...  17.1 us
    ppermute x1, waiting for transfers between devices, body(): got = lax.ppermute(to_send, 'vir', SWAP)  4.12 us
    pallas_call x1, Pallas kernels, second_window(): pl.pallas_call(second_kernel, out_shape=jax.ShapeDtypeStruct((matrices.sh...  3.36 us
    ppermute x1, starting transfers between devices, body(): across = lax.ppermute(moved, 'core', SWAP)  3.05 us
    ppermute x1, starting transfers between devices, body(): from_core = lax.ppermute(to_core, 'core', SWAP)  3.01 us
    pallas_call x1, Pallas kernels, first_window(): pl.pallas_call(functools.partial(first_kernel, occupied=occupied), out_sh...  2.66 us
    pallas_call x1, Pallas kernels, order(): pl.pallas_call(functools.partial(order_kernel, occupied=occupied), out_sh...  1.92 us
  transfers between devices with their start and end apart: 5, of which 3 were waited for; matrix products, arithmetic and copies ran while one was open for 1% of the time, Pallas kernels for 7%

profile of v9, /device:TPU:1, one launch (start us, length us, event | category | flops | bytes accessed | tf_op | source)
XLA Modules:
  0.0 80.7 jit_solution(13211157359940249236)
XLA Ops:
  0.0 0.0 copy-start
  0.0 1.3 %regroup.1 = bf16[64,12,4,128]{3,2,1,0:T(4,128)(2,1)S(1)} custom-call(bf16[2,6,64,4,128]{4,3,2,1,0:T(4,128)(2,1)} %bitcast.14), custom_call_target="tpu_custom_call" | custom-call | tf_op jit(solution)/shard_map/regroup/pallas_call | solution.py:45
  1.3 37.8 %all_to_all.10 = bf16[64,12,4,128]{3,2,1,0:T(4,128)(2,1)S(1)} all-to-all(bf16[64,12,4,128]{3,2,1,0:T(4,128)(2,1)S(1)} %regroup.1), channel_id=1, replica_groups=mesh['chip'=64,'core'=2,'vir'=2] {'chip'}, dimensions={0} | all-to-all | bytes 1572864 | tf_op jit(solution)/shard_map/all_to_all | solution.py:335
  39.1 3.0 %collective-permute-start = (bf16[3072,128]{1,0:T(8,128)(2,1)S(1)}, bf16[3072,128]{1,0:T(8,128)(2,1)S(1)}, u32[]{:S(2)}, u32[]{:S(2)}) collective-permute-start(bf16[3072,128]{1,0:T(8,128)(2,1)S(1)} %bitcast.8), channel_id=1, source_target_pairs={{0,2},{2,0},{1,3},{3,1},{4,6},{6,4},{5,7},{7,5},{8,10},{10,8},{9,1... | collective-permute-start | bytes 2359304 | tf_op jit(solution)/shard_map/ppermute | solution.py:339
  42.2 0.0 copy-done
  42.2 0.2 reshape.32
  42.3 0.1 reshape.38.tables
  42.5 1.9 %order.1 = (bf16[256,3072]{1,0:T(8,128)(2,1)S(1)}, bf16[2,3072,256]{2,1,0:T(8,128)(2,1)S(1)}, bf16[768,384]{1,0:T(8,128)(2,1)S(1)}) custom-call(s32[1]{0:T(128)} %bitcast.place, bf16[3072,128]{1,0:T(8,128)(2,1)S(1)} %bitcast.9, s32[2,1,384]{2,1,0:T(1,128)S(1)} %reshape.38.tables, bf16[2,4,3072,256]{3,2,1,0:T(8,128)(2,1)} %bitcast.12), custom_call_target="tpu_custom_call" | custom-call | flops 603979776 | bytes 6291456 | tf_op jit(solution)/shard_map/order/pallas_call | solution.py:121
  44.5 0.0 copy-start.1
  44.5 0.0 collective-permute-done.moved
  44.5 2.7 %first_window.1 = (bf16[256,3072]{1,0:T(8,128)(2,1)S(1)}, f32[256,256]{1,0:T(8,128)S(1)}) custom-call(bf16[256,3072]{1,0:T(8,128)(2,1)S(1)} %get-tuple-element.16.mine, bf16[3072,128]{1,0:T(8,128)(2,1)S(1)} %collective-permute-done.moved, bf16[768,384]{1,0:T(8,128)(2,1)S(1)} %get-tuple-element.17.chooser, bf16[2,3072,256]{2,1,0:T(8,128)(2,1)S(1)} %get-tuple-element.18.slabs), custom_call_target="tpu_custom_call" | custom-call | flops 805306368 | bytes 3145728 | tf_op jit(solution)/shard_map/first_window/pallas_call | solution.py:176
  47.1 0.4 collective-permute-start.1
  47.5 0.0 copy-done.1
  47.5 0.1 compare_convert_fusion.orders
  47.7 3.4 %second_window.1.kept = f32[256,256]{1,0:T(8,128)S(1)} custom-call(s32[1]{0:T(128)} %bitcast.place, bf16[256,3072]{1,0:T(8,128)(2,1)S(1)} %get-tuple-element.19.matrices, bf16[2,4,3072,256]{3,2,1,0:T(8,128)(2,1)} %bitcast.13), custom_call_target="tpu_custom_call" | custom-call | flops 805306368 | bytes 3145728 | tf_op jit(solution)/shard_map/second_window/pallas_call | solution.py:205
  51.0 4.1 %collective-permute-done.1.got = f32[256,256]{1,0:T(8,128)S(1)} collective-permute-done((f32[256,256]{1,0:T(8,128)S(1)}, f32[256,256]{1,0:T(8,128)S(1)}, u32[]{:S(2)}, u32[]{:S(2)}) %collective-permute-start.1) | collective-permute-done | bytes 262176 | tf_op jit(solution)/shard_map/ppermute | solution.py:348
  55.2 0.6 combine.1
  55.7 17.1 %all_to_all.11 = f32[64,8,128]{2,1,0:T(8,128)S(1)} all-to-all(f32[64,8,128]{2,1,0:T(8,128)S(1)} %bitcast.11), channel_id=1, replica_groups=mesh['chip'=64,'core'=2,'vir'=2] {'chip'}, dimensions={0} | all-to-all | bytes 524288 | tf_op jit(solution)/shard_map/all_to_all | solution.py:351
  72.8 0.1 subtract.1
  73.0 3.0 %collective-permute-start.2 = (bf16[2,64,128]{2,1,0:T(8,128)(2,1)S(1)}, bf16[2,64,128]{2,1,0:T(8,128)(2,1)S(1)}, u32[]{:S(2)}, u32[]{:S(2)}) collective-permute-start(bf16[2,64,128]{2,1,0:T(8,128)(2,1)S(1)} %get-tuple-element.24), channel_id=1, source_target_pairs={{0,2},{2,0},{1,3},{3,1},{4,6},{6,4},{5,7},{7,5},{8,10},{10,8},{9,1... | collective-permute-start | bytes 98312 | tf_op jit(solution)/shard_map/ppermute | solution.py:355
  76.0 0.3 collective-permute-start.3
  76.3 1.4 %collective-permute-start.4 = (bf16[2,64,128]{2,1,0:T(8,128)(2,1)S(1)}, bf16[2,64,128]{2,1,0:T(8,128)(2,1)S(1)}, u32[]{:S(2)}, u32[]{:S(2)}) collective-permute-start(bf16[2,64,128]{2,1,0:T(8,128)(2,1)S(1)} %get-tuple-element.26), channel_id=1, source_target_pairs={{0,3},{1,2},{2,1},{3,0},{4,7},{5,6},{6,5},{7,4},{8,11},{9,10},{10,... | collective-permute-start | bytes 98312 | tf_op jit(solution)/shard_map/ppermute | solution.py:354
  77.7 0.0 collective-permute-done.2.from_core
  77.7 1.0 %collective-permute-done.3.from_vir = bf16[2,64,128]{2,1,0:T(8,128)(2,1)S(1)} collective-permute-done((bf16[2,64,128]{2,1,0:T(8,128)(2,1)S(1)}, bf16[2,64,128]{2,1,0:T(8,128)(2,1)S(1)}, u32[]{:S(2)}, u32[]{:S(2)}) %collective-permute-start.3) | collective-permute-done | bytes 32800 | tf_op jit(solution)/shard_map/ppermute | solution.py:353
  78.8 1.2 %collective-permute-done.4.from_both = bf16[2,64,128]{2,1,0:T(8,128)(2,1)S(1)} collective-permute-done((bf16[2,64,128]{2,1,0:T(8,128)(2,1)S(1)}, bf16[2,64,128]{2,1,0:T(8,128)(2,1)S(1)}, u32[]{:S(2)}, u32[]{:S(2)}) %collective-permute-start.4) | collective-permute-done | bytes 32800 | tf_op jit(solution)/shard_map/ppermute | solution.py:354
  80.0 0.7 finish.1
  (4 shorter events, 0.0 us)
Async XLA Ops:
  0.0 42.2 %copy-start = (s32[768]{0:T(1024)S(1)}, s32[768]{0:T(1024)}, u32[]{:S(2)}) copy-start(s32[768]{0:T(1024)} %param.6) | copy-start | bytes 9220
  39.1 5.4 %collective-permute-start = (bf16[3072,128]{1,0:T(8,128)(2,1)S(1)}, bf16[3072,128]{1,0:T(8,128)(2,1)S(1)}, u32[]{:S(2)}, u32[]{:S(2)}) collective-permute-start(bf16[3072,128]{1,0:T(8,128)(2,1)S(1)} %bitcast.8), channel_id=1, source_target_pairs={{0,2},{2,0},{1,3},{3,1},{4,6},{6,4},{5,7},{7,5},{8,10},{10,8},{9,1... | collective-permute-start | bytes 2359304 | tf_op jit(solution)/shard_map/ppermute | solution.py:339
  44.5 3.1 %copy-start.1 = (s32[256]{0:T(256)S(1)}, s32[256]{0:T(256)}, u32[]{:S(2)}) copy-start(s32[256]{0:T(256)} %param.7) | copy-start | bytes 3076
  47.1 8.0 %collective-permute-start.1 = (f32[256,256]{1,0:T(8,128)S(1)}, f32[256,256]{1,0:T(8,128)S(1)}, u32[]{:S(2)}, u32[]{:S(2)}) collective-permute-start(f32[256,256]{1,0:T(8,128)S(1)} %get-tuple-element.20), channel_id=1, source_target_pairs={{0,1},{1,0},{2,3},{3,2},{4,5},{5,4},{6,7},{7,6},{8,9},{9,8},{10,11... | collective-permute-start | bytes 786440 | tf_op jit(solution)/shard_map/ppermute | solution.py:348
  73.0 4.7 %collective-permute-start.2 = (bf16[2,64,128]{2,1,0:T(8,128)(2,1)S(1)}, bf16[2,64,128]{2,1,0:T(8,128)(2,1)S(1)}, u32[]{:S(2)}, u32[]{:S(2)}) collective-permute-start(bf16[2,64,128]{2,1,0:T(8,128)(2,1)S(1)} %get-tuple-element.24), channel_id=1, source_target_pairs={{0,2},{2,0},{1,3},{3,1},{4,6},{6,4},{5,7},{7,5},{8,10},{10,8},{9,1... | collective-permute-start | bytes 98312 | tf_op jit(solution)/shard_map/ppermute | solution.py:355
  76.0 2.8 %collective-permute-start.3 = (bf16[2,64,128]{2,1,0:T(8,128)(2,1)S(1)}, bf16[2,64,128]{2,1,0:T(8,128)(2,1)S(1)}, u32[]{:S(2)}, u32[]{:S(2)}) collective-permute-start(bf16[2,64,128]{2,1,0:T(8,128)(2,1)S(1)} %get-tuple-element.25), channel_id=1, source_target_pairs={{0,1},{1,0},{2,3},{3,2},{4,5},{5,4},{6,7},{7,6},{8,9},{9,8},{10,11... | collective-permute-start | bytes 98312 | tf_op jit(solution)/shard_map/ppermute | solution.py:353
  76.3 3.7 %collective-permute-start.4 = (bf16[2,64,128]{2,1,0:T(8,128)(2,1)S(1)}, bf16[2,64,128]{2,1,0:T(8,128)(2,1)S(1)}, u32[]{:S(2)}, u32[]{:S(2)}) collective-permute-start(bf16[2,64,128]{2,1,0:T(8,128)(2,1)S(1)} %get-tuple-element.26), channel_id=1, source_target_pairs={{0,3},{1,2},{2,1},{3,0},{4,7},{5,6},{6,5},{7,4},{8,11},{9,10},{10,... | collective-permute-start | bytes 98312 | tf_op jit(solution)/shard_map/ppermute | solution.py:354

commit v10 on v3

--- a/solution.py
+++ b/solution.py
@@ -253,6 +253,8 @@
     return pl.pallas_call(
         combine_kernel,
         out_shape=(jax.ShapeDtypeStruct(kept.shape, F32), jax.ShapeDtypeStruct((chips * 8, kept.shape[0] // 2), F32)),
+        in_specs=[IN_VMEM] * 4,
+        out_specs=(IN_VMEM,) * 2,
         compiler_params=PARAMS,
         name="combine",
     )(kept, got, natural_order, chip_order)

time: 80.9 us -> 80.9 us (level)
  no operation moved by 1% of the time
where the time goes in v10:
time: 80.9 us; the launch traced here: 80.7 us
  blocking collectives  54.9 us (68%)
  Pallas kernels  10.6 us (13%)
  starting transfers between devices  8.14 us (10%)
  waiting for transfers between devices  6.44 us (8%)
    all_to_all x1, blocking collectives, body(): lax.all_to_all(pieces, 'chip', split_axis=0, concat_axis=0, tiled=True)  37.8 us
    all_to_all x1, blocking collectives, body(): lax.all_to_all(mirror.reshape(chips, 8, -1), 'chip', split_axis=0, concat...  17.1 us
    ppermute x1, waiting for transfers between devices, body(): got = lax.ppermute(to_send, 'vir', SWAP)  4.15 us
    pallas_call x1, Pallas kernels, second_window(): pl.pallas_call(second_kernel, out_shape=jax.ShapeDtypeStruct((matrices.sh...  3.36 us
    ppermute x1, starting transfers between devices, body(): across = lax.ppermute(moved, 'core', SWAP)  3.05 us
    ppermute x1, starting transfers between devices, body(): from_core = lax.ppermute(to_core, 'core', SWAP)  2.96 us
    pallas_call x1, Pallas kernels, first_window(): pl.pallas_call(functools.partial(first_kernel, occupied=occupied), out_sh...  2.66 us
    pallas_call x1, Pallas kernels, order(): pl.pallas_call(functools.partial(order_kernel, occupied=occupied), out_sh...  1.92 us
  transfers between devices with their start and end apart: 5, of which 3 were waited for; matrix products, arithmetic and copies ran while one was open for 1% of the time, Pallas kernels for 7%

profile of v10, /device:TPU:1, one launch (start us, length us, event | category | flops | bytes accessed | tf_op | source)
XLA Modules:
  0.0 80.7 jit_solution(7578386010368624795)
XLA Ops:
  0.0 0.0 copy-start
  0.0 1.3 %regroup.1 = bf16[64,12,4,128]{3,2,1,0:T(4,128)(2,1)S(1)} custom-call(bf16[2,6,64,4,128]{4,3,2,1,0:T(4,128)(2,1)} %bitcast.14), custom_call_target="tpu_custom_call" | custom-call | tf_op jit(solution)/shard_map/regroup/pallas_call | solution.py:45
  1.3 37.8 %all_to_all.10 = bf16[64,12,4,128]{3,2,1,0:T(4,128)(2,1)S(1)} all-to-all(bf16[64,12,4,128]{3,2,1,0:T(4,128)(2,1)S(1)} %regroup.1), channel_id=1, replica_groups=mesh['chip'=64,'core'=2,'vir'=2] {'chip'}, dimensions={0} | all-to-all | bytes 1572864 | tf_op jit(solution)/shard_map/all_to_all | solution.py:335
  39.1 3.0 %collective-permute-start = (bf16[3072,128]{1,0:T(8,128)(2,1)S(1)}, bf16[3072,128]{1,0:T(8,128)(2,1)S(1)}, u32[]{:S(2)}, u32[]{:S(2)}) collective-permute-start(bf16[3072,128]{1,0:T(8,128)(2,1)S(1)} %bitcast.8), channel_id=1, source_target_pairs={{0,2},{2,0},{1,3},{3,1},{4,6},{6,4},{5,7},{7,5},{8,10},{10,8},{9,1... | collective-permute-start | bytes 2359304 | tf_op jit(solution)/shard_map/ppermute | solution.py:339
  42.2 0.0 copy-done
  42.2 0.2 reshape.86
  42.3 0.1 reshape.92.tables
  42.5 1.9 %order.1 = (bf16[256,3072]{1,0:T(8,128)(2,1)S(1)}, bf16[2,3072,256]{2,1,0:T(8,128)(2,1)S(1)}, bf16[768,384]{1,0:T(8,128)(2,1)S(1)}) custom-call(s32[1]{0:T(128)} %bitcast.place, bf16[3072,128]{1,0:T(8,128)(2,1)S(1)} %bitcast.9, s32[2,1,384]{2,1,0:T(1,128)S(1)} %reshape.92.tables, bf16[2,4,3072,256]{3,2,1,0:T(8,128)(2,1)} %bitcast.12), custom_call_target="tpu_custom_call" | custom-call | flops 603979776 | bytes 6291456 | tf_op jit(solution)/shard_map/order/pallas_call | solution.py:121
  44.4 0.0 copy-start.1
  44.4 0.0 collective-permute-done.moved
  44.4 2.7 %first_window.1 = (bf16[256,3072]{1,0:T(8,128)(2,1)S(1)}, f32[256,256]{1,0:T(8,128)S(1)}) custom-call(bf16[256,3072]{1,0:T(8,128)(2,1)S(1)} %get-tuple-element.16.mine, bf16[3072,128]{1,0:T(8,128)(2,1)S(1)} %collective-permute-done.moved, bf16[768,384]{1,0:T(8,128)(2,1)S(1)} %get-tuple-element.17.chooser, bf16[2,3072,256]{2,1,0:T(8,128)(2,1)S(1)} %get-tuple-element.18.slabs), custom_call_target="tpu_custom_call" | custom-call | flops 805306368 | bytes 3145728 | tf_op jit(solution)/shard_map/first_window/pallas_call | solution.py:176
  47.1 0.4 collective-permute-start.1
  47.5 0.0 copy-done.1
  47.5 0.1 compare_convert_fusion
  47.6 3.4 %second_window.1.kept = f32[256,256]{1,0:T(8,128)S(1)} custom-call(s32[1]{0:T(128)} %bitcast.place, bf16[256,3072]{1,0:T(8,128)(2,1)S(1)} %get-tuple-element.19.matrices, bf16[2,4,3072,256]{3,2,1,0:T(8,128)(2,1)} %bitcast.13), custom_call_target="tpu_custom_call" | custom-call | flops 805306368 | bytes 3145728 | tf_op jit(solution)/shard_map/second_window/pallas_call | solution.py:205
  51.0 4.1 %collective-permute-done.1.got = f32[256,256]{1,0:T(8,128)S(1)} collective-permute-done((f32[256,256]{1,0:T(8,128)S(1)}, f32[256,256]{1,0:T(8,128)S(1)}, u32[]{:S(2)}, u32[]{:S(2)}) %collective-permute-start.1) | collective-permute-done | bytes 262176 | tf_op jit(solution)/shard_map/ppermute | solution.py:348
  55.1 0.6 combine.1
  55.7 17.1 %all_to_all.11 = f32[64,8,128]{2,1,0:T(8,128)S(1)} all-to-all(f32[64,8,128]{2,1,0:T(8,128)S(1)} %bitcast.11), channel_id=1, replica_groups=mesh['chip'=64,'core'=2,'vir'=2] {'chip'}, dimensions={0} | all-to-all | bytes 524288 | tf_op jit(solution)/shard_map/all_to_all | solution.py:351
  72.8 0.1 subtract.1
  73.0 3.0 %collective-permute-start.2 = (bf16[2,64,128]{2,1,0:T(8,128)(2,1)S(1)}, bf16[2,64,128]{2,1,0:T(8,128)(2,1)S(1)}, u32[]{:S(2)}, u32[]{:S(2)}) collective-permute-start(bf16[2,64,128]{2,1,0:T(8,128)(2,1)S(1)} %get-tuple-element.24), channel_id=1, source_target_pairs={{0,2},{2,0},{1,3},{3,1},{4,6},{6,4},{5,7},{7,5},{8,10},{10,8},{9,1... | collective-permute-start | bytes 98312 | tf_op jit(solution)/shard_map/ppermute | solution.py:355
  76.0 0.3 collective-permute-start.3
  76.3 1.4 %collective-permute-start.4 = (bf16[2,64,128]{2,1,0:T(8,128)(2,1)S(1)}, bf16[2,64,128]{2,1,0:T(8,128)(2,1)S(1)}, u32[]{:S(2)}, u32[]{:S(2)}) collective-permute-start(bf16[2,64,128]{2,1,0:T(8,128)(2,1)S(1)} %get-tuple-element.26), channel_id=1, source_target_pairs={{0,3},{1,2},{2,1},{3,0},{4,7},{5,6},{6,5},{7,4},{8,11},{9,10},{10,... | collective-permute-start | bytes 98312 | tf_op jit(solution)/shard_map/ppermute | solution.py:354
  77.7 0.0 collective-permute-done.2.from_core
  77.7 1.0 %collective-permute-done.3.from_vir = bf16[2,64,128]{2,1,0:T(8,128)(2,1)S(1)} collective-permute-done((bf16[2,64,128]{2,1,0:T(8,128)(2,1)S(1)}, bf16[2,64,128]{2,1,0:T(8,128)(2,1)S(1)}, u32[]{:S(2)}, u32[]{:S(2)}) %collective-permute-start.3) | collective-permute-done | bytes 32800 | tf_op jit(solution)/shard_map/ppermute | solution.py:353
  78.7 1.2 %collective-permute-done.4.from_both = bf16[2,64,128]{2,1,0:T(8,128)(2,1)S(1)} collective-permute-done((bf16[2,64,128]{2,1,0:T(8,128)(2,1)S(1)}, bf16[2,64,128]{2,1,0:T(8,128)(2,1)S(1)}, u32[]{:S(2)}, u32[]{:S(2)}) %collective-permute-start.4) | collective-permute-done | bytes 32800 | tf_op jit(solution)/shard_map/ppermute | solution.py:354
  80.0 0.7 finish.1
  (2 shorter events, 0.0 us)
Async XLA Ops:
  0.0 42.2 %copy-start = (s32[768]{0:T(1024)S(1)}, s32[768]{0:T(1024)}, u32[]{:S(2)}) copy-start(s32[768]{0:T(1024)} %param.6) | copy-start | bytes 9220
  39.1 5.3 %collective-permute-start = (bf16[3072,128]{1,0:T(8,128)(2,1)S(1)}, bf16[3072,128]{1,0:T(8,128)(2,1)S(1)}, u32[]{:S(2)}, u32[]{:S(2)}) collective-permute-start(bf16[3072,128]{1,0:T(8,128)(2,1)S(1)} %bitcast.8), channel_id=1, source_target_pairs={{0,2},{2,0},{1,3},{3,1},{4,6},{6,4},{5,7},{7,5},{8,10},{10,8},{9,1... | collective-permute-start | bytes 2359304 | tf_op jit(solution)/shard_map/ppermute | solution.py:339
  44.4 3.1 %copy-start.1 = (s32[256]{0:T(256)S(1)}, s32[256]{0:T(256)}, u32[]{:S(2)}) copy-start(s32[256]{0:T(256)} %param.7) | copy-start | bytes 3076
  47.1 8.0 %collective-permute-start.1 = (f32[256,256]{1,0:T(8,128)S(1)}, f32[256,256]{1,0:T(8,128)S(1)}, u32[]{:S(2)}, u32[]{:S(2)}) collective-permute-start(f32[256,256]{1,0:T(8,128)S(1)} %get-tuple-element.20), channel_id=1, source_target_pairs={{0,1},{1,0},{2,3},{3,2},{4,5},{5,4},{6,7},{7,6},{8,9},{9,8},{10,11... | collective-permute-start | bytes 786440 | tf_op jit(solution)/shard_map/ppermute | solution.py:348
  73.0 4.7 %collective-permute-start.2 = (bf16[2,64,128]{2,1,0:T(8,128)(2,1)S(1)}, bf16[2,64,128]{2,1,0:T(8,128)(2,1)S(1)}, u32[]{:S(2)}, u32[]{:S(2)}) collective-permute-start(bf16[2,64,128]{2,1,0:T(8,128)(2,1)S(1)} %get-tuple-element.24), channel_id=1, source_target_pairs={{0,2},{2,0},{1,3},{3,1},{4,6},{6,4},{5,7},{7,5},{8,10},{10,8},{9,1... | collective-permute-start | bytes 98312 | tf_op jit(solution)/shard_map/ppermute | solution.py:355
  76.0 2.8 %collective-permute-start.3 = (bf16[2,64,128]{2,1,0:T(8,128)(2,1)S(1)}, bf16[2,64,128]{2,1,0:T(8,128)(2,1)S(1)}, u32[]{:S(2)}, u32[]{:S(2)}) collective-permute-start(bf16[2,64,128]{2,1,0:T(8,128)(2,1)S(1)} %get-tuple-element.25), channel_id=1, source_target_pairs={{0,1},{1,0},{2,3},{3,2},{4,5},{5,4},{6,7},{7,6},{8,9},{9,8},{10,11... | collective-permute-start | bytes 98312 | tf_op jit(solution)/shard_map/ppermute | solution.py:353
  76.3 3.7 %collective-permute-start.4 = (bf16[2,64,128]{2,1,0:T(8,128)(2,1)S(1)}, bf16[2,64,128]{2,1,0:T(8,128)(2,1)S(1)}, u32[]{:S(2)}, u32[]{:S(2)}) collective-permute-start(bf16[2,64,128]{2,1,0:T(8,128)(2,1)S(1)} %get-tuple-element.26), channel_id=1, source_target_pairs={{0,3},{1,2},{2,1},{3,0},{4,7},{5,6},{6,5},{7,4},{8,11},{9,10},{10,... | collective-permute-start | bytes 98312 | tf_op jit(solution)/shard_map/ppermute | solution.py:354
